TPU v7x, 512 devices: a whole 4x4x16 slice. The times are simulated.
512 devices in a mesh: seq: 64 (over z, x_hi, core), tp: 4 (over y), pair: 2 (over x_lo).
Axes of the slice: x: 4 (x_hi: 2, x_lo: 2; x = x_hi * 2 + x_lo), y: 4, z: 16, core: 2. Of those that a mesh axis runs over, the one named last changes fastest.
Arguments:
- queries: bfloat16 [8192, 4096], P('seq', ('tp', 'pair')), may hold values from -18 to 18
- stored_key_value: bfloat16 [8192, 1024], P('seq', ('tp', 'pair')), may hold values from -18 to 18, as said below
- out_grad: bfloat16 [8192, 4096], P('seq', ('tp', 'pair')), may hold values from -6 to 6
- attn_out: bfloat16 [8192, 4096], P('seq', ('tp', 'pair')), may hold values from -3 to 3
- segment_ids: int32 [8192], P('seq'), may hold values from 0 to 5, as said below
- loss_mask: int32 [8192], P('seq'), may hold values 0 or 1
Outputs:
- query_gradient: bfloat16 [8192, 4096], P('seq', ('tp', 'pair'))
- kv_grad: bfloat16 [8192, 1024], P('seq', ('tp', 'pair'))
Inputs may be any that keep to these rules, and one draw needn't show every extreme that they name: `stored_key_value`: each row of a key-value head's keys lies within the range. `segment_ids`: document numbers never decrease along the row; each document is contiguous; the first document holds exactly 6144 tokens and the others share the rest, each of one token or more.
All inputs are finite; a program needn't handle non-finite values. No bound on the sum of `loss_mask` on one device may be relied on, other than what follows from the above.
Results may differ from a plain program's by a relative error of at most 0.007.
Values may be sent and summed in bfloat16 or wider, within the bound.
No kernel may reach another device: no remote copies, remote signals or barrier semaphores. Data moves between devices by JAX's collectives and lax.ppermute only.
A program may use at most 64 MiB of HBM per device.

v0:
```python
import math

import jax
import jax.numpy as jnp
from jax import lax
from jax.sharding import PartitionSpec as P

NEGATIVE = -1e30


def swapped(array, axis, stride):
    return lax.ppermute(array, axis, [(i, i ^ 1 << stride) for i in range(lax.axis_size(axis))])


def block_width(row_count):
    for option_width in (512, 256, 128):
        return option_width
    return row_count


def masked_scores(q_heads, key_block, seg_block, block_first, query_pos, query_seg, scale_factor):
    scores = (
        jnp.einsum("thd,wd->htw", q_heads, key_block, preferred_element_type=jnp.float32)
        * scale_factor
    )
    key_pos = block_first + jnp.arange(key_block.shape[0], dtype=jnp.int32)
    allowed = (key_pos[None, :] <= query_pos[:, None]) & (seg_block[None, :] == query_seg[:, None])
    return (jnp.where(allowed[None], scores, NEGATIVE), allowed)


def add_rows(total, term, row_first):
    current = lax.dynamic_slice_in_dim(total, row_first, term.shape[0], 0)
    return lax.dynamic_update_slice_in_dim(total, current + term, row_first, 0)


def over_blocks(update, running, arrays):
    row_count = arrays[0].shape[0]
    blk_rows = block_width(row_count)

    def one_block(state_now, blk_index):
        offset = blk_index * blk_rows
        blocks = tuple((lax.dynamic_slice_in_dim(member, offset, blk_rows, 0) for member in arrays))
        state_next = update(state_now, blocks, offset)
        return (state_next, None)

    running, _ = lax.scan(one_block, running, jnp.arange(row_count // blk_rows, dtype=jnp.int32))
    return running


def per_device(queries, stored_key_value, out_grad, attn_out, segment_ids, loss_mask):
    tok_rows = queries.shape[0]
    head_dim = stored_key_value.shape[1]
    head_count = queries.shape[1] // head_dim
    scale_factor = 1.0 / math.sqrt(head_dim)
    full_length = tok_rows * lax.axis_size("seq")
    query_pos = lax.axis_index("seq") * tok_rows + jnp.arange(tok_rows, dtype=jnp.int32)
    kv_pair = lax.all_gather(stored_key_value, "pair", axis=1, tiled=True)
    q_heads = queries.reshape(tok_rows, head_count, head_dim)
    cotangent = (out_grad * loss_mask[:, None].astype(jnp.bfloat16)).reshape(
        tok_rows, head_count, head_dim
    )
    out_heads = attn_out.reshape(tok_rows, head_count, head_dim)
    delta_rows = jnp.einsum("thd,thd->ht", cotangent, out_heads, preferred_element_type=jnp.float32)

    def forward_update(statistics, blocks, block_first):
        run_max, run_sum = statistics
        scores, allowed = masked_scores(
            q_heads, blocks[0], blocks[1], block_first, query_pos, segment_ids, scale_factor
        )
        new_max = jnp.maximum(run_max, jnp.max(scores, axis=2))
        terms = jnp.where(allowed[None], jnp.exp(scores - new_max[..., None]), 0.0)
        return (new_max, run_sum * jnp.exp(run_max - new_max) + jnp.sum(terms, axis=2))

    def backward_update(running, blocks, block_first):
        grad_q, grad_kv = running
        kv_block, seg_block = blocks
        key_block = kv_block[:, :head_dim]
        value_block = kv_block[:, head_dim:]
        scores, allowed = masked_scores(
            q_heads, key_block, seg_block, block_first, query_pos, segment_ids, scale_factor
        )
        softmax_w = jnp.where(allowed[None], jnp.exp(scores - log_norm[..., None]), 0.0)
        grad_probs = jnp.einsum(
            "thd,wd->htw", cotangent, value_block, preferred_element_type=jnp.float32
        )
        grad_scores = (scale_factor * softmax_w * (grad_probs - delta_rows[..., None])).astype(
            jnp.bfloat16
        )
        grad_q = grad_q + jnp.einsum(
            "htw,wd->thd", grad_scores, key_block, preferred_element_type=jnp.float32
        )
        key_term = jnp.einsum(
            "htw,thd->wd", grad_scores, q_heads, preferred_element_type=jnp.float32
        )
        value_term = jnp.einsum(
            "htw,thd->wd",
            softmax_w.astype(jnp.bfloat16),
            cotangent,
            preferred_element_type=jnp.float32,
        )
        grad_kv = add_rows(grad_kv, jnp.concatenate([key_term, value_term], axis=1), block_first)
        return (grad_q, grad_kv)

    init_stats = (
        jnp.full((head_count, tok_rows), NEGATIVE, jnp.float32),
        jnp.zeros((head_count, tok_rows), jnp.float32),
    )
    init_grads = (
        jnp.zeros((tok_rows, head_count, head_dim), jnp.float32),
        jnp.zeros((full_length, 2 * head_dim), jnp.float32),
    )
    keys_full = kv_pair[:, :head_dim]
    run_max, run_sum = over_blocks(
        forward_update,
        init_stats,
        (
            lax.all_gather(keys_full, "seq", axis=0, tiled=True),
            lax.all_gather(segment_ids, "seq", axis=0, tiled=True),
        ),
    )
    log_norm = run_max + jnp.log(run_sum)
    grad_q, grad_kv = over_blocks(
        backward_update,
        init_grads,
        (
            lax.all_gather(kv_pair, "seq", axis=0, tiled=True),
            lax.all_gather(segment_ids, "seq", axis=0, tiled=True),
        ),
    )
    pair_index = lax.axis_index("pair")
    own_part = lax.dynamic_slice_in_dim(grad_kv, pair_index * head_dim, head_dim, 1)
    other_part = lax.dynamic_slice_in_dim(grad_kv, (1 - pair_index) * head_dim, head_dim, 1)
    partner_part = swapped(other_part.astype(jnp.bfloat16), "pair", 0)
    kv_grad = lax.psum_scatter(
        own_part + partner_part.astype(jnp.float32), "seq", scatter_dimension=0, tiled=True
    )
    query_gradient = grad_q.reshape(tok_rows, head_count * head_dim).astype(jnp.bfloat16)
    return (query_gradient, kv_grad.astype(jnp.bfloat16))


def solution(mesh):
    placed = (
        P("seq", ("tp", "pair")),
        P("seq", ("tp", "pair")),
        P("seq", ("tp", "pair")),
        P("seq", ("tp", "pair")),
        P("seq"),
        P("seq"),
    )
    return jax.shard_map(
        per_device,
        mesh=mesh,
        in_specs=placed,
        out_specs=(P("seq", ("tp", "pair")), P("seq", ("tp", "pair"))),
        check_vma=False,
    )
```

profile of v0, /device:TPU:24, one launch (start us, length us, event | category | flops | bytes accessed | tf_op | source)
XLA Modules:
  0.0 728.8 jit_solution(3592614845742727201)
XLA Ops:
  7.2 4.8 all_gather.13
  13.5 83.0 %all-gather = s32[64,1,128]{2,1,0:T(1,128)S(1)} all-gather(s32[1,1,128]{2,1,0:T(1,128)} %bitcast.104), channel_id=1, replica_groups=mesh['seq'=64,'tp'=4,'pair'=2] {'seq'}, dimensions={0}, use_global_device_ids=true | all-gather | bytes 33280 | tf_op jit(solution)/shard_map/all_gather | solution.py:127
  100.9 60.0 %all-gather.6.cloned.1.call-done = bf16[8192,128]{1,0:T(8,128)(2,1)} async-done(((bf16[128,128]{1,0:T(8,128)(2,1)}), bf16[8192,128]{1,0:T(8,128)(2,1)}) %all-gather.6.cloned.1.call-update) | async-done | bytes 2097168 | tf_op jit(solution)/shard_map/all_gather | solution.py:117
  160.9 59.2 %while.26 = (s32[]{:T(128)}, f32[4,128]{1,0:T(4,128)S(1)}, f32[4,128]{1,0:T(4,128)S(1)}, s32[16]{0:T(128)S(1)}, s32[8192]{0:T(1024)S(1)}, /*index=5*/s32[128]{0:...) while((s32[]{:T(128)}, f32[4,128]{1,0:T(4,128)S(1)}, ...), condition=%wide.region_3.4_spmd.clone, body=%wide.region_0.3_spmd.clone.sunk | while | flops 68881544 | bytes 2594522 | solution.py:46
  220.1 90.2 %all-gather.4.cloned.1.call-done = bf16[8192,256]{1,0:T(8,128)(2,1)} async-done(((bf16[128,256]{1,0:T(8,128)(2,1)}), bf16[8192,256]{1,0:T(8,128)(2,1)}) %all-gather.4.cloned.1.call-update) | async-done | bytes 4194320 | tf_op jit(solution)/shard_map/all_gather | solution.py:126
  310.2 3.8 broadcast_in_dim.61.clone
  314.0 132.8 %while.27 = (s32[]{:T(128)}, f32[128,4,128]{0,2,1:T(8,128)S(1)}, f32[8192,256]{1,0:T(8,128)}, s32[16]{0:T(128)S(1)}, bf16[8192,256]{1,0:T(8,128)(2,1)}, /*index=...) while((s32[]{:T(128)}, f32[128,4,128]{0,2,1:T(8,128)S(1)}, ...), condition=%wide.region_5.6_spmd.clone, body=%wide.region_4.5_spmd.clone.sunk | while | flops 338494080 | bytes 12599065 | solution.py:46
  323.8 1.3 fusion.53
  332.1 1.3 fusion.53
  340.4 1.3 fusion.53
  348.7 1.3 fusion.53
  357.0 1.3 fusion.53
  365.3 1.3 fusion.53
  373.6 1.3 fusion.53
  398.5 1.3 fusion.53
  406.8 1.3 fusion.53
  423.4 1.3 fusion.53
  440.0 1.3 fusion.53
  446.8 2.4 dynamic-slice_convert_fusion
  449.2 2.5 collective-permute-start
  451.7 47.3 %collective-permute-done = bf16[8192,128]{1,0:T(8,128)(2,1)} collective-permute-done((bf16[8192,128]{1,0:T(8,128)(2,1)S(1)}, bf16[8192,128]{1,0:T(8,128)(2,1)}, u32[]{:S(2)}, u32[]{:S(2)}) %collective-permute-start) | collective-permute-done | bytes 2097184 | tf_op jit(solution)/shard_map/ppermute | solution.py:12
  499.0 5.1 convert_add_fusion
  504.9 215.9 %reduce-scatter.2.cloned.1.call-done = f32[128,128]{1,0:T(8,128)} async-done(((f32[8192,128]{1,0:T(8,128)}), f32[128,128]{1,0:T(8,128)}) %reduce-scatter.2.cloned.1.call-update) | async-done | bytes 65552 | tf_op jit(solution)/shard_map/reduce_scatter | solution.py:134
  720.8 1.5 convert_element_type.30
  (417 shorter events, 161.1 us)
Async XLA Ops:
  7.2 153.7 %all-gather.6.cloned.1.call-start = ((), (), s32[]{:S(2)}) async-start(), calls=%async_computation.2 | async-start | bytes 2129920 | tf_op jit(solution)/shard_map/all_gather | solution.py:117
  12.0 0.7 copy-start
  12.7 297.5 %all-gather.4.cloned.1.call-start = ((), (), s32[]{:S(2)}) async-start(), calls=%async_computation.1 | async-start | bytes 4259840 | tf_op jit(solution)/shard_map/all_gather | solution.py:126
  13.4 707.4 %reduce-scatter.2.cloned.1.call-start = ((), (), s32[]{:S(2)}) async-start(), calls=%async_computation.3 | async-start | bytes 4259840 | tf_op jit(solution)/shard_map/reduce_scatter | solution.py:134
  310.2 3.8 copy-start.1
  449.2 49.8 %collective-permute-start = (bf16[8192,128]{1,0:T(8,128)(2,1)S(1)}, bf16[8192,128]{1,0:T(8,128)(2,1)}, u32[]{:S(2)}, u32[]{:S(2)}) collective-permute-start(bf16[8192,128]{1,0:T(8,128)(2,1)S(1)} %dynamic-slice_convert_fusion), channel_id=1, source_target_pairs={{0,1},{1,0},{2,3},{3,2},{4,5},{5,4},{6,7},{7,6},{8,9},{9,8},{10,11... | collective-permute-start | bytes 6291464 | tf_op jit(solution)/shard_map/ppermute | solution.py:12
Sparse Core Ops, SparseCore 0:
  12.8 148.0 all-gather.5
  164.7 145.4 all-gather.3
  504.2 216.5 reduce-scatter.1
where the time goes:
time: 732 us; the launch traced here: 729 us
  waiting for transfers between devices  414 us (57%)
  matrix products  88.2 us (12%)
  blocking collectives  87.8 us (12%)
  local copies, waits for them, and re-layouts  68.3 us (9%)
  other arithmetic  30.6 us (4%)
  loops' own time  23.2 us (3%)
  between operations  13.9 us (2%)
    reduce_scatter x1, waiting for transfers between devices, per_device(): lax.psum_scatter(own_part + partner_part.astype(jnp.float32), 'seq', scat...  216 us
    all_gather x1, waiting for transfers between devices, per_device(): lax.all_gather(kv_pair, 'seq', axis=0, tiled=True)  90.2 us
    all_gather x1, blocking collectives, per_device(): lax.all_gather(segment_ids, 'seq', axis=0, tiled=True)  83 us
    all_gather x1, waiting for transfers between devices, per_device(): lax.all_gather(keys_full, 'seq', axis=0, tiled=True)  60 us
    ppermute x1, waiting for transfers between devices, swapped(): lax.ppermute(array, axis, [(i, i ^ 1 << stride) for i in range(lax.axis_s...  47.3 us
    dot_general x32, matrix products, masked_scores(): jnp.einsum('thd,wd->htw', q_heads, key_block, preferred_element_type=jnp....  40.2 us
    another operation x2, loops' own time, over_blocks(): lax.scan(one_block, running, jnp.arange(row_count // blk_rows, dtype=jnp....  23.2 us
    dynamic_slice x32, local copies, waits for them, and re-layouts, add_rows(): current = lax.dynamic_slice_in_dim(total, row_first, term.shape[0], 0)  20.5 us
  transfers between devices with their start and end apart: 4, of which 4 were waited for; matrix products, arithmetic and copies ran while one was open for 7% of the time, Pallas kernels for 0%

commit v1 on v0

v1 whole, which is shorter than its diff:
```python
import functools
import math

import jax
import jax.numpy as jnp
from jax import lax
from jax.experimental import pallas as pl
from jax.experimental.pallas import tpu as pltpu
from jax.sharding import Mesh, PartitionSpec as P

BF = jnp.bfloat16
F32 = jnp.float32
NEGATIVE = -1e30
TOK = 128
HEAD = 128
HEADS = 4
COLS = HEADS * TOK
GROUP = 4
SLOTS = 3
HALF = TOK // 2
KEYS = GROUP * HALF
Q_ROWS = 2 * COLS + 16
KV_ROWS = SLOTS * HALF + 16
SCALE = 1.0 / math.sqrt(HEAD)
SCALE2 = SCALE * math.log2(math.e)
LOG_SCALE = math.log2(SCALE)
X_AXES = ("xh", "pair")
PLANE = ("xh", "core", "pair")
NT = (((1,), (1,)), ((), ()))
NN = (((1,), (0,)), ((), ()))
VMEM_LIMIT = 56 * 1024 * 1024


def dot(a, b, dims):
    return lax.dot_general(a, b, dims, preferred_element_type=F32)


def call(kernel, name, out_shape, scratch=()):
    return pl.pallas_call(
        kernel,
        out_shape=out_shape,
        scratch_shapes=scratch,
        name=name,
        compiler_params=pltpu.CompilerParams(vmem_limit_bytes=VMEM_LIMIT),
    )


def shape(dims, dtype):
    return jax.ShapeDtypeStruct(dims, dtype)


def pack_queries(q_ref, g_ref, o_ref, seg_ref, mask_ref, out_ref):
    mask = jnp.broadcast_to(mask_ref[...].astype(F32), (TOK, TOK)).T
    rows = []
    for h in range(HEADS):
        lanes = slice(h * HEAD, (h + 1) * HEAD)
        cot = g_ref[:, lanes].astype(F32) * mask
        rows.append(jnp.sum((cot * o_ref[:, lanes].astype(F32)).T, axis=0, keepdims=True))
        cot = cot.astype(BF)
        for x in range(4):
            out_ref[x, h * TOK : (h + 1) * TOK, :] = q_ref[:, lanes]
            out_ref[x, COLS + h * TOK : COLS + (h + 1) * TOK, :] = cot
    delta = jnp.concatenate(rows, axis=0)
    high = delta.astype(BF).astype(F32)
    low = delta - high
    tail = jnp.concatenate(
        [high, low, seg_ref[...].astype(F32), jnp.zeros((7, TOK), F32)], axis=0
    ).astype(BF)
    for x in range(4):
        out_ref[x, 2 * COLS :, :] = tail


def pack_keys(own_ref, one_ref, two_ref, seg_ref, out_ref):
    tail = jnp.concatenate(
        [seg_ref[...].astype(F32), jnp.zeros((15, TOK), F32)], axis=0
    ).astype(BF)
    for s, ref in enumerate((own_ref, one_ref, two_ref)):
        for half in range(2):
            part = ref[half * HALF : (half + 1) * HALF, :]
            for r in range(GROUP):
                out_ref[2 * r + half, s * HALF : (s + 1) * HALF, :] = part
    for i in range(2 * GROUP):
        out_ref[i, SLOTS * HALF :, :] = tail


def position():
    return (
        lax.axis_index("zg"),
        lax.axis_index("zr"),
        lax.axis_index("xh"),
        lax.axis_index("core"),
        lax.axis_index("pair"),
    )


def slot_count(zg):
    return jnp.where(zg == 3, 1, zg + 1)


def key_block(kv_ref, kind, s):
    first = s * HALF if isinstance(s, int) else pl.multiple_of(s * HALF, HALF)
    return kv_ref[:, kind, pl.ds(first, HALF), :].reshape(KEYS, HEAD)


def key_segments(kv_ref, pair, turn_ref, seg_ref):
    for r in range(GROUP):
        row = kv_ref[r, 0, SLOTS * HALF :, :].astype(F32)[0:1]
        turn_ref[...] = jnp.broadcast_to(row, (TOK, TOK)).T
        seg_ref[r * HALF : (r + 1) * HALF, :] = turn_ref[
            pl.ds(pl.multiple_of(pair * HALF, HALF), HALF), :
        ]


def allowed_pairs(place, q_ref, x, other, seg_ref):
    zg, zr, xh, core, pair = place
    row = lax.broadcasted_iota(jnp.int32, (KEYS, TOK), 0)
    key_pos = (row // HALF) * 512 + row % HALF + ((2 * xh + core) * TOK + pair * HALF)
    from_core = (1 - core) if other else core
    lane = lax.broadcasted_iota(jnp.int32, (KEYS, TOK), 1)
    query_pos = lane + (zr * 512 + (2 * (x // 2) + from_core) * TOK)
    query_seg = q_ref[x, 2 * COLS :, :].astype(F32)[8:9]
    return (key_pos <= query_pos) & (seg_ref[...] == query_seg)


def tiled(mask):
    return jnp.concatenate([mask] * HEADS, axis=1)


def row_sums(same_ref, other_ref, kv_ref, out_ref, turn_ref, seg_ref):
    place = position()
    zg, zr, xh, core, pair = place
    count = slot_count(zg)
    key_segments(kv_ref, pair, turn_ref, seg_ref)

    for other, q_ref in enumerate((same_ref, other_ref)):
        from_core = (1 - core) if other else core

        def source(x, _, q_ref=q_ref, other=other, from_core=from_core):
            q = q_ref[x, :COLS, :]
            allowed = tiled(allowed_pairs(place, q_ref, x, other, seg_ref))
            s = dot(key_block(kv_ref, 0, 0), q, NT) * SCALE2
            s = jnp.where(allowed, s, NEGATIVE)
            top = jnp.maximum(jnp.max(s, axis=0, keepdims=True), 0.1 * NEGATIVE)
            total = jnp.sum(jnp.exp2(s - top), axis=0, keepdims=True)

            def block(j, state):
                top, total = state
                s = dot(key_block(kv_ref, 0, j), q, NT) * SCALE2
                new_top = jnp.maximum(top, jnp.max(s, axis=0, keepdims=True))
                part = jnp.sum(jnp.exp2(s - new_top), axis=0, keepdims=True)
                return new_top, total * jnp.exp2(top - new_top) + part

            top, total = lax.fori_loop(1, count, block, (top, total))
            norm = jnp.maximum(top + jnp.log2(total), NEGATIVE)
            for h in range(HEADS):
                piece = jnp.broadcast_to(norm[:, h * TOK : (h + 1) * TOK], (8, TOK))
                out_ref[:, from_core, x, h : h + 1, :] = piece.reshape(8, 1, TOK)
            return 0

        lax.fori_loop(0, 4, source, 0)


def gradients(
    same_ref, other_ref, kv_ref, norm_ref,
    dq_same_ref, dq_other_ref, dkv_ref,
    turn_ref, seg_ref, log_ref, turned_ref, dk_ref, dv_ref,
):
    place = position()
    zg, zr, xh, core, pair = place
    count = slot_count(zg)
    key_segments(kv_ref, pair, turn_ref, seg_ref)
    norms = norm_ref[...]
    top = jnp.max(norms, axis=0)
    log_ref[...] = top + jnp.log2(jnp.sum(jnp.exp2(norms - top[None]), axis=0)) - LOG_SCALE
    for s in range(SLOTS):
        turned_ref[s] = key_block(kv_ref, 0, s).astype(F32).T.astype(BF)
    dk_ref[...] = jnp.zeros_like(dk_ref)
    dv_ref[...] = jnp.zeros_like(dv_ref)

    for other, q_ref, dq_ref in ((1, other_ref, dq_other_ref), (0, same_ref, dq_same_ref)):
        from_core = (1 - core) if other else core

        def source(x, _, q_ref=q_ref, dq_ref=dq_ref, other=other, from_core=from_core):
            q = q_ref[x, :COLS, :]
            cot = q_ref[x, COLS : 2 * COLS, :]
            tail = q_ref[x, 2 * COLS :, :].astype(F32)
            delta = tail[0:HEADS] + tail[HEADS : 2 * HEADS]
            delta = jnp.concatenate([delta[h : h + 1] for h in range(HEADS)], axis=1)
            norms = log_ref[from_core, x]
            norm = jnp.concatenate([norms[h : h + 1] for h in range(HEADS)], axis=1)

            def block(j, allowed):
                s = dot(key_block(kv_ref, 0, j), q, NT)
                prob = jnp.exp2(s * SCALE2 - norm)
                if allowed is not None:
                    prob = jnp.where(allowed, prob, 0.0)
                dprob = dot(key_block(kv_ref, 1, j), cot, NT)
                dscore = (prob * (dprob - delta)).astype(BF)
                dk_ref[j] += dot(dscore, q, NN)
                dv_ref[j] += dot(prob.astype(BF), cot, NN)
                return dot(turned_ref[j], dscore, NN)

            dq = block(0, tiled(allowed_pairs(place, q_ref, x, other, seg_ref)))
            dq = lax.fori_loop(1, count, lambda j, dq: dq + block(j, None), dq)
            dq_ref[x] = dq.astype(BF)
            return 0

        lax.fori_loop(0, 4, source, 0)

    for s in range(SLOTS):
        for r in range(GROUP):
            rows = slice(r * HALF, (r + 1) * HALF)
            dkv_ref[2 * r, s] = dk_ref[s, rows, :].astype(BF)
            dkv_ref[2 * r + 1, s] = (dv_ref[s, rows, :] * (1.0 / SCALE)).astype(BF)


def add_parts(dkv_ref, same_ref, other_ref, own_ref, one_ref, two_ref, dq_ref):
    for s, ref in enumerate((own_ref, one_ref, two_ref)):
        for half in range(2):
            total = dkv_ref[half, s].astype(F32)
            for r in range(1, GROUP):
                total += dkv_ref[2 * r + half, s].astype(F32)
            ref[half * HALF : (half + 1) * HALF, :] = total.astype(ref.dtype)
    dq_ref[...] = (same_ref[...].astype(F32) + other_ref[...].astype(F32)).astype(BF)


def finish(dq_ref, own_ref, one_ref, two_ref, out_q_ref, out_kv_ref):
    total = dq_ref[0].astype(F32)
    for x in range(1, 4):
        total += dq_ref[x].astype(F32)
    for h in range(HEADS):
        lanes = slice(h * HEAD, (h + 1) * HEAD)
        out_q_ref[:, lanes] = total[:, lanes].T.astype(BF)
    out_kv_ref[...] = (
        own_ref[...] + one_ref[...].astype(F32) + two_ref[...].astype(F32)
    ).astype(BF)


def per_device(queries, stored_key_value, out_grad, attn_out, segment_ids, loss_mask):
    seg = segment_ids.reshape(1, TOK)
    mask = loss_mask.reshape(1, TOK)
    swap = [(0, 1), (1, 0)]

    one = lax.ppermute(stored_key_value, "zg", [(0, 1), (1, 2)])
    two = lax.ppermute(stored_key_value, "zg", [(0, 2)])
    packed = call(pack_queries, "pack_queries", shape((4, Q_ROWS, HEAD), BF))(
        queries, out_grad, attn_out, seg, mask
    )
    same = lax.all_to_all(packed, X_AXES, 0, 0, tiled=True)
    other = lax.ppermute(same, "core", swap)
    kv_packed = call(pack_keys, "pack_keys", shape((2 * GROUP, KV_ROWS, HEAD), BF))(
        stored_key_value, one, two, seg
    )
    kv = lax.all_to_all(kv_packed, ("zr", "pair"), 0, 0, tiled=True)
    kv = kv.reshape(GROUP, 2, KV_ROWS, HEAD)

    segs = [pltpu.VMEM((TOK, TOK), F32), pltpu.VMEM((KEYS, TOK), F32)]
    norms = call(row_sums, "row_sums", shape((8, 2, 4, HEADS, TOK), F32), segs)(same, other, kv)
    norms = lax.all_to_all(norms, PLANE, 0, 0, tiled=True)

    dq_same, dq_other, dkv = call(
        gradients,
        "gradients",
        (
            shape((4, HEAD, COLS), BF),
            shape((4, HEAD, COLS), BF),
            shape((2 * GROUP, SLOTS, HALF, HEAD), BF),
        ),
        segs
        + [
            pltpu.VMEM((2, 4, HEADS, TOK), F32),
            pltpu.VMEM((SLOTS, HEAD, KEYS), BF),
            pltpu.VMEM((SLOTS, KEYS, HEAD), F32),
            pltpu.VMEM((SLOTS, KEYS, HEAD), F32),
        ],
    )(same, other, kv, norms)
    dq_other = lax.ppermute(dq_other, "core", swap)
    dkv = lax.all_to_all(dkv, ("zr", "pair"), 0, 0, tiled=True)

    own, one, two, dq = call(
        add_parts,
        "add_parts",
        (
            shape((TOK, HEAD), F32),
            shape((TOK, HEAD), BF),
            shape((TOK, HEAD), BF),
            shape((4, HEAD, COLS), BF),
        ),
    )(dkv, dq_same, dq_other)
    one = lax.ppermute(one, "zg", [(1, 0), (2, 1)])
    two = lax.ppermute(two, "zg", [(2, 0)])
    dq = lax.all_to_all(dq, X_AXES, 0, 0, tiled=True)
    return call(
        finish, "finish", (shape((TOK, HEADS * HEAD), BF), shape((TOK, HEAD), BF))
    )(dq, own, one, two)


def solution(mesh):
    fine = Mesh(
        mesh.devices.reshape(4, 4, 2, 2, 4, 2), ("zg", "zr", "xh", "core", "tp", "pair")
    )
    rows = ("zg", "zr", "xh", "core")
    wide = P(rows, ("tp", "pair"))
    return jax.shard_map(
        per_device,
        mesh=fine,
        in_specs=(wide, wide, wide, wide, P(rows), P(rows)),
        out_specs=(wide, wide),
        check_vma=False,
    )
```

time: 732 us -> 124 us (0.17)
  waiting for transfers between devices: 414 us -> 47.8 us
  matrix products: 88.2 us -> 0 us
  blocking collectives: 87.8 us -> 10.2 us
  local copies, waits for them, and re-layouts: 68.3 us -> 3.3 us
  starting transfers between devices: 2.6 us -> 39.4 us
  other arithmetic: 30.6 us -> 0 us
  loops' own time: 23.2 us -> 0 us
  Pallas kernels: 0 us -> 21 us
  between operations: 13.9 us -> 0.74 us
    reduce_scatter x1 -> x0, waiting for transfers between devices: 216 us -> none  [per_device(): lax.psum_scatter(own_part + partner_part.astype(jnp.float32), 'seq', scat...]
    all_gather x2 -> x0, waiting for transfers between devices: 150 us -> none  [the longest x1 90.2 us: per_device(): lax.all_gather(kv_pair, 'seq', axis=0, tiled=True)]
    dot_general x96 -> x0, matrix products: 88.2 us -> none  [the longest x32 40.2 us: masked_scores(): jnp.einsum('thd,wd->htw', q_heads, key_block, preferred_element_type=jnp....]
    all_gather x2 -> x0, blocking collectives: 87.8 us -> none  [the longest x1 83 us: per_device(): lax.all_gather(segment_ids, 'seq', axis=0, tiled=True)]
    dynamic_slice x96 -> x0, local copies, waits for them, and re-layouts: 41.7 us -> none  [the longest x32 20.5 us: add_rows(): current = lax.dynamic_slice_in_dim(total, row_first, term.shape[0], 0)]
    another operation x2 -> x0, loops' own time: 23.2 us -> none  [over_blocks(): lax.scan(one_block, running, jnp.arange(row_count // blk_rows, dtype=jnp....]
    pallas_call x0 -> x6, Pallas kernels: none -> 21 us  [the longest x1 7.69 us: per_device(): call(gradients, 'gradients', (shape((4, HEAD, COLS), BF), shape((4, HEAD,...]
    ppermute x1 -> x6, starting transfers between devices: 2.48 us -> 23.4 us  [the longest x1 9.08 us: per_device(): one = lax.ppermute(stored_key_value, 'zg', [(0, 1), (1, 2)])]
  transfers between devices with their start and end apart: 4 -> 10, of which waited for: 4 -> 6; matrix products, arithmetic and copies ran while one was open for 7% -> 0% of each run, Pallas kernels for 0% -> 1%
where the time goes in v1:
time: 124 us; the launch traced here: 122 us
  waiting for transfers between devices  47.8 us (39%)
  starting transfers between devices  39.4 us (32%)
  Pallas kernels  21 us (17%)
  blocking collectives  10.2 us (8%)
  local copies, waits for them, and re-layouts  3.3 us (3%)
    ppermute x1, waiting for transfers between devices, per_device(): two = lax.ppermute(two, 'zg', [(2, 0)])  15.6 us
    ppermute x1, waiting for transfers between devices, per_device(): one = lax.ppermute(one, 'zg', [(1, 0), (2, 1)])  11.9 us
    all_to_all x1, blocking collectives, per_device(): norms = lax.all_to_all(norms, PLANE, 0, 0, tiled=True)  10.2 us
    ppermute x1, starting transfers between devices, per_device(): one = lax.ppermute(stored_key_value, 'zg', [(0, 1), (1, 2)])  9.08 us
    all_to_all x1, waiting for transfers between devices, per_device(): kv = lax.all_to_all(kv_packed, ('zr', 'pair'), 0, 0, tiled=True)  9.05 us
    ppermute x1, starting transfers between devices, per_device(): two = lax.ppermute(stored_key_value, 'zg', [(0, 2)])  7.92 us
    pallas_call x1, Pallas kernels, per_device(): call(gradients, 'gradients', (shape((4, HEAD, COLS), BF), shape((4, HEAD,...  7.69 us
    all_to_all x1, waiting for transfers between devices, per_device(): dkv = lax.all_to_all(dkv, ('zr', 'pair'), 0, 0, tiled=True)  7.54 us
  transfers between devices with their start and end apart: 10, of which 6 were waited for; matrix products, arithmetic and copies ran while one was open for 0% of the time, Pallas kernels for 1%

profile of v1, /device:TPU:24, one launch (start us, length us, event | category | flops | bytes accessed | tf_op | source)
XLA Modules:
  0.0 122.5 jit_solution(12238819985765703741)
XLA Ops:
  0.6 2.3 %pack_queries.1 = bf16[4,1040,128]{2,1,0:T(8,128)(2,1)} custom-call(bf16[128,512]{1,0:T(8,128)(2,1)} %q_ref.1, bf16[128,512]{1,0:T(8,128)(2,1)} %g_ref.1, bf16[128,512]{1,0:T(8,128)(2,1)} %o_ref.1, s32[1,128]{1,0:T(1,128)} %bitcast.5, s32[1,128]{1,0:T(1,128)} %bitcast.7), custom_call_target="tpu_custom_call" | custom-call | tf_op jit(solution)/shard_map/pack_queries/pallas_call | solution.py:246
  2.9 4.4 %all-to-all-start = ((bf16[4,1040,128]{2,1,0:T(8,128)(2,1)}), bf16[4,1040,128]{2,1,0:T(8,128)(2,1)S(1)}, u32[]{:S(2)}, u32[]{:S(2)}) async-start(bf16[4,1040,128]{2,1,0:T(8,128)(2,1)} %pack_queries.1), calls=%async_computation | async-start | bytes 2129920 | tf_op jit(solution)/shard_map/all_to_all | solution.py:249
  7.3 9.1 %collective-permute-start.1 = (bf16[128,128]{1,0:T(8,128)(2,1)S(1)}, bf16[128,128]{1,0:T(8,128)(2,1)S(1)}, u32[]{:S(2)}, u32[]{:S(2)}) collective-permute-start(bf16[128,128]{1,0:T(8,128)(2,1)S(1)} %copy-done.6), channel_id=1, source_target_pairs={{0,128},{128,256},{1,129},{129,257},{2,130},{130,258},{3,131},{131... | collective-permute-start | bytes 98312 | tf_op jit(solution)/shard_map/ppermute | solution.py:244
  16.4 7.9 %collective-permute-start.2 = (bf16[128,128]{1,0:T(8,128)(2,1)S(1)}, bf16[128,128]{1,0:T(8,128)(2,1)S(1)}, u32[]{:S(2)}, u32[]{:S(2)}) collective-permute-start(bf16[128,128]{1,0:T(8,128)(2,1)S(1)} %copy-done.6), channel_id=1, source_target_pairs={{0,256},{1,257},{2,258},{3,259},{4,260},{5,261},{6,262},{7,263},{8... | collective-permute-start | bytes 98312 | tf_op jit(solution)/shard_map/ppermute | solution.py:245
  24.4 1.6 %collective-permute-done.2.two_ref = bf16[128,128]{1,0:T(8,128)(2,1)S(1)} collective-permute-done((bf16[128,128]{1,0:T(8,128)(2,1)S(1)}, bf16[128,128]{1,0:T(8,128)(2,1)S(1)}, u32[]{:S(2)}, u32[]{:S(2)}) %collective-permute-start.2) | collective-permute-done | bytes 32800 | tf_op jit(solution)/shard_map/ppermute | solution.py:245
  26.6 1.6 %pack_keys.1 = bf16[8,208,128]{2,1,0:T(8,128)(2,1)} custom-call(bf16[128,128]{1,0:T(8,128)(2,1)} %own_ref.1, bf16[128,128]{1,0:T(8,128)(2,1)} %copy-done.9, bf16[128,128]{1,0:T(8,128)(2,1)} %copy-done.10, s32[1,128]{1,0:T(1,128)} %bitcast.6), custom_call_target="tpu_custom_call" | custom-call | tf_op jit(solution)/shard_map/pack_keys/pallas_call | solution.py:251
  28.2 4.7 %all-to-all-start.1 = ((bf16[8,208,128]{2,1,0:T(8,128)(2,1)}), bf16[8,208,128]{2,1,0:T(8,128)(2,1)S(1)}, u32[]{:S(2)}, u32[]{:S(2)}) async-start(bf16[8,208,128]{2,1,0:T(8,128)(2,1)} %pack_keys.1), calls=%async_computation.1 | async-start | bytes 851968 | tf_op jit(solution)/shard_map/all_to_all | solution.py:254
  32.8 1.9 %collective-permute-start = (bf16[4,1040,128]{2,1,0:T(8,128)(2,1)S(1)}, bf16[4,1040,128]{2,1,0:T(8,128)(2,1)S(1)}, u32[]{:S(2)}, u32[]{:S(2)}) collective-permute-start(bf16[4,1040,128]{2,1,0:T(8,128)(2,1)S(1)} %all-to-all-done.same_ref), channel_id=1, source_target_pairs={{0,8},{8,0},{1,9},{9,1},{2,10},{10,2},{3,11},{11,3},{4,12},{12,4},... | collective-permute-start | bytes 3194888 | tf_op jit(solution)/shard_map/ppermute | solution.py:250
  34.7 9.0 %all-to-all-done.1 = bf16[8,208,128]{2,1,0:T(8,128)(2,1)S(1)} async-done(((bf16[8,208,128]{2,1,0:T(8,128)(2,1)}), bf16[8,208,128]{2,1,0:T(8,128)(2,1)S(1)}, u32[]{:S(2)}, u32[]{:S(2)}) %all-to-all-start.1) | async-done | bytes 426016 | tf_op jit(solution)/shard_map/all_to_all | solution.py:254
  44.9 5.3 %row_sums.1 = f32[8,2,4,4,128]{4,3,2,1,0:T(4,128)} custom-call(bf16[4,1040,128]{2,1,0:T(8,128)(2,1)} %copy-done, bf16[4,1040,128]{2,1,0:T(8,128)(2,1)} %copy-done.1, bf16[4,2,208,128]{3,2,1,0:T(8,128)(2,1)} %bitcast.3), custom_call_target="tpu_custom_call" | custom-call | tf_op jit(solution)/shard_map/row_sums/pallas_call | solution.py:258
  50.2 10.2 %all_to_all.25.norm_ref = f32[8,2,4,4,128]{4,3,2,1,0:T(4,128)} all-to-all(f32[8,2,4,4,128]{4,3,2,1,0:T(4,128)} %row_sums.1), channel_id=1, replica_groups=mesh['zg'=4,'zr'=4,'xh'=2,'core'=2,'tp'=4,'pair'=2] {'xh','core','pair'}, dimensions={0} | all-to-all | bytes 262144 | tf_op jit(solution)/shard_map/all_to_all | solution.py:259
  60.4 7.7 %gradients.1 = (bf16[4,128,512]{2,1,0:T(8,128)(2,1)}, bf16[4,128,512]{2,1,0:T(8,128)(2,1)}, bf16[8,3,64,128]{3,2,1,0:T(8,128)(2,1)}) custom-call(bf16[4,1040,128]{2,1,0:T(8,128)(2,1)} %copy-done, bf16[4,1040,128]{2,1,0:T(8,128)(2,1)} %copy-done.1, bf16[4,2,208,128]{3,2,1,0:T(8,128)(2,1)} %bitcast.4, f32[8,2,4,4,128]{4,3,2,1,0:T(4,128)} %all_to_all.25.norm_ref), custom_call_target="tpu_custom_call" | custom-call | tf_op jit(solution)/shard_map/gradients/pallas_call | solution.py:261
  68.1 3.5 %all-to-all-start.3 = ((bf16[8,3,64,128]{3,2,1,0:T(8,128)(2,1)}), bf16[8,3,64,128]{3,2,1,0:T(8,128)(2,1)S(1)}, u32[]{:S(2)}, u32[]{:S(2)}) async-start(bf16[8,3,64,128]{3,2,1,0:T(8,128)(2,1)} %get-tuple-element.9), calls=%async_computation.3 | async-start | bytes 786432 | tf_op jit(solution)/shard_map/all_to_all | solution.py:278
  71.6 1.9 %collective-permute-start.3 = (bf16[4,128,512]{2,1,0:T(8,128)(2,1)}, bf16[4,128,512]{2,1,0:T(8,128)(2,1)S(1)}, u32[]{:S(2)}, u32[]{:S(2)}) collective-permute-start(bf16[4,128,512]{2,1,0:T(8,128)(2,1)} %get-tuple-element.11), channel_id=1, source_target_pairs={{0,8},{8,0},{1,9},{9,1},{2,10},{10,2},{3,11},{11,3},{4,12},{12,4},... | collective-permute-start | bytes 1572872 | tf_op jit(solution)/shard_map/ppermute | solution.py:277
  73.5 2.1 %collective-permute-done.3.other_ref = bf16[4,128,512]{2,1,0:T(8,128)(2,1)S(1)} collective-permute-done((bf16[4,128,512]{2,1,0:T(8,128)(2,1)}, bf16[4,128,512]{2,1,0:T(8,128)(2,1)S(1)}, u32[]{:S(2)}, u32[]{:S(2)}) %collective-permute-start.3) | collective-permute-done | bytes 524320 | tf_op jit(solution)/shard_map/ppermute | solution.py:277
  75.6 7.5 %all-to-all-done.3.dkv_ref = bf16[8,3,64,128]{3,2,1,0:T(8,128)(2,1)S(1)} async-done(((bf16[8,3,64,128]{3,2,1,0:T(8,128)(2,1)}), bf16[8,3,64,128]{3,2,1,0:T(8,128)(2,1)S(1)}, u32[]{:S(2)}, u32[]{:S(2)}) %all-to-all-start.3) | async-done | bytes 393248 | tf_op jit(solution)/shard_map/all_to_all | solution.py:278
  83.1 0.7 copy-done.4
  83.9 2.3 %add_parts.1 = (f32[128,128]{1,0:T(8,128)}, bf16[128,128]{1,0:T(8,128)(2,1)}, bf16[128,128]{1,0:T(8,128)(2,1)}, bf16[4,128,512]{2,1,0:T(8,128)(2,1)}) custom-call(bf16[8,3,64,128]{3,2,1,0:T(8,128)(2,1)} %copy-done.4, bf16[4,128,512]{2,1,0:T(8,128)(2,1)} %get-tuple-element.10.same_ref, bf16[4,128,512]{2,1,0:T(8,128)(2,1)} %copy-done.5), custom_call_target="tpu_custom_call" | custom-call | tf_op jit(solution)/shard_map/add_parts/pallas_call | solution.py:280
  86.2 3.5 %all-to-all-start.4 = ((bf16[4,128,512]{2,1,0:T(8,128)(2,1)}), bf16[4,128,512]{2,1,0:T(8,128)(2,1)S(1)}, u32[]{:S(2)}, u32[]{:S(2)}) async-start(bf16[4,128,512]{2,1,0:T(8,128)(2,1)} %get-tuple-element.12), calls=%async_computation.4 | async-start | bytes 1048576 | tf_op jit(solution)/shard_map/all_to_all | solution.py:292
  89.6 1.3 %collective-permute-start.4 = (bf16[128,128]{1,0:T(8,128)(2,1)}, bf16[128,128]{1,0:T(8,128)(2,1)S(1)}, u32[]{:S(2)}, u32[]{:S(2)}) collective-permute-start(bf16[128,128]{1,0:T(8,128)(2,1)} %get-tuple-element.14), channel_id=1, source_target_pairs={{128,0},{256,128},{129,1},{257,129},{130,2},{258,130},{131,3},{259... | collective-permute-start | bytes 98312 | tf_op jit(solution)/shard_map/ppermute | solution.py:290
  90.9 1.3 %collective-permute-start.5 = (bf16[128,128]{1,0:T(8,128)(2,1)}, bf16[128,128]{1,0:T(8,128)(2,1)S(1)}, u32[]{:S(2)}, u32[]{:S(2)}) collective-permute-start(bf16[128,128]{1,0:T(8,128)(2,1)} %get-tuple-element.15), channel_id=1, source_target_pairs={{256,0},{257,1},{258,2},{259,3},{260,4},{261,5},{262,6},{263,7},{2... | collective-permute-start | bytes 98312 | tf_op jit(solution)/shard_map/ppermute | solution.py:291
  92.2 11.9 %collective-permute-done.4.one_ref = bf16[128,128]{1,0:T(8,128)(2,1)S(1)} collective-permute-done((bf16[128,128]{1,0:T(8,128)(2,1)}, bf16[128,128]{1,0:T(8,128)(2,1)S(1)}, u32[]{:S(2)}, u32[]{:S(2)}) %collective-permute-start.4) | collective-permute-done | bytes 32800 | tf_op jit(solution)/shard_map/ppermute | solution.py:290
  104.2 15.6 %collective-permute-done.5.two_ref = bf16[128,128]{1,0:T(8,128)(2,1)S(1)} collective-permute-done((bf16[128,128]{1,0:T(8,128)(2,1)}, bf16[128,128]{1,0:T(8,128)(2,1)S(1)}, u32[]{:S(2)}, u32[]{:S(2)}) %collective-permute-start.5) | collective-permute-done | bytes 32800 | tf_op jit(solution)/shard_map/ppermute | solution.py:291
  120.6 1.9 %finish.1 = (bf16[128,512]{1,0:T(8,128)(2,1)}, bf16[128,128]{1,0:T(8,128)(2,1)}) custom-call(bf16[4,128,512]{2,1,0:T(8,128)(2,1)} %copy-done.3, f32[128,128]{1,0:T(8,128)} %get-tuple-element.13.own_ref, bf16[128,128]{1,0:T(8,128)(2,1)} %copy-done.7, bf16[128,128]{1,0:T(8,128)(2,1)} %copy-done.8), custom_call_target="tpu_custom_call" | custom-call | tf_op jit(solution)/shard_map/finish/pallas_call | solution.py:293
  (25 shorter events, 2.6 us)
Async XLA Ops:
  2.9 4.4 %copy-start.6 = (bf16[128,128]{1,0:T(8,128)(2,1)S(1)}, bf16[128,128]{1,0:T(8,128)(2,1)}, u32[]{:S(2)}) copy-start(bf16[128,128]{1,0:T(8,128)(2,1)} %own_ref.1) | copy-start | bytes 98308
  2.9 25.2 %all-to-all-start = ((bf16[4,1040,128]{2,1,0:T(8,128)(2,1)}), bf16[4,1040,128]{2,1,0:T(8,128)(2,1)S(1)}, u32[]{:S(2)}, u32[]{:S(2)}) async-start(bf16[4,1040,128]{2,1,0:T(8,128)(2,1)} %pack_queries.1), calls=%async_computation | async-start | bytes 2129920 | tf_op jit(solution)/shard_map/all_to_all | solution.py:249
  7.3 17.0 %collective-permute-start.1 = (bf16[128,128]{1,0:T(8,128)(2,1)S(1)}, bf16[128,128]{1,0:T(8,128)(2,1)S(1)}, u32[]{:S(2)}, u32[]{:S(2)}) collective-permute-start(bf16[128,128]{1,0:T(8,128)(2,1)S(1)} %copy-done.6), channel_id=1, source_target_pairs={{0,128},{128,256},{1,129},{129,257},{2,130},{130,258},{3,131},{131... | collective-permute-start | bytes 98312 | tf_op jit(solution)/shard_map/ppermute | solution.py:244
  16.4 9.5 %collective-permute-start.2 = (bf16[128,128]{1,0:T(8,128)(2,1)S(1)}, bf16[128,128]{1,0:T(8,128)(2,1)S(1)}, u32[]{:S(2)}, u32[]{:S(2)}) collective-permute-start(bf16[128,128]{1,0:T(8,128)(2,1)S(1)} %copy-done.6), channel_id=1, source_target_pairs={{0,256},{1,257},{2,258},{3,259},{4,260},{5,261},{6,262},{7,263},{8... | collective-permute-start | bytes 98312 | tf_op jit(solution)/shard_map/ppermute | solution.py:245
  24.4 1.6 %copy-start.9 = (bf16[128,128]{1,0:T(8,128)(2,1)}, bf16[128,128]{1,0:T(8,128)(2,1)S(1)}, u32[]{:S(2)}) copy-start(bf16[128,128]{1,0:T(8,128)(2,1)S(1)} %collective-permute-done.1.one_ref) | copy-start | bytes 98308
  25.9 0.6 copy-start.10
  28.2 15.6 %copy-start = (bf16[4,1040,128]{2,1,0:T(8,128)(2,1)}, bf16[4,1040,128]{2,1,0:T(8,128)(2,1)S(1)}, u32[]{:S(2)}) copy-start(bf16[4,1040,128]{2,1,0:T(8,128)(2,1)S(1)} %all-to-all-done.same_ref) | copy-start | bytes 3194884
  28.2 15.6 %all-to-all-start.1 = ((bf16[8,208,128]{2,1,0:T(8,128)(2,1)}), bf16[8,208,128]{2,1,0:T(8,128)(2,1)S(1)}, u32[]{:S(2)}, u32[]{:S(2)}) async-start(bf16[8,208,128]{2,1,0:T(8,128)(2,1)} %pack_keys.1), calls=%async_computation.1 | async-start | bytes 851968 | tf_op jit(solution)/shard_map/all_to_all | solution.py:254
  32.8 11.0 %collective-permute-start = (bf16[4,1040,128]{2,1,0:T(8,128)(2,1)S(1)}, bf16[4,1040,128]{2,1,0:T(8,128)(2,1)S(1)}, u32[]{:S(2)}, u32[]{:S(2)}) collective-permute-start(bf16[4,1040,128]{2,1,0:T(8,128)(2,1)S(1)} %all-to-all-done.same_ref), channel_id=1, source_target_pairs={{0,8},{8,0},{1,9},{9,1},{2,10},{10,2},{3,11},{11,3},{4,12},{12,4},... | collective-permute-start | bytes 3194888 | tf_op jit(solution)/shard_map/ppermute | solution.py:250
  43.8 0.8 copy-start.2
  43.8 1.1 copy-start.1
  68.1 15.0 %all-to-all-start.3 = ((bf16[8,3,64,128]{3,2,1,0:T(8,128)(2,1)}), bf16[8,3,64,128]{3,2,1,0:T(8,128)(2,1)S(1)}, u32[]{:S(2)}, u32[]{:S(2)}) async-start(bf16[8,3,64,128]{3,2,1,0:T(8,128)(2,1)} %get-tuple-element.9), calls=%async_computation.3 | async-start | bytes 786432 | tf_op jit(solution)/shard_map/all_to_all | solution.py:278
  71.6 4.0 %collective-permute-start.3 = (bf16[4,128,512]{2,1,0:T(8,128)(2,1)}, bf16[4,128,512]{2,1,0:T(8,128)(2,1)S(1)}, u32[]{:S(2)}, u32[]{:S(2)}) collective-permute-start(bf16[4,128,512]{2,1,0:T(8,128)(2,1)} %get-tuple-element.11), channel_id=1, source_target_pairs={{0,8},{8,0},{1,9},{9,1},{2,10},{10,2},{3,11},{11,3},{4,12},{12,4},... | collective-permute-start | bytes 1572872 | tf_op jit(solution)/shard_map/ppermute | solution.py:277
  75.6 7.5 %copy-start.5 = (bf16[4,128,512]{2,1,0:T(8,128)(2,1)}, bf16[4,128,512]{2,1,0:T(8,128)(2,1)S(1)}, u32[]{:S(2)}) copy-start(bf16[4,128,512]{2,1,0:T(8,128)(2,1)S(1)} %collective-permute-done.3.other_ref) | copy-start | bytes 1572868
  83.1 0.7 copy-start.4
  86.2 33.6 %all-to-all-start.4 = ((bf16[4,128,512]{2,1,0:T(8,128)(2,1)}), bf16[4,128,512]{2,1,0:T(8,128)(2,1)S(1)}, u32[]{:S(2)}, u32[]{:S(2)}) async-start(bf16[4,128,512]{2,1,0:T(8,128)(2,1)} %get-tuple-element.12), calls=%async_computation.4 | async-start | bytes 1048576 | tf_op jit(solution)/shard_map/all_to_all | solution.py:292
  89.6 14.5 %collective-permute-start.4 = (bf16[128,128]{1,0:T(8,128)(2,1)}, bf16[128,128]{1,0:T(8,128)(2,1)S(1)}, u32[]{:S(2)}, u32[]{:S(2)}) collective-permute-start(bf16[128,128]{1,0:T(8,128)(2,1)} %get-tuple-element.14), channel_id=1, source_target_pairs={{128,0},{256,128},{129,1},{257,129},{130,2},{258,130},{131,3},{259... | collective-permute-start | bytes 98312 | tf_op jit(solution)/shard_map/ppermute | solution.py:290
  90.9 28.8 %collective-permute-start.5 = (bf16[128,128]{1,0:T(8,128)(2,1)}, bf16[128,128]{1,0:T(8,128)(2,1)S(1)}, u32[]{:S(2)}, u32[]{:S(2)}) collective-permute-start(bf16[128,128]{1,0:T(8,128)(2,1)} %get-tuple-element.15), channel_id=1, source_target_pairs={{256,0},{257,1},{258,2},{259,3},{260,4},{261,5},{262,6},{263,7},{2... | collective-permute-start | bytes 98312 | tf_op jit(solution)/shard_map/ppermute | solution.py:291
  104.2 15.6 %copy-start.7 = (bf16[128,128]{1,0:T(8,128)(2,1)}, bf16[128,128]{1,0:T(8,128)(2,1)S(1)}, u32[]{:S(2)}) copy-start(bf16[128,128]{1,0:T(8,128)(2,1)S(1)} %collective-permute-done.4.one_ref) | copy-start | bytes 98308
  119.8 0.6 copy-start.8
  119.8 0.8 copy-start.3

commit v2 on v1

--- a/solution.py
+++ b/solution.py
@@ -28,21 +28,26 @@
 PLANE = ("xh", "core", "pair")
 NT = (((1,), (1,)), ((), ()))
 NN = (((1,), (0,)), ((), ()))
-VMEM_LIMIT = 56 * 1024 * 1024
+VMEM_LIMIT = 32 * 1024 * 1024
 
 
 def dot(a, b, dims):
     return lax.dot_general(a, b, dims, preferred_element_type=F32)
 
 
-def call(kernel, name, out_shape, scratch=()):
-    return pl.pallas_call(
+def near(array):
+    return pltpu.with_memory_space_constraint(array, pltpu.VMEM)
+
+
+def call(kernel, name, out_shape, scratch=(), resident=()):
+    run = pl.pallas_call(
         kernel,
         out_shape=out_shape,
         scratch_shapes=scratch,
         name=name,
         compiler_params=pltpu.CompilerParams(vmem_limit_bytes=VMEM_LIMIT),
     )
+    return lambda *args: run(*(near(a) if i in resident else a for i, a in enumerate(args)))
 
 
 def shape(dims, dtype):
@@ -111,14 +116,12 @@
         ]
 
 
-def allowed_pairs(place, q_ref, x, other, seg_ref):
+def allowed_pairs(place, query_seg, hx, from_core, seg_ref):
     zg, zr, xh, core, pair = place
     row = lax.broadcasted_iota(jnp.int32, (KEYS, TOK), 0)
     key_pos = (row // HALF) * 512 + row % HALF + ((2 * xh + core) * TOK + pair * HALF)
-    from_core = (1 - core) if other else core
     lane = lax.broadcasted_iota(jnp.int32, (KEYS, TOK), 1)
-    query_pos = lane + (zr * 512 + (2 * (x // 2) + from_core) * TOK)
-    query_seg = q_ref[x, 2 * COLS :, :].astype(F32)[8:9]
+    query_pos = lane + (zr * 512 + (2 * hx + from_core) * TOK)
     return (key_pos <= query_pos) & (seg_ref[...] == query_seg)
 
 
@@ -126,38 +129,50 @@
     return jnp.concatenate([mask] * HEADS, axis=1)
 
 
+def by_count(place, body):
+    count = slot_count(place[0])
+    for n in (1, 2, 3):
+
+        @pl.when(count == n)
+        def _(n=n):
+            body(n)
+
+
+def flat(rows):
+    return jnp.concatenate([rows[h : h + 1] for h in range(HEADS)], axis=1)
+
+
 def row_sums(same_ref, other_ref, kv_ref, out_ref, turn_ref, seg_ref):
     place = position()
-    zg, zr, xh, core, pair = place
-    count = slot_count(zg)
+    core, pair = place[3:]
     key_segments(kv_ref, pair, turn_ref, seg_ref)
 
-    for other, q_ref in enumerate((same_ref, other_ref)):
-        from_core = (1 - core) if other else core
-
-        def source(x, _, q_ref=q_ref, other=other, from_core=from_core):
-            q = q_ref[x, :COLS, :]
-            allowed = tiled(allowed_pairs(place, q_ref, x, other, seg_ref))
-            s = dot(key_block(kv_ref, 0, 0), q, NT) * SCALE2
-            s = jnp.where(allowed, s, NEGATIVE)
-            top = jnp.maximum(jnp.max(s, axis=0, keepdims=True), 0.1 * NEGATIVE)
-            total = jnp.sum(jnp.exp2(s - top), axis=0, keepdims=True)
-
-            def block(j, state):
-                top, total = state
-                s = dot(key_block(kv_ref, 0, j), q, NT) * SCALE2
-                new_top = jnp.maximum(top, jnp.max(s, axis=0, keepdims=True))
-                part = jnp.sum(jnp.exp2(s - new_top), axis=0, keepdims=True)
-                return new_top, total * jnp.exp2(top - new_top) + part
-
-            top, total = lax.fori_loop(1, count, block, (top, total))
-            norm = jnp.maximum(top + jnp.log2(total), NEGATIVE)
-            for h in range(HEADS):
-                piece = jnp.broadcast_to(norm[:, h * TOK : (h + 1) * TOK], (8, TOK))
-                out_ref[:, from_core, x, h : h + 1, :] = piece.reshape(8, 1, TOK)
+    def body(n):
+        def sources(hx, _):
+            for other, q_ref in enumerate((same_ref, other_ref)):
+                from_core = (1 - core) if other else core
+                segs = q_ref[2 * hx, 2 * COLS :, :].astype(F32)[8:9]
+                allowed = tiled(allowed_pairs(place, segs, hx, from_core, seg_ref))
+                for p in range(2):
+                    x = 2 * hx + p
+                    q = q_ref[x, :COLS, :]
+                    scores = [dot(key_block(kv_ref, 0, j), q, NT) * SCALE2 for j in range(n)]
+                    scores[0] = jnp.where(allowed, scores[0], NEGATIVE)
+                    top = jnp.full((1, COLS), 0.1 * NEGATIVE, F32)
+                    for s in scores:
+                        top = jnp.maximum(top, jnp.max(s, axis=0, keepdims=True))
+                    total = jnp.zeros((1, COLS), F32)
+                    for s in scores:
+                        total += jnp.sum(jnp.exp2(s - top), axis=0, keepdims=True)
+                    norm = jnp.maximum(top + jnp.log2(total), NEGATIVE)
+                    for h in range(HEADS):
+                        piece = jnp.broadcast_to(norm[:, h * TOK : (h + 1) * TOK], (8, TOK))
+                        out_ref[:, from_core, x, h : h + 1, :] = piece.reshape(8, 1, TOK)
             return 0
 
-        lax.fori_loop(0, 4, source, 0)
+        lax.fori_loop(0, 2, sources, 0)
+
+    by_count(place, body)
 
 
 def gradients(
@@ -166,8 +181,7 @@
     turn_ref, seg_ref, log_ref, turned_ref, dk_ref, dv_ref,
 ):
     place = position()
-    zg, zr, xh, core, pair = place
-    count = slot_count(zg)
+    core, pair = place[3:]
     key_segments(kv_ref, pair, turn_ref, seg_ref)
     norms = norm_ref[...]
     top = jnp.max(norms, axis=0)
@@ -177,35 +191,38 @@
     dk_ref[...] = jnp.zeros_like(dk_ref)
     dv_ref[...] = jnp.zeros_like(dv_ref)
 
-    for other, q_ref, dq_ref in ((1, other_ref, dq_other_ref), (0, same_ref, dq_same_ref)):
-        from_core = (1 - core) if other else core
-
-        def source(x, _, q_ref=q_ref, dq_ref=dq_ref, other=other, from_core=from_core):
-            q = q_ref[x, :COLS, :]
-            cot = q_ref[x, COLS : 2 * COLS, :]
-            tail = q_ref[x, 2 * COLS :, :].astype(F32)
-            delta = tail[0:HEADS] + tail[HEADS : 2 * HEADS]
-            delta = jnp.concatenate([delta[h : h + 1] for h in range(HEADS)], axis=1)
-            norms = log_ref[from_core, x]
-            norm = jnp.concatenate([norms[h : h + 1] for h in range(HEADS)], axis=1)
-
-            def block(j, allowed):
-                s = dot(key_block(kv_ref, 0, j), q, NT)
-                prob = jnp.exp2(s * SCALE2 - norm)
-                if allowed is not None:
-                    prob = jnp.where(allowed, prob, 0.0)
-                dprob = dot(key_block(kv_ref, 1, j), cot, NT)
-                dscore = (prob * (dprob - delta)).astype(BF)
-                dk_ref[j] += dot(dscore, q, NN)
-                dv_ref[j] += dot(prob.astype(BF), cot, NN)
-                return dot(turned_ref[j], dscore, NN)
-
-            dq = block(0, tiled(allowed_pairs(place, q_ref, x, other, seg_ref)))
-            dq = lax.fori_loop(1, count, lambda j, dq: dq + block(j, None), dq)
-            dq_ref[x] = dq.astype(BF)
-            return 0
-
-        lax.fori_loop(0, 4, source, 0)
+    def body(n):
+        for other, q_ref, dq_ref in ((1, other_ref, dq_other_ref), (0, same_ref, dq_same_ref)):
+            from_core = (1 - core) if other else core
+
+            def sources(hx, _, q_ref=q_ref, dq_ref=dq_ref, from_core=from_core):
+                segs = q_ref[2 * hx, 2 * COLS :, :].astype(F32)[8:9]
+                allowed = tiled(allowed_pairs(place, segs, hx, from_core, seg_ref))
+                for p in range(2):
+                    x = 2 * hx + p
+                    q = q_ref[x, :COLS, :]
+                    cot = q_ref[x, COLS : 2 * COLS, :]
+                    tail = q_ref[x, 2 * COLS :, :].astype(F32)
+                    delta = flat(tail[0:HEADS] + tail[HEADS : 2 * HEADS])
+                    norm = flat(log_ref[from_core, x])
+                    dq = None
+                    for j in range(n):
+                        s = dot(key_block(kv_ref, 0, j), q, NT)
+                        prob = jnp.exp2(s * SCALE2 - norm)
+                        if j == 0:
+                            prob = jnp.where(allowed, prob, 0.0)
+                        dprob = dot(key_block(kv_ref, 1, j), cot, NT)
+                        dscore = (prob * (dprob - delta)).astype(BF)
+                        dk_ref[j] += dot(dscore, q, NN)
+                        dv_ref[j] += dot(prob.astype(BF), cot, NN)
+                        part = dot(turned_ref[j], dscore, NN)
+                        dq = part if dq is None else dq + part
+                    dq_ref[x] = dq.astype(BF)
+                return 0
+
+            lax.fori_loop(0, 2, sources, 0)
+
+    by_count(place, body)
 
     for s in range(SLOTS):
         for r in range(GROUP):
@@ -248,14 +265,18 @@
     )
     same = lax.all_to_all(packed, X_AXES, 0, 0, tiled=True)
     other = lax.ppermute(same, "core", swap)
-    kv_packed = call(pack_keys, "pack_keys", shape((2 * GROUP, KV_ROWS, HEAD), BF))(
+    kv_packed = call(
+        pack_keys, "pack_keys", shape((2 * GROUP, KV_ROWS, HEAD), BF), resident=(1, 2)
+    )(
         stored_key_value, one, two, seg
     )
     kv = lax.all_to_all(kv_packed, ("zr", "pair"), 0, 0, tiled=True)
     kv = kv.reshape(GROUP, 2, KV_ROWS, HEAD)
 
     segs = [pltpu.VMEM((TOK, TOK), F32), pltpu.VMEM((KEYS, TOK), F32)]
-    norms = call(row_sums, "row_sums", shape((8, 2, 4, HEADS, TOK), F32), segs)(same, other, kv)
+    norms = call(
+        row_sums, "row_sums", shape((8, 2, 4, HEADS, TOK), F32), segs, resident=(0, 1, 2)
+    )(same, other, kv)
     norms = lax.all_to_all(norms, PLANE, 0, 0, tiled=True)
 
     dq_same, dq_other, dkv = call(
@@ -273,6 +294,7 @@
             pltpu.VMEM((SLOTS, KEYS, HEAD), F32),
             pltpu.VMEM((SLOTS, KEYS, HEAD), F32),
         ],
+        resident=(0, 1, 2, 3),
     )(same, other, kv, norms)
     dq_other = lax.ppermute(dq_other, "core", swap)
     dkv = lax.all_to_all(dkv, ("zr", "pair"), 0, 0, tiled=True)
@@ -286,12 +308,16 @@
             shape((TOK, HEAD), BF),
             shape((4, HEAD, COLS), BF),
         ),
+        resident=(0, 1, 2),
     )(dkv, dq_same, dq_other)
     one = lax.ppermute(one, "zg", [(1, 0), (2, 1)])
     two = lax.ppermute(two, "zg", [(2, 0)])
     dq = lax.all_to_all(dq, X_AXES, 0, 0, tiled=True)
     return call(
-        finish, "finish", (shape((TOK, HEADS * HEAD), BF), shape((TOK, HEAD), BF))
+        finish,
+        "finish",
+        (shape((TOK, HEADS * HEAD), BF), shape((TOK, HEAD), BF)),
+        resident=(0, 1, 2, 3),
     )(dq, own, one, two)
 
 

time: 124 us -> 108 us (0.87)
  Pallas kernels: 21 us -> 10.8 us
  waiting for transfers between devices: 47.8 us -> 41.5 us
  local copies, waits for them, and re-layouts: 3.3 us -> 4.82 us
    pallas_call x6, Pallas kernels: 21 us -> 10.8 us  [call(): run(*(near(a) if i in resident else a for i, a in enumerate(args)))]
    ppermute x1, waiting for transfers between devices: 15.6 us -> 12 us  [per_device(): two = lax.ppermute(two, 'zg', [(2, 0)])]
    ppermute x1, waiting for transfers between devices: 11.9 us -> 9.35 us  [per_device(): one = lax.ppermute(one, 'zg', [(1, 0), (2, 1)])]
    unnamed x22 -> x16, local copies, waits for them, and re-layouts: 3.3 us -> 4.82 us
where the time goes in v2:
time: 108 us; the launch traced here: 107 us
  waiting for transfers between devices  41.5 us (38%)
  starting transfers between devices  39.4 us (36%)
  Pallas kernels  10.8 us (10%)
  blocking collectives  9.89 us (9%)
  local copies, waits for them, and re-layouts  4.82 us (4%)
    ppermute x1, waiting for transfers between devices, per_device(): two = lax.ppermute(two, 'zg', [(2, 0)])  12 us
    pallas_call x6, Pallas kernels, call(): run(*(near(a) if i in resident else a for i, a in enumerate(args)))  10.8 us
    all_to_all x1, blocking collectives, per_device(): norms = lax.all_to_all(norms, PLANE, 0, 0, tiled=True)  9.89 us
    ppermute x1, waiting for transfers between devices, per_device(): one = lax.ppermute(one, 'zg', [(1, 0), (2, 1)])  9.35 us
    ppermute x1, starting transfers between devices, per_device(): one = lax.ppermute(stored_key_value, 'zg', [(0, 1), (1, 2)])  9.08 us
    all_to_all x1, waiting for transfers between devices, per_device(): kv = lax.all_to_all(kv_packed, ('zr', 'pair'), 0, 0, tiled=True)  9.05 us
    ppermute x1, starting transfers between devices, per_device(): two = lax.ppermute(stored_key_value, 'zg', [(0, 2)])  7.92 us
    all_to_all x1, waiting for transfers between devices, per_device(): dkv = lax.all_to_all(dkv, ('zr', 'pair'), 0, 0, tiled=True)  7.51 us
  transfers between devices with their start and end apart: 10, of which 6 were waited for; matrix products, arithmetic and copies ran while one was open for 0% of the time, Pallas kernels for 1%

profile of v2, /device:TPU:24, one launch (start us, length us, event | category | flops | bytes accessed | tf_op | source)
XLA Modules:
  0.0 107.2 jit_solution(10416002566178951627)
XLA Ops:
  0.6 0.9 copy-done
  1.5 0.9 copy-done.1
  2.4 0.9 copy-done.2
  4.7 1.2 %pack_queries.1 = bf16[4,1040,128]{2,1,0:T(8,128)(2,1)} custom-call(bf16[128,512]{1,0:T(8,128)(2,1)S(1)} %copy-done, bf16[128,512]{1,0:T(8,128)(2,1)S(1)} %copy-done.1, bf16[128,512]{1,0:T(8,128)(2,1)S(1)} %copy-done.2, s32[1,128]{1,0:T(1,128)S(1)} %bitcast.5, s32[1,128]{1,0:T(1,128)S(1)} %bitcast.7), custom_call_target="tpu_custom_call" | custom-call | tf_op jit(solution)/shard_map/pack_queries/pallas_call | solution.py:50
  5.9 4.4 %all-to-all-start = ((bf16[4,1040,128]{2,1,0:T(8,128)(2,1)}), bf16[4,1040,128]{2,1,0:T(8,128)(2,1)S(1)}, u32[]{:S(2)}, u32[]{:S(2)}) async-start(bf16[4,1040,128]{2,1,0:T(8,128)(2,1)} %pack_queries.1), calls=%async_computation | async-start | bytes 2129920 | tf_op jit(solution)/shard_map/all_to_all | solution.py:266
  10.3 9.1 %collective-permute-start.1 = (bf16[128,128]{1,0:T(8,128)(2,1)S(1)}, bf16[128,128]{1,0:T(8,128)(2,1)S(1)}, u32[]{:S(2)}, u32[]{:S(2)}) collective-permute-start(bf16[128,128]{1,0:T(8,128)(2,1)S(1)} %copy-done.3), channel_id=1, source_target_pairs={{0,128},{128,256},{1,129},{129,257},{2,130},{130,258},{3,131},{131... | collective-permute-start | bytes 98312 | tf_op jit(solution)/shard_map/ppermute | solution.py:261
  19.4 7.9 %collective-permute-start.2 = (bf16[128,128]{1,0:T(8,128)(2,1)S(1)}, bf16[128,128]{1,0:T(8,128)(2,1)S(1)}, u32[]{:S(2)}, u32[]{:S(2)}) collective-permute-start(bf16[128,128]{1,0:T(8,128)(2,1)S(1)} %copy-done.3), channel_id=1, source_target_pairs={{0,256},{1,257},{2,258},{3,259},{4,260},{5,261},{6,262},{7,263},{8... | collective-permute-start | bytes 98312 | tf_op jit(solution)/shard_map/ppermute | solution.py:262
  27.3 1.6 %collective-permute-done.2.two_ref = bf16[128,128]{1,0:T(8,128)(2,1)S(1)} collective-permute-done((bf16[128,128]{1,0:T(8,128)(2,1)S(1)}, bf16[128,128]{1,0:T(8,128)(2,1)S(1)}, u32[]{:S(2)}, u32[]{:S(2)}) %collective-permute-start.2) | collective-permute-done | bytes 32800 | tf_op jit(solution)/shard_map/ppermute | solution.py:262
  29.7 4.7 %all-to-all-start.1 = ((bf16[8,208,128]{2,1,0:T(8,128)(2,1)}), bf16[8,208,128]{2,1,0:T(8,128)(2,1)S(1)}, u32[]{:S(2)}, u32[]{:S(2)}) async-start(bf16[8,208,128]{2,1,0:T(8,128)(2,1)} %pack_keys.1), calls=%async_computation.1 | async-start | bytes 851968 | tf_op jit(solution)/shard_map/all_to_all | solution.py:273
  34.4 1.9 %collective-permute-start = (bf16[4,1040,128]{2,1,0:T(8,128)(2,1)S(1)}, bf16[4,1040,128]{2,1,0:T(8,128)(2,1)S(1)}, u32[]{:S(2)}, u32[]{:S(2)}) collective-permute-start(bf16[4,1040,128]{2,1,0:T(8,128)(2,1)S(1)} %all-to-all-done.same_ref), channel_id=1, source_target_pairs={{0,8},{8,0},{1,9},{9,1},{2,10},{10,2},{3,11},{11,3},{4,12},{12,4},... | collective-permute-start | bytes 3194888 | tf_op jit(solution)/shard_map/ppermute | solution.py:267
  36.3 9.0 %all-to-all-done.1 = bf16[8,208,128]{2,1,0:T(8,128)(2,1)S(1)} async-done(((bf16[8,208,128]{2,1,0:T(8,128)(2,1)}), bf16[8,208,128]{2,1,0:T(8,128)(2,1)S(1)}, u32[]{:S(2)}, u32[]{:S(2)}) %all-to-all-start.1) | async-done | bytes 426016 | tf_op jit(solution)/shard_map/all_to_all | solution.py:273
  45.4 1.8 %row_sums.1 = f32[8,2,4,4,128]{4,3,2,1,0:T(4,128)S(1)} custom-call(bf16[4,1040,128]{2,1,0:T(8,128)(2,1)S(1)} %all-to-all-done.same_ref, bf16[4,1040,128]{2,1,0:T(8,128)(2,1)S(1)} %collective-permute-done.other_ref, bf16[4,2,208,128]{3,2,1,0:T(8,128)(2,1)S(1)} %bitcast.3), custom_call_target="tpu_custom_call" | custom-call | tf_op jit(solution)/shard_map/row_sums/pallas_call | solution.py:50
  47.2 9.9 %all_to_all.25.norm_ref = f32[8,2,4,4,128]{4,3,2,1,0:T(4,128)S(1)} all-to-all(f32[8,2,4,4,128]{4,3,2,1,0:T(4,128)S(1)} %row_sums.1), channel_id=1, replica_groups=mesh['zg'=4,'zr'=4,'xh'=2,'core'=2,'tp'=4,'pair'=2] {'xh','core','pair'}, dimensions={0} | all-to-all | bytes 262144 | tf_op jit(solution)/shard_map/all_to_all | solution.py:280
  57.1 5.2 %gradients.1 = (bf16[4,128,512]{2,1,0:T(8,128)(2,1)S(1)}, bf16[4,128,512]{2,1,0:T(8,128)(2,1)S(1)}, bf16[8,3,64,128]{3,2,1,0:T(8,128)(2,1)}) custom-call(bf16[4,1040,128]{2,1,0:T(8,128)(2,1)S(1)} %all-to-all-done.same_ref, bf16[4,1040,128]{2,1,0:T(8,128)(2,1)S(1)} %collective-permute-done.other_ref, bf16[4,2,208,128]{3,2,1,0:T(8,128)(2,1)S(1)} %bitcast.4, ...), custom_call_target="tpu_custom_call" | custom-call | tf_op jit(solution)/shard_map/gradients/pallas_call | solution.py:50
  63.1 3.5 %all-to-all-start.3 = ((bf16[8,3,64,128]{3,2,1,0:T(8,128)(2,1)}), bf16[8,3,64,128]{3,2,1,0:T(8,128)(2,1)S(1)}, u32[]{:S(2)}, u32[]{:S(2)}) async-start(bf16[8,3,64,128]{3,2,1,0:T(8,128)(2,1)} %get-tuple-element.9), calls=%async_computation.3 | async-start | bytes 786432 | tf_op jit(solution)/shard_map/all_to_all | solution.py:300
  66.5 1.9 %collective-permute-start.3 = (bf16[4,128,512]{2,1,0:T(8,128)(2,1)}, bf16[4,128,512]{2,1,0:T(8,128)(2,1)S(1)}, u32[]{:S(2)}, u32[]{:S(2)}) collective-permute-start(bf16[4,128,512]{2,1,0:T(8,128)(2,1)} %copy-done.7), channel_id=1, source_target_pairs={{0,8},{8,0},{1,9},{9,1},{2,10},{10,2},{3,11},{11,3},{4,12},{12,4},... | collective-permute-start | bytes 1572872 | tf_op jit(solution)/shard_map/ppermute | solution.py:299
  68.5 2.1 %collective-permute-done.3.other_ref = bf16[4,128,512]{2,1,0:T(8,128)(2,1)S(1)} collective-permute-done((bf16[4,128,512]{2,1,0:T(8,128)(2,1)}, bf16[4,128,512]{2,1,0:T(8,128)(2,1)S(1)}, u32[]{:S(2)}, u32[]{:S(2)}) %collective-permute-start.3) | collective-permute-done | bytes 524320 | tf_op jit(solution)/shard_map/ppermute | solution.py:299
  70.5 7.5 %all-to-all-done.3.dkv_ref = bf16[8,3,64,128]{3,2,1,0:T(8,128)(2,1)S(1)} async-done(((bf16[8,3,64,128]{3,2,1,0:T(8,128)(2,1)}), bf16[8,3,64,128]{3,2,1,0:T(8,128)(2,1)S(1)}, u32[]{:S(2)}, u32[]{:S(2)}) %all-to-all-start.3) | async-done | bytes 393248 | tf_op jit(solution)/shard_map/all_to_all | solution.py:300
  78.0 0.9 add_parts.1
  79.0 3.5 %all-to-all-start.4 = ((bf16[4,128,512]{2,1,0:T(8,128)(2,1)}), bf16[4,128,512]{2,1,0:T(8,128)(2,1)S(1)}, u32[]{:S(2)}, u32[]{:S(2)}) async-start(bf16[4,128,512]{2,1,0:T(8,128)(2,1)} %get-tuple-element.12), calls=%async_computation.4 | async-start | bytes 1048576 | tf_op jit(solution)/shard_map/all_to_all | solution.py:315
  82.4 1.3 %collective-permute-start.4 = (bf16[128,128]{1,0:T(8,128)(2,1)S(1)}, bf16[128,128]{1,0:T(8,128)(2,1)S(1)}, u32[]{:S(2)}, u32[]{:S(2)}) collective-permute-start(bf16[128,128]{1,0:T(8,128)(2,1)S(1)} %get-tuple-element.14), channel_id=1, source_target_pairs={{128,0},{256,128},{129,1},{257,129},{130,2},{258,130},{131,3},{259... | collective-permute-start | bytes 98312 | tf_op jit(solution)/shard_map/ppermute | solution.py:313
  83.7 1.3 %collective-permute-start.5 = (bf16[128,128]{1,0:T(8,128)(2,1)S(1)}, bf16[128,128]{1,0:T(8,128)(2,1)S(1)}, u32[]{:S(2)}, u32[]{:S(2)}) collective-permute-start(bf16[128,128]{1,0:T(8,128)(2,1)S(1)} %get-tuple-element.15), channel_id=1, source_target_pairs={{256,0},{257,1},{258,2},{259,3},{260,4},{261,5},{262,6},{263,7},{2... | collective-permute-start | bytes 98312 | tf_op jit(solution)/shard_map/ppermute | solution.py:314
  85.0 9.4 %collective-permute-done.4.one_ref = bf16[128,128]{1,0:T(8,128)(2,1)S(1)} collective-permute-done((bf16[128,128]{1,0:T(8,128)(2,1)S(1)}, bf16[128,128]{1,0:T(8,128)(2,1)S(1)}, u32[]{:S(2)}, u32[]{:S(2)}) %collective-permute-start.4) | collective-permute-done | bytes 32800 | tf_op jit(solution)/shard_map/ppermute | solution.py:313
  94.4 12.0 %collective-permute-done.5.two_ref = bf16[128,128]{1,0:T(8,128)(2,1)S(1)} collective-permute-done((bf16[128,128]{1,0:T(8,128)(2,1)S(1)}, bf16[128,128]{1,0:T(8,128)(2,1)S(1)}, u32[]{:S(2)}, u32[]{:S(2)}) %collective-permute-start.5) | collective-permute-done | bytes 32800 | tf_op jit(solution)/shard_map/ppermute | solution.py:314
  (19 shorter events, 3.8 us)
Async XLA Ops:
  0.6 0.9 copy-start
  1.5 0.9 copy-start.1
  2.4 0.9 copy-start.2
  3.3 0.7 copy-start.4
  4.0 0.7 copy-start.6
  5.9 4.4 %copy-start.3 = (bf16[128,128]{1,0:T(8,128)(2,1)S(1)}, bf16[128,128]{1,0:T(8,128)(2,1)}, u32[]{:S(2)}) copy-start(bf16[128,128]{1,0:T(8,128)(2,1)} %own_ref.1) | copy-start | bytes 98308
  5.9 23.0 %copy-start.5 = (s32[128]{0:T(128)S(1)}, s32[128]{0:T(128)}, u32[]{:S(2)}) copy-start(s32[128]{0:T(128)} %param.10) | copy-start | bytes 1540
  5.9 23.9 %all-to-all-start = ((bf16[4,1040,128]{2,1,0:T(8,128)(2,1)}), bf16[4,1040,128]{2,1,0:T(8,128)(2,1)S(1)}, u32[]{:S(2)}, u32[]{:S(2)}) async-start(bf16[4,1040,128]{2,1,0:T(8,128)(2,1)} %pack_queries.1), calls=%async_computation | async-start | bytes 2129920 | tf_op jit(solution)/shard_map/all_to_all | solution.py:266
  10.3 17.0 %collective-permute-start.1 = (bf16[128,128]{1,0:T(8,128)(2,1)S(1)}, bf16[128,128]{1,0:T(8,128)(2,1)S(1)}, u32[]{:S(2)}, u32[]{:S(2)}) collective-permute-start(bf16[128,128]{1,0:T(8,128)(2,1)S(1)} %copy-done.3), channel_id=1, source_target_pairs={{0,128},{128,256},{1,129},{129,257},{2,130},{130,258},{3,131},{131... | collective-permute-start | bytes 98312 | tf_op jit(solution)/shard_map/ppermute | solution.py:261
  19.4 9.5 %collective-permute-start.2 = (bf16[128,128]{1,0:T(8,128)(2,1)S(1)}, bf16[128,128]{1,0:T(8,128)(2,1)S(1)}, u32[]{:S(2)}, u32[]{:S(2)}) collective-permute-start(bf16[128,128]{1,0:T(8,128)(2,1)S(1)} %copy-done.3), channel_id=1, source_target_pairs={{0,256},{1,257},{2,258},{3,259},{4,260},{5,261},{6,262},{7,263},{8... | collective-permute-start | bytes 98312 | tf_op jit(solution)/shard_map/ppermute | solution.py:262
  29.7 15.6 %all-to-all-start.1 = ((bf16[8,208,128]{2,1,0:T(8,128)(2,1)}), bf16[8,208,128]{2,1,0:T(8,128)(2,1)S(1)}, u32[]{:S(2)}, u32[]{:S(2)}) async-start(bf16[8,208,128]{2,1,0:T(8,128)(2,1)} %pack_keys.1), calls=%async_computation.1 | async-start | bytes 851968 | tf_op jit(solution)/shard_map/all_to_all | solution.py:273
  34.4 11.0 %collective-permute-start = (bf16[4,1040,128]{2,1,0:T(8,128)(2,1)S(1)}, bf16[4,1040,128]{2,1,0:T(8,128)(2,1)S(1)}, u32[]{:S(2)}, u32[]{:S(2)}) collective-permute-start(bf16[4,1040,128]{2,1,0:T(8,128)(2,1)S(1)} %all-to-all-done.same_ref), channel_id=1, source_target_pairs={{0,8},{8,0},{1,9},{9,1},{2,10},{10,2},{3,11},{11,3},{4,12},{12,4},... | collective-permute-start | bytes 3194888 | tf_op jit(solution)/shard_map/ppermute | solution.py:267
  62.3 0.8 copy-start.7
  63.1 15.0 %all-to-all-start.3 = ((bf16[8,3,64,128]{3,2,1,0:T(8,128)(2,1)}), bf16[8,3,64,128]{3,2,1,0:T(8,128)(2,1)S(1)}, u32[]{:S(2)}, u32[]{:S(2)}) async-start(bf16[8,3,64,128]{3,2,1,0:T(8,128)(2,1)} %get-tuple-element.9), calls=%async_computation.3 | async-start | bytes 786432 | tf_op jit(solution)/shard_map/all_to_all | solution.py:300
  66.5 4.0 %collective-permute-start.3 = (bf16[4,128,512]{2,1,0:T(8,128)(2,1)}, bf16[4,128,512]{2,1,0:T(8,128)(2,1)S(1)}, u32[]{:S(2)}, u32[]{:S(2)}) collective-permute-start(bf16[4,128,512]{2,1,0:T(8,128)(2,1)} %copy-done.7), channel_id=1, source_target_pairs={{0,8},{8,0},{1,9},{9,1},{2,10},{10,2},{3,11},{11,3},{4,12},{12,4},... | collective-permute-start | bytes 1572872 | tf_op jit(solution)/shard_map/ppermute | solution.py:299
  79.0 27.4 %all-to-all-start.4 = ((bf16[4,128,512]{2,1,0:T(8,128)(2,1)}), bf16[4,128,512]{2,1,0:T(8,128)(2,1)S(1)}, u32[]{:S(2)}, u32[]{:S(2)}) async-start(bf16[4,128,512]{2,1,0:T(8,128)(2,1)} %get-tuple-element.12), calls=%async_computation.4 | async-start | bytes 1048576 | tf_op jit(solution)/shard_map/all_to_all | solution.py:315
  82.4 12.0 %collective-permute-start.4 = (bf16[128,128]{1,0:T(8,128)(2,1)S(1)}, bf16[128,128]{1,0:T(8,128)(2,1)S(1)}, u32[]{:S(2)}, u32[]{:S(2)}) collective-permute-start(bf16[128,128]{1,0:T(8,128)(2,1)S(1)} %get-tuple-element.14), channel_id=1, source_target_pairs={{128,0},{256,128},{129,1},{257,129},{130,2},{258,130},{131,3},{259... | collective-permute-start | bytes 98312 | tf_op jit(solution)/shard_map/ppermute | solution.py:313
  83.7 22.6 %collective-permute-start.5 = (bf16[128,128]{1,0:T(8,128)(2,1)S(1)}, bf16[128,128]{1,0:T(8,128)(2,1)S(1)}, u32[]{:S(2)}, u32[]{:S(2)}) collective-permute-start(bf16[128,128]{1,0:T(8,128)(2,1)S(1)} %get-tuple-element.15), channel_id=1, source_target_pairs={{256,0},{257,1},{258,2},{259,3},{260,4},{261,5},{262,6},{263,7},{2... | collective-permute-start | bytes 98312 | tf_op jit(solution)/shard_map/ppermute | solution.py:314

commit v3 on v2

v3 whole, which is shorter than its diff:
```python
import functools
import math

import jax
import jax.numpy as jnp
from jax import lax
from jax.experimental import pallas as pl
from jax.experimental.pallas import tpu as pltpu
from jax.sharding import Mesh, PartitionSpec as P

BF = jnp.bfloat16
F32 = jnp.float32
NEGATIVE = -1e30
TOK = 128
HEAD = 128
HEADS = 4
COLS = HEADS * TOK
GROUP = 4
SLOTS = 3
HALF = TOK // 2
KEYS = GROUP * HALF
Q_ROWS = 2 * COLS + 16
KV_ROWS = SLOTS * HALF + 16
FULL = (2, 4, SLOTS, KEYS, COLS)
SCALE = 1.0 / math.sqrt(HEAD)
SCALE2 = SCALE * math.log2(math.e)
LOG_SCALE = math.log2(SCALE)
X_AXES = ("xh", "pair")
Z_AXES = ("zg", "zr")
MIRROR = [(r, 11 - r) for r in range(4)]
PLANE = ("xh", "core", "pair")
NT = (((1,), (1,)), ((), ()))
NN = (((1,), (0,)), ((), ()))
VMEM_LIMIT = 40 * 1024 * 1024


def dot(a, b, dims):
    return lax.dot_general(a, b, dims, preferred_element_type=F32)


def call(kernel, name, out_shape, scratch=(), near=(), far=(), far_out=()):
    def bound(*args):
        specs = [
            pl.BlockSpec(memory_space=pltpu.HBM if i in far else pltpu.VMEM)
            for i in range(len(args))
        ]
        outs = out_shape if isinstance(out_shape, tuple) else (out_shape,)
        out_specs = tuple(
            pl.BlockSpec(memory_space=pltpu.HBM if i in far_out else pltpu.VMEM)
            for i in range(len(outs))
        )
        kept = [
            pltpu.with_memory_space_constraint(a, pltpu.VMEM if i in near else pltpu.HBM)
            for i, a in enumerate(args)
        ]
        run = pl.pallas_call(
            kernel,
            out_shape=outs,
            in_specs=specs,
            out_specs=out_specs,
            scratch_shapes=scratch,
            name=name,
            compiler_params=pltpu.CompilerParams(vmem_limit_bytes=VMEM_LIMIT),
        )
        got = run(*kept)
        return got if isinstance(out_shape, tuple) else got[0]

    return bound


def shape(dims, dtype):
    return jax.ShapeDtypeStruct(dims, dtype)


def pack_queries(
    q_hbm, g_hbm, o_hbm, seg_hbm, mask_hbm, out_ref, q_ref, g_ref, o_ref, seg_ref, mask_ref, sems
):
    copies = [
        pltpu.make_async_copy(far, ref, sems.at[i])
        for i, (far, ref) in enumerate(
            (
                (mask_hbm, mask_ref),
                (g_hbm, g_ref),
                (o_hbm, o_ref),
                (q_hbm, q_ref),
                (seg_hbm, seg_ref),
            )
        )
    ]
    for copy in copies:
        copy.start()
    for copy in copies:
        copy.wait()
    mask = jnp.broadcast_to(mask_ref[...].astype(F32), (TOK, TOK)).T
    rows = []
    for h in range(HEADS):
        lanes = slice(h * HEAD, (h + 1) * HEAD)
        cot = g_ref[:, lanes].astype(F32) * mask
        rows.append(jnp.sum((cot * o_ref[:, lanes].astype(F32)).T, axis=0, keepdims=True))
        cot = cot.astype(BF)
        for x in range(4):
            out_ref[x, h * TOK : (h + 1) * TOK, :] = q_ref[:, lanes]
            out_ref[x, COLS + h * TOK : COLS + (h + 1) * TOK, :] = cot
    delta = jnp.concatenate(rows, axis=0)
    high = delta.astype(BF).astype(F32)
    low = delta - high
    tail = jnp.concatenate(
        [high, low, seg_ref[...].astype(F32), jnp.zeros((7, TOK), F32)], axis=0
    ).astype(BF)
    for x in range(4):
        out_ref[x, 2 * COLS :, :] = tail


def pack_keys(own_ref, one_ref, two_ref, seg_ref, out_ref):
    tail = jnp.concatenate(
        [seg_ref[...].astype(F32), jnp.zeros((15, TOK), F32)], axis=0
    ).astype(BF)
    for s, ref in enumerate((own_ref, one_ref, two_ref)):
        for half in range(2):
            part = ref[half * HALF : (half + 1) * HALF, :]
            for r in range(GROUP):
                out_ref[2 * r + half, s * HALF : (s + 1) * HALF, :] = part
    for i in range(2 * GROUP):
        out_ref[i, SLOTS * HALF :, :] = tail


def position():
    return (
        lax.axis_index("zg"),
        lax.axis_index("zr"),
        lax.axis_index("xh"),
        lax.axis_index("core"),
        lax.axis_index("pair"),
    )


def slot_count(zg):
    return jnp.where(zg == 3, 1, zg + 1)


def key_block(kv_ref, kind, s):
    first = s * HALF if isinstance(s, int) else pl.multiple_of(s * HALF, HALF)
    return kv_ref[:, kind, pl.ds(first, HALF), :].reshape(KEYS, HEAD)


def key_segments(kv_ref, pair, turn_ref, seg_ref):
    for r in range(GROUP):
        row = kv_ref[r, 0, SLOTS * HALF :, :].astype(F32)[0:1]
        turn_ref[...] = jnp.broadcast_to(row, (TOK, TOK)).T
        seg_ref[r * HALF : (r + 1) * HALF, :] = turn_ref[
            pl.ds(pl.multiple_of(pair * HALF, HALF), HALF), :
        ]


def allowed_pairs(place, query_seg, hx, from_core, seg_ref):
    zg, zr, xh, core, pair = place
    row = lax.broadcasted_iota(jnp.int32, (KEYS, TOK), 0)
    key_pos = (row // HALF) * 512 + row % HALF + ((2 * xh + core) * TOK + pair * HALF)
    lane = lax.broadcasted_iota(jnp.int32, (KEYS, TOK), 1)
    query_pos = lane + (zr * 512 + (2 * hx + from_core) * TOK)
    return (key_pos <= query_pos) & (seg_ref[...] == query_seg)


def tiled(mask):
    return jnp.concatenate([mask] * HEADS, axis=1)


def by_count(place, body):
    count = slot_count(place[0])
    for n in (1, 2, 3):

        @pl.when(count == n)
        def _(n=n):
            body(n)


def flat(rows):
    return jnp.concatenate([rows[h : h + 1] for h in range(HEADS)], axis=1)


def blocks(from_ref, to_ref, n, other, x, sems):
    return pltpu.make_async_copy(
        from_ref.at[other, x, pl.ds(0, n)], to_ref.at[other, x, pl.ds(0, n)], sems.at[other, x]
    )


def row_sums(
    same_ref, other_ref, kv_ref, out_ref, top_ref, prob_hbm, turn_ref, seg_ref, prob_ref, sems
):
    place = position()
    core, pair = place[3:]
    key_segments(kv_ref, pair, turn_ref, seg_ref)

    def body(n):
        def sources(hx, _):
            for other, q_ref in enumerate((same_ref, other_ref)):
                from_core = (1 - core) if other else core
                segs = q_ref[2 * hx, 2 * COLS :, :].astype(F32)[8:9]
                allowed = tiled(allowed_pairs(place, segs, hx, from_core, seg_ref))
                for p in range(2):
                    x = 2 * hx + p
                    q = q_ref[x, :COLS, :]
                    scores = [dot(key_block(kv_ref, 0, j), q, NT) * SCALE2 for j in range(n)]
                    scores[0] = jnp.where(allowed, scores[0], NEGATIVE)
                    top = jnp.full((1, COLS), 0.1 * NEGATIVE, F32)
                    for s in scores:
                        top = jnp.maximum(top, jnp.max(s, axis=0, keepdims=True))
                    total = jnp.zeros((1, COLS), F32)
                    for j, s in enumerate(scores):
                        prob = jnp.exp2(s - top)
                        total += jnp.sum(prob, axis=0, keepdims=True)
                        prob_ref[other, x, j] = prob.astype(BF)
                    norm = jnp.maximum(top + jnp.log2(total), NEGATIVE)
                    for h in range(HEADS):
                        lanes = slice(h * TOK, (h + 1) * TOK)
                        top_ref[other, x, h : h + 1, :] = top[:, lanes]
                        piece = jnp.broadcast_to(norm[:, lanes], (8, TOK))
                        out_ref[:, from_core, x, h : h + 1, :] = piece.reshape(8, 1, TOK)
                    blocks(prob_ref, prob_hbm, n, other, x, sems).start()
            return 0

        lax.fori_loop(0, 2, sources, 0)
        for other in range(2):
            for x in range(4):
                blocks(prob_ref, prob_hbm, n, other, x, sems).wait()

    by_count(place, body)


def raw_scores(
    same_ref, other_ref, kv_ref, prob_hbm, score_hbm, prob_ref, score_ref, in_sems, out_sems
):
    def body(n):
        for x in range(4):
            for other in range(2):
                blocks(prob_hbm, prob_ref, n, other, x, in_sems).start()

        def sources(x, _):
            for other, g_ref in enumerate((same_ref, other_ref)):
                cot = g_ref[x, COLS : 2 * COLS, :]
                tail = g_ref[x, 2 * COLS :, :].astype(F32)
                delta = flat(tail[0:HEADS] + tail[HEADS : 2 * HEADS])
                blocks(prob_hbm, prob_ref, n, other, x, in_sems).wait()
                for j in range(n):
                    dprob = dot(key_block(kv_ref, 1, j), cot, NT)
                    score_ref[other, x, j] = (
                        prob_ref[other, x, j].astype(F32) * (dprob - delta)
                    ).astype(BF)
                blocks(score_ref, score_hbm, n, other, x, out_sems).start()
            return 0

        lax.fori_loop(0, 4, sources, 0)
        for x in range(4):
            for other in range(2):
                blocks(score_ref, score_hbm, n, other, x, out_sems).wait()

    by_count(position(), body)


def over_sources(left_ref, right_ref, j):
    total = None
    for other in range(2):
        for x in range(4):
            part = dot(left_ref[other, x, j], right_ref[other, x], NN)
            total = part if total is None else total + part
    return total


def key_gradients(
    same_ref, other_ref, norm_ref, top_ref, prob_hbm, score_hbm,
    dkv_ref, weight_ref, q_ref, g_ref, prob_ref, score_ref, sems,
):
    place = position()
    core = place[3]
    count = slot_count(place[0])

    def fetch(j, kind):
        far, near = ((score_hbm, score_ref), (prob_hbm, prob_ref))[kind]
        return pltpu.make_async_copy(far.at[:, :, j], near.at[:, :, j], sems.at[j, kind])

    for j in range(SLOTS):

        @pl.when(j < count)
        def _(j=j):
            fetch(j, 0).start()
            fetch(j, 1).start()

    norms = norm_ref[...]
    top = jnp.max(norms, axis=0)
    log_norm = top + jnp.log2(jnp.sum(jnp.exp2(norms - top[None]), axis=0))
    own = jnp.where(core == 0, log_norm[0], log_norm[1])
    far = jnp.where(core == 0, log_norm[1], log_norm[0])
    weight_ref[0] = jnp.exp2(top_ref[0] - own)
    weight_ref[1] = jnp.exp2(top_ref[1] - far)

    def scaled(x, _):
        for other, source_ref in enumerate((same_ref, other_ref)):
            weights = weight_ref[other, x]
            for h in range(HEADS):
                rows = slice(h * TOK, (h + 1) * TOK)
                below = slice(COLS + h * TOK, COLS + (h + 1) * TOK)
                by_row = jnp.broadcast_to(weights[h : h + 1], (TOK, TOK)).T
                q = source_ref[x, rows, :].astype(F32) * (by_row * SCALE)
                q_ref[other, x, rows, :] = q.astype(BF)
                g_ref[other, x, rows, :] = (
                    source_ref[x, below, :].astype(F32) * by_row
                ).astype(BF)
        return 0

    lax.fori_loop(0, 4, scaled, 0)

    def body(n):
        for s in range(SLOTS):
            for kind, left_ref, right_ref in ((0, score_ref, q_ref), (1, prob_ref, g_ref)):
                if s < n:
                    fetch(s, kind).wait()
                    total = over_sources(left_ref, right_ref, s).astype(BF)
                else:
                    total = jnp.zeros((KEYS, HEAD), BF)
                for r in range(GROUP):
                    dkv_ref[2 * r + kind, s * HALF : (s + 1) * HALF, :] = total[
                        r * HALF : (r + 1) * HALF
                    ]

    by_count(place, body)


def query_gradients(
    kv_ref, score_hbm, weight_ref, same_ref, other_ref, turned_ref, score_ref, sems
):

    def body(n):
        for x in range(4):
            for other in (1, 0):
                blocks(score_hbm, score_ref, n, other, x, sems).start()
        for s in range(n):
            turned_ref[s] = key_block(kv_ref, 0, s).astype(F32).T.astype(BF)

        def sources(x, _):
            for other, dq_ref in ((1, other_ref), (0, same_ref)):
                blocks(score_hbm, score_ref, n, other, x, sems).wait()
                dq = dot(turned_ref[0], score_ref[other, x, 0], NN)
                for j in range(1, n):
                    dq += dot(turned_ref[j], score_ref[other, x, j], NN)
                dq_ref[x] = (dq * (flat(weight_ref[other, x]) * SCALE)).astype(BF)
            return 0

        lax.fori_loop(0, 4, sources, 0)

    by_count(position(), body)


def sum_keys(dkv_ref, own_ref, one_ref, two_ref):
    for s, ref in enumerate((own_ref, one_ref, two_ref)):
        for half in range(2):
            total = dkv_ref[half, s * HALF : (s + 1) * HALF, :].astype(F32)
            for r in range(1, GROUP):
                total += dkv_ref[2 * r + half, s * HALF : (s + 1) * HALF, :].astype(F32)
            ref[half * HALF : (half + 1) * HALF, :] = total.astype(ref.dtype)


def sum_cores(same_ref, other_ref, out_ref):
    out_ref[...] = (same_ref[...].astype(F32) + other_ref[...].astype(F32)).astype(BF)


def finish(dq_ref, own_ref, one_ref, two_ref, out_q_ref, out_kv_ref):
    total = dq_ref[0].astype(F32)
    for x in range(1, 4):
        total += dq_ref[x].astype(F32)
    for h in range(HEADS):
        lanes = slice(h * HEAD, (h + 1) * HEAD)
        out_q_ref[:, lanes] = total[:, lanes].T.astype(BF)
    out_kv_ref[...] = (
        own_ref[...] + one_ref[...].astype(F32) + two_ref[...].astype(F32)
    ).astype(BF)


def local_kernels(same, other, kv, exchange):
    norms, tops, prob = call(
        row_sums,
        "row_sums",
        (
            shape((8, 2, 4, HEADS, TOK), F32),
            pltpu.VMEM((2, 4, HEADS, TOK), F32),
            pltpu.HBM(FULL, BF),
        ),
        [
            pltpu.VMEM((TOK, TOK), F32),
            pltpu.VMEM((KEYS, TOK), F32),
            pltpu.VMEM(FULL, BF),
            pltpu.SemaphoreType.DMA((2, 4)),
        ],
        near=range(3),
        far_out=(2,),
    )(same, other, kv)
    norms = exchange(norms)
    scores = call(
        raw_scores,
        "raw_scores",
        pltpu.HBM(FULL, BF),
        [
            pltpu.VMEM(FULL, BF),
            pltpu.VMEM(FULL, BF),
            pltpu.SemaphoreType.DMA((2, 4)),
            pltpu.SemaphoreType.DMA((2, 4)),
        ],
        near=range(3),
        far=(3,),
        far_out=(0,),
    )(same, other, kv, prob)
    dkv, weights = call(
        key_gradients,
        "key_gradients",
        (
            shape((2 * GROUP, SLOTS * HALF, HEAD), BF),
            pltpu.VMEM((2, 4, HEADS, TOK), F32),
        ),
        [
            pltpu.VMEM((2, 4, COLS, HEAD), BF),
            pltpu.VMEM((2, 4, COLS, HEAD), BF),
            pltpu.VMEM(FULL, BF),
            pltpu.VMEM(FULL, BF),
            pltpu.SemaphoreType.DMA((SLOTS, 2)),
        ],
        near=range(4),
        far=(4, 5),
    )(same, other, norms, tops, prob, scores)
    dq_same, dq_other = call(
        query_gradients,
        "query_gradients",
        (pltpu.VMEM((4, HEAD, COLS), BF), shape((4, HEAD, COLS), BF)),
        [
            pltpu.VMEM((SLOTS, HEAD, KEYS), BF),
            pltpu.VMEM(FULL, BF),
            pltpu.SemaphoreType.DMA((2, 4)),
        ],
        near=(0, 2),
        far=(1,),
    )(kv, scores, weights)
    return dkv, dq_same, dq_other


def per_device(queries, stored_key_value, out_grad, attn_out, segment_ids, loss_mask):
    seg = segment_ids.reshape(1, TOK)
    mask = loss_mask.reshape(1, TOK)
    swap = [(0, 1), (1, 0)]

    two = lax.ppermute(stored_key_value, Z_AXES, MIRROR)
    one = lax.ppermute(stored_key_value, "zg", [(0, 1), (1, 2)])
    wide = pltpu.VMEM((TOK, HEADS * HEAD), BF)
    line = pltpu.VMEM((1, TOK), jnp.int32)
    packed = call(
        pack_queries,
        "pack_queries",
        shape((4, Q_ROWS, HEAD), BF),
        [wide, wide, wide, line, line, pltpu.SemaphoreType.DMA((5,))],
        far=range(5),
    )(queries, out_grad, attn_out, seg, mask)
    same = lax.all_to_all(packed, X_AXES, 0, 0, tiled=True)
    other = lax.ppermute(same, "core", swap)
    kv = call(pack_keys, "pack_keys", shape((2 * GROUP, KV_ROWS, HEAD), BF), near=(1, 2))(
        stored_key_value, one, two, seg
    )
    kv = lax.all_to_all(kv, ("zr", "pair"), 0, 0, tiled=True).reshape(GROUP, 2, KV_ROWS, HEAD)

    dkv, dq_same, dq_other = local_kernels(
        same, other, kv, lambda norms: lax.all_to_all(norms, PLANE, 0, 0, tiled=True)
    )
    dkv = lax.all_to_all(dkv, ("zr", "pair"), 0, 0, tiled=True)
    dq_other = lax.ppermute(dq_other, "core", swap)
    own, one, two = call(
        sum_keys,
        "sum_keys",
        (pltpu.VMEM((TOK, HEAD), F32), shape((TOK, HEAD), BF), shape((TOK, HEAD), BF)),
        near=(0,),
    )(dkv)
    one = lax.ppermute(one, "zg", [(1, 0), (2, 1)])
    two = lax.ppermute(two, Z_AXES, [(b, a) for a, b in MIRROR])
    dq = call(sum_cores, "sum_cores", shape((4, HEAD, COLS), BF), near=(0, 1))(dq_same, dq_other)
    dq = lax.all_to_all(dq, X_AXES, 0, 0, tiled=True)
    return call(
        finish,
        "finish",
        (shape((TOK, HEADS * HEAD), BF), shape((TOK, HEAD), BF)),
        near=range(4),
    )(dq, own, one, two)


def solution(mesh):
    fine = Mesh(
        mesh.devices.reshape(4, 4, 2, 2, 4, 2), ("zg", "zr", "xh", "core", "tp", "pair")
    )
    rows = ("zg", "zr", "xh", "core")
    wide = P(rows, ("tp", "pair"))
    return jax.shard_map(
        per_device,
        mesh=fine,
        in_specs=(wide, wide, wide, wide, P(rows), P(rows)),
        out_specs=(wide, wide),
        check_vma=False,
    )
```

time: 108 us -> 100 us (0.926)
  blocking collectives: 9.89 us -> 0 us
  Pallas kernels: 10.8 us -> 19.2 us
  waiting for transfers between devices: 41.5 us -> 36.6 us
  local copies, waits for them, and re-layouts: 4.82 us -> 0.01 us
  starting transfers between devices: 39.4 us -> 42.2 us
    all_to_all x1 -> x0, blocking collectives: 9.89 us -> none  [per_device(): norms = lax.all_to_all(norms, PLANE, 0, 0, tiled=True)]
    pallas_call x6 -> x9, Pallas kernels: 10.8 us -> 19.2 us  [bound(): got = run(*kept)]
    all_to_all x1, waiting for transfers between devices: 0.01 us -> 5.59 us  [per_device(): dq = lax.all_to_all(dq, X_AXES, 0, 0, tiled=True)]
    ppermute x1, waiting for transfers between devices: 9.35 us -> 4.11 us  [per_device(): one = lax.ppermute(one, 'zg', [(1, 0), (2, 1)])]
    unnamed x16 -> x2, local copies, waits for them, and re-layouts: 4.82 us -> 0.01 us
    ppermute x2, waiting for transfers between devices: 13.5 us -> 9.28 us  [the longest x1 7.56 us: per_device(): two = lax.ppermute(two, Z_AXES, [(b, a) for a, b in MIRROR])]
    all_to_all x1 -> x2, starting transfers between devices: 4.66 us -> 8.91 us  [the longest x1 4.94 us: per_device(): lax.all_to_all(kv, ('zr', 'pair'), 0, 0, tiled=True)]
    all_to_all x1, waiting for transfers between devices: 7.51 us -> 4.26 us  [per_device(): dkv = lax.all_to_all(dkv, ('zr', 'pair'), 0, 0, tiled=True)]
  transfers between devices with their start and end apart: 10 -> 11, of which waited for: 6 -> 8; matrix products, arithmetic and copies ran while one was open for 0% -> 0% of each run, Pallas kernels for 1% -> 9%
where the time goes in v3:
time: 100 us; the launch traced here: 98.8 us
  starting transfers between devices  42.2 us (42%)
  waiting for transfers between devices  36.6 us (37%)
  Pallas kernels  19.2 us (19%)
    pallas_call x9, Pallas kernels, bound(): got = run(*kept)  19.2 us
    ppermute x1, starting transfers between devices, per_device(): one = lax.ppermute(stored_key_value, 'zg', [(0, 1), (1, 2)])  9.08 us
    all_to_all x1, waiting for transfers between devices, per_device(): lax.all_to_all(kv, ('zr', 'pair'), 0, 0, tiled=True)  9.05 us
    ppermute x1, waiting for transfers between devices, per_device(): two = lax.ppermute(two, Z_AXES, [(b, a) for a, b in MIRROR])  7.56 us
    ppermute x1, starting transfers between devices, per_device(): two = lax.ppermute(stored_key_value, Z_AXES, MIRROR)  6.58 us
    all_to_all x1, waiting for transfers between devices, per_device(): dq = lax.all_to_all(dq, X_AXES, 0, 0, tiled=True)  5.59 us
    all_to_all x1, starting transfers between devices, per_device(): lax.all_to_all(kv, ('zr', 'pair'), 0, 0, tiled=True)  4.94 us
    all_to_all x1, starting transfers between devices, per_device(): same = lax.all_to_all(packed, X_AXES, 0, 0, tiled=True)  4.3 us
  transfers between devices with their start and end apart: 11, of which 8 were waited for; matrix products, arithmetic and copies ran while one was open for 0% of the time, Pallas kernels for 9%

profile of v3, /device:TPU:24, one launch (start us, length us, event | category | flops | bytes accessed | tf_op | source)
XLA Modules:
  0.0 98.8 jit_solution(18079983754210566648)
XLA Ops:
  0.6 2.3 %pack_queries.1 = bf16[4,1040,128]{2,1,0:T(8,128)(2,1)} custom-call(bf16[128,512]{1,0:T(8,128)(2,1)} %q_hbm.1, bf16[128,512]{1,0:T(8,128)(2,1)} %g_hbm.1, bf16[128,512]{1,0:T(8,128)(2,1)} %o_hbm.1, s32[1,128]{1,0:T(1,128)} %bitcast.6, s32[1,128]{1,0:T(1,128)} %bitcast.8), custom_call_target="tpu_custom_call" | custom-call | tf_op jit(solution)/shard_map/pack_queries/pallas_call | solution.py:65
  3.0 4.3 %all-to-all-start.1 = ((bf16[4,1040,128]{2,1,0:T(8,128)(2,1)}), bf16[4,1040,128]{2,1,0:T(8,128)(2,1)S(1)}, u32[]{:S(2)}, u32[]{:S(2)}) async-start(bf16[4,1040,128]{2,1,0:T(8,128)(2,1)} %pack_queries.1), calls=%async_computation.1 | async-start | bytes 2129920 | tf_op jit(solution)/shard_map/all_to_all | solution.py:459
  7.3 9.1 %collective-permute-start = (bf16[128,128]{1,0:T(8,128)(2,1)S(1)}, bf16[128,128]{1,0:T(8,128)(2,1)S(1)}, u32[]{:S(2)}, u32[]{:S(2)}) collective-permute-start(bf16[128,128]{1,0:T(8,128)(2,1)S(1)} %copy-done), channel_id=1, source_target_pairs={{0,128},{128,256},{1,129},{129,257},{2,130},{130,258},{3,131},{131... | collective-permute-start | bytes 98312 | tf_op jit(solution)/shard_map/ppermute | solution.py:449
  16.4 6.6 %collective-permute-start.1 = (bf16[128,128]{1,0:T(8,128)(2,1)S(1)}, bf16[128,128]{1,0:T(8,128)(2,1)S(1)}, u32[]{:S(2)}, u32[]{:S(2)}) collective-permute-start(bf16[128,128]{1,0:T(8,128)(2,1)S(1)} %copy-done), channel_id=1, source_target_pairs={{0,352},{32,320},{64,288},{96,256},{1,353},{33,321},{65,289},{97,2... | collective-permute-start | bytes 98312 | tf_op jit(solution)/shard_map/ppermute | solution.py:448
  23.0 1.7 %collective-permute-done.1.two_ref = bf16[128,128]{1,0:T(8,128)(2,1)S(1)} collective-permute-done((bf16[128,128]{1,0:T(8,128)(2,1)S(1)}, bf16[128,128]{1,0:T(8,128)(2,1)S(1)}, u32[]{:S(2)}, u32[]{:S(2)}) %collective-permute-start.1) | collective-permute-done | bytes 32800 | tf_op jit(solution)/shard_map/ppermute | solution.py:448
  24.7 1.6 %pack_keys.1 = bf16[8,208,128]{2,1,0:T(8,128)(2,1)} custom-call(bf16[128,128]{1,0:T(8,128)(2,1)} %own_ref.1, bf16[128,128]{1,0:T(8,128)(2,1)S(1)} %collective-permute-done.one_ref, bf16[128,128]{1,0:T(8,128)(2,1)S(1)} %collective-permute-done.1.two_ref, s32[1,128]{1,0:T(1,128)} %bitcast.7), custom_call_target="tpu_custom_call" | custom-call | tf_op jit(solution)/shard_map/pack_keys/pallas_call | solution.py:65
  26.3 4.9 %all-to-all-start = ((bf16[8,208,128]{2,1,0:T(8,128)(2,1)}), bf16[8,208,128]{2,1,0:T(8,128)(2,1)S(1)}, u32[]{:S(2)}, u32[]{:S(2)}) async-start(bf16[8,208,128]{2,1,0:T(8,128)(2,1)} %pack_keys.1), calls=%async_computation | async-start | bytes 851968 | tf_op jit(solution)/shard_map/all_to_all | solution.py:464
  31.2 1.9 %collective-permute-start.2 = (bf16[4,1040,128]{2,1,0:T(8,128)(2,1)S(1)}, bf16[4,1040,128]{2,1,0:T(8,128)(2,1)S(1)}, u32[]{:S(2)}, u32[]{:S(2)}) collective-permute-start(bf16[4,1040,128]{2,1,0:T(8,128)(2,1)S(1)} %all-to-all-done.1.same_ref), channel_id=1, source_target_pairs={{0,8},{8,0},{1,9},{9,1},{2,10},{10,2},{3,11},{11,3},{4,12},{12,4},... | collective-permute-start | bytes 3194888 | tf_op jit(solution)/shard_map/ppermute | solution.py:460
  33.1 9.0 %all-to-all-done = bf16[8,208,128]{2,1,0:T(8,128)(2,1)S(1)} async-done(((bf16[8,208,128]{2,1,0:T(8,128)(2,1)}), bf16[8,208,128]{2,1,0:T(8,128)(2,1)S(1)}, u32[]{:S(2)}, u32[]{:S(2)}) %all-to-all-start) | async-done | bytes 426016 | tf_op jit(solution)/shard_map/all_to_all | solution.py:464
  42.2 3.3 %row_sums.1 = (f32[8,2,4,4,128]{4,3,2,1,0:T(4,128)}, f32[2,4,4,128]{3,2,1,0:T(4,128)S(1)}, bf16[2,4,3,256,512]{4,3,2,1,0:T(8,128)(2,1)}) custom-call(bf16[4,1040,128]{2,1,0:T(8,128)(2,1)S(1)} %all-to-all-done.1.same_ref, bf16[4,1040,128]{2,1,0:T(8,128)(2,1)S(1)} %collective-permute-done.2.other_ref, bf16[4,2,208,128]{3,2,1,0:T(8,128)(2,1)S(1)} %bitcast.3), custom_call_target="tpu_custom_call" | custom-call | tf_op jit(solution)/shard_map/row_sums/pallas_call | solution.py:65
  45.5 4.0 %all-to-all-start.2 = ((f32[8,2,4,4,128]{4,3,2,1,0:T(4,128)}), f32[8,2,4,4,128]{4,3,2,1,0:T(4,128)S(1)}, u32[]{:S(2)}, u32[]{:S(2)}) async-start(f32[8,2,4,4,128]{4,3,2,1,0:T(4,128)} %get-tuple-element.13), calls=%async_computation.2 | async-start | bytes 262144 | tf_op jit(solution)/shard_map/all_to_all | solution.py:467
  49.4 3.7 %raw_scores.1.score_hbm = bf16[2,4,3,256,512]{4,3,2,1,0:T(8,128)(2,1)} custom-call(bf16[4,1040,128]{2,1,0:T(8,128)(2,1)S(1)} %all-to-all-done.1.same_ref, bf16[4,1040,128]{2,1,0:T(8,128)(2,1)S(1)} %collective-permute-done.2.other_ref, bf16[4,2,208,128]{3,2,1,0:T(8,128)(2,1)S(1)} %bitcast.4, bf16[2,4,3,256,512]{4,3,2,1,0:T(8,128)(2,1)} %get-tuple-element.12.prob_hbm), custom_call_target="tpu_custom_call" | custom-call | tf_op jit(solution)/shard_map/raw_scores/pallas_call | solution.py:65
  53.1 2.4 %all-to-all-done.2.norm_ref = f32[8,2,4,4,128]{4,3,2,1,0:T(4,128)S(1)} async-done(((f32[8,2,4,4,128]{4,3,2,1,0:T(4,128)}), f32[8,2,4,4,128]{4,3,2,1,0:T(4,128)S(1)}, u32[]{:S(2)}, u32[]{:S(2)}) %all-to-all-start.2) | async-done | bytes 131104 | tf_op jit(solution)/shard_map/all_to_all | solution.py:467
  55.6 4.0 %key_gradients.1 = (bf16[8,192,128]{2,1,0:T(8,128)(2,1)}, f32[2,4,4,128]{3,2,1,0:T(4,128)S(1)}) custom-call(bf16[4,1040,128]{2,1,0:T(8,128)(2,1)S(1)} %all-to-all-done.1.same_ref, bf16[4,1040,128]{2,1,0:T(8,128)(2,1)S(1)} %collective-permute-done.2.other_ref, f32[8,2,4,4,128]{4,3,2,1,0:T(4,128)S(1)} %all-to-all-done.2.norm_ref, ...), custom_call_target="tpu_custom_call" | custom-call | tf_op jit(solution)/shard_map/key_gradients/pallas_call | solution.py:65
  59.6 3.5 %all-to-all-start.4 = ((bf16[8,192,128]{2,1,0:T(8,128)(2,1)}), bf16[8,192,128]{2,1,0:T(8,128)(2,1)S(1)}, u32[]{:S(2)}, u32[]{:S(2)}) async-start(bf16[8,192,128]{2,1,0:T(8,128)(2,1)} %get-tuple-element.18), calls=%async_computation.4 | async-start | bytes 786432 | tf_op jit(solution)/shard_map/all_to_all | solution.py:469
  63.1 2.6 %query_gradients.1 = (bf16[4,128,512]{2,1,0:T(8,128)(2,1)S(1)}, bf16[4,128,512]{2,1,0:T(8,128)(2,1)S(1)}) custom-call(bf16[4,2,208,128]{3,2,1,0:T(8,128)(2,1)S(1)} %bitcast.5, bf16[2,4,3,256,512]{4,3,2,1,0:T(8,128)(2,1)} %raw_scores.1.score_hbm, f32[2,4,4,128]{3,2,1,0:T(4,128)S(1)} %get-tuple-element.15.weight_ref), custom_call_target="tpu_custom_call" | custom-call | tf_op jit(solution)/shard_map/query_gradients/pallas_call | solution.py:65
  65.7 1.9 %collective-permute-start.3 = (bf16[4,128,512]{2,1,0:T(8,128)(2,1)S(1)}, bf16[4,128,512]{2,1,0:T(8,128)(2,1)S(1)}, u32[]{:S(2)}, u32[]{:S(2)}) collective-permute-start(bf16[4,128,512]{2,1,0:T(8,128)(2,1)S(1)} %get-tuple-element.17), channel_id=1, source_target_pairs={{0,8},{8,0},{1,9},{9,1},{2,10},{10,2},{3,11},{11,3},{4,12},{12,4},... | collective-permute-start | bytes 1572872 | tf_op jit(solution)/shard_map/ppermute | solution.py:470
  67.6 1.9 %collective-permute-done.3.other_ref = bf16[4,128,512]{2,1,0:T(8,128)(2,1)S(1)} collective-permute-done((bf16[4,128,512]{2,1,0:T(8,128)(2,1)S(1)}, bf16[4,128,512]{2,1,0:T(8,128)(2,1)S(1)}, u32[]{:S(2)}, u32[]{:S(2)}) %collective-permute-start.3) | collective-permute-done | bytes 524320 | tf_op jit(solution)/shard_map/ppermute | solution.py:470
  70.4 4.3 %all-to-all-done.4.dkv_ref = bf16[8,192,128]{2,1,0:T(8,128)(2,1)S(1)} async-done(((bf16[8,192,128]{2,1,0:T(8,128)(2,1)}), bf16[8,192,128]{2,1,0:T(8,128)(2,1)S(1)}, u32[]{:S(2)}, u32[]{:S(2)}) %all-to-all-start.4) | async-done | bytes 393248 | tf_op jit(solution)/shard_map/all_to_all | solution.py:469
  74.6 3.5 %all-to-all-start.3 = ((bf16[4,128,512]{2,1,0:T(8,128)(2,1)}), bf16[4,128,512]{2,1,0:T(8,128)(2,1)S(1)}, u32[]{:S(2)}, u32[]{:S(2)}) async-start(bf16[4,128,512]{2,1,0:T(8,128)(2,1)} %sum_cores.1), calls=%async_computation.3 | async-start | bytes 1048576 | tf_op jit(solution)/shard_map/all_to_all | solution.py:480
  78.2 1.3 %collective-permute-start.4 = (bf16[128,128]{1,0:T(8,128)(2,1)S(1)}, bf16[128,128]{1,0:T(8,128)(2,1)S(1)}, u32[]{:S(2)}, u32[]{:S(2)}) collective-permute-start(bf16[128,128]{1,0:T(8,128)(2,1)S(1)} %get-tuple-element.20), channel_id=1, source_target_pairs={{128,0},{256,128},{129,1},{257,129},{130,2},{258,130},{131,3},{259... | collective-permute-start | bytes 98312 | tf_op jit(solution)/shard_map/ppermute | solution.py:477
  80.8 5.6 %all-to-all-done.3.dq_ref = bf16[4,128,512]{2,1,0:T(8,128)(2,1)S(1)} async-done(((bf16[4,128,512]{2,1,0:T(8,128)(2,1)}), bf16[4,128,512]{2,1,0:T(8,128)(2,1)S(1)}, u32[]{:S(2)}, u32[]{:S(2)}) %all-to-all-start.3) | async-done | bytes 524320 | tf_op jit(solution)/shard_map/all_to_all | solution.py:480
  86.4 4.1 %collective-permute-done.4.one_ref = bf16[128,128]{1,0:T(8,128)(2,1)S(1)} collective-permute-done((bf16[128,128]{1,0:T(8,128)(2,1)S(1)}, bf16[128,128]{1,0:T(8,128)(2,1)S(1)}, u32[]{:S(2)}, u32[]{:S(2)}) %collective-permute-start.4) | collective-permute-done | bytes 32800 | tf_op jit(solution)/shard_map/ppermute | solution.py:477
  90.5 7.6 %collective-permute-done.5.two_ref = bf16[128,128]{1,0:T(8,128)(2,1)S(1)} collective-permute-done((bf16[128,128]{1,0:T(8,128)(2,1)S(1)}, bf16[128,128]{1,0:T(8,128)(2,1)S(1)}, u32[]{:S(2)}, u32[]{:S(2)}) %collective-permute-start.5) | collective-permute-done | bytes 32800 | tf_op jit(solution)/shard_map/ppermute | solution.py:478
  (9 shorter events, 3.1 us)
Async XLA Ops:
  2.9 4.3 %copy-start = (bf16[128,128]{1,0:T(8,128)(2,1)S(1)}, bf16[128,128]{1,0:T(8,128)(2,1)}, u32[]{:S(2)}) copy-start(bf16[128,128]{1,0:T(8,128)(2,1)} %own_ref.1) | copy-start | bytes 98308
  3.0 23.3 %all-to-all-start.1 = ((bf16[4,1040,128]{2,1,0:T(8,128)(2,1)}), bf16[4,1040,128]{2,1,0:T(8,128)(2,1)S(1)}, u32[]{:S(2)}, u32[]{:S(2)}) async-start(bf16[4,1040,128]{2,1,0:T(8,128)(2,1)} %pack_queries.1), calls=%async_computation.1 | async-start | bytes 2129920 | tf_op jit(solution)/shard_map/all_to_all | solution.py:459
  7.3 15.7 %collective-permute-start = (bf16[128,128]{1,0:T(8,128)(2,1)S(1)}, bf16[128,128]{1,0:T(8,128)(2,1)S(1)}, u32[]{:S(2)}, u32[]{:S(2)}) collective-permute-start(bf16[128,128]{1,0:T(8,128)(2,1)S(1)} %copy-done), channel_id=1, source_target_pairs={{0,128},{128,256},{1,129},{129,257},{2,130},{130,258},{3,131},{131... | collective-permute-start | bytes 98312 | tf_op jit(solution)/shard_map/ppermute | solution.py:449
  16.4 8.3 %collective-permute-start.1 = (bf16[128,128]{1,0:T(8,128)(2,1)S(1)}, bf16[128,128]{1,0:T(8,128)(2,1)S(1)}, u32[]{:S(2)}, u32[]{:S(2)}) collective-permute-start(bf16[128,128]{1,0:T(8,128)(2,1)S(1)} %copy-done), channel_id=1, source_target_pairs={{0,352},{32,320},{64,288},{96,256},{1,353},{33,321},{65,289},{97,2... | collective-permute-start | bytes 98312 | tf_op jit(solution)/shard_map/ppermute | solution.py:448
  26.3 15.9 %all-to-all-start = ((bf16[8,208,128]{2,1,0:T(8,128)(2,1)}), bf16[8,208,128]{2,1,0:T(8,128)(2,1)S(1)}, u32[]{:S(2)}, u32[]{:S(2)}) async-start(bf16[8,208,128]{2,1,0:T(8,128)(2,1)} %pack_keys.1), calls=%async_computation | async-start | bytes 851968 | tf_op jit(solution)/shard_map/all_to_all | solution.py:464
  31.2 11.0 %collective-permute-start.2 = (bf16[4,1040,128]{2,1,0:T(8,128)(2,1)S(1)}, bf16[4,1040,128]{2,1,0:T(8,128)(2,1)S(1)}, u32[]{:S(2)}, u32[]{:S(2)}) collective-permute-start(bf16[4,1040,128]{2,1,0:T(8,128)(2,1)S(1)} %all-to-all-done.1.same_ref), channel_id=1, source_target_pairs={{0,8},{8,0},{1,9},{9,1},{2,10},{10,2},{3,11},{11,3},{4,12},{12,4},... | collective-permute-start | bytes 3194888 | tf_op jit(solution)/shard_map/ppermute | solution.py:460
  45.5 10.1 %all-to-all-start.2 = ((f32[8,2,4,4,128]{4,3,2,1,0:T(4,128)}), f32[8,2,4,4,128]{4,3,2,1,0:T(4,128)S(1)}, u32[]{:S(2)}, u32[]{:S(2)}) async-start(f32[8,2,4,4,128]{4,3,2,1,0:T(4,128)} %get-tuple-element.13), calls=%async_computation.2 | async-start | bytes 262144 | tf_op jit(solution)/shard_map/all_to_all | solution.py:467
  59.6 15.0 %all-to-all-start.4 = ((bf16[8,192,128]{2,1,0:T(8,128)(2,1)}), bf16[8,192,128]{2,1,0:T(8,128)(2,1)S(1)}, u32[]{:S(2)}, u32[]{:S(2)}) async-start(bf16[8,192,128]{2,1,0:T(8,128)(2,1)} %get-tuple-element.18), calls=%async_computation.4 | async-start | bytes 786432 | tf_op jit(solution)/shard_map/all_to_all | solution.py:469
  65.7 3.8 %collective-permute-start.3 = (bf16[4,128,512]{2,1,0:T(8,128)(2,1)S(1)}, bf16[4,128,512]{2,1,0:T(8,128)(2,1)S(1)}, u32[]{:S(2)}, u32[]{:S(2)}) collective-permute-start(bf16[4,128,512]{2,1,0:T(8,128)(2,1)S(1)} %get-tuple-element.17), channel_id=1, source_target_pairs={{0,8},{8,0},{1,9},{9,1},{2,10},{10,2},{3,11},{11,3},{4,12},{12,4},... | collective-permute-start | bytes 1572872 | tf_op jit(solution)/shard_map/ppermute | solution.py:470
  74.6 11.7 %all-to-all-start.3 = ((bf16[4,128,512]{2,1,0:T(8,128)(2,1)}), bf16[4,128,512]{2,1,0:T(8,128)(2,1)S(1)}, u32[]{:S(2)}, u32[]{:S(2)}) async-start(bf16[4,128,512]{2,1,0:T(8,128)(2,1)} %sum_cores.1), calls=%async_computation.3 | async-start | bytes 1048576 | tf_op jit(solution)/shard_map/all_to_all | solution.py:480
  78.2 12.3 %collective-permute-start.4 = (bf16[128,128]{1,0:T(8,128)(2,1)S(1)}, bf16[128,128]{1,0:T(8,128)(2,1)S(1)}, u32[]{:S(2)}, u32[]{:S(2)}) collective-permute-start(bf16[128,128]{1,0:T(8,128)(2,1)S(1)} %get-tuple-element.20), channel_id=1, source_target_pairs={{128,0},{256,128},{129,1},{257,129},{130,2},{258,130},{131,3},{259... | collective-permute-start | bytes 98312 | tf_op jit(solution)/shard_map/ppermute | solution.py:477
  79.5 18.6 %collective-permute-start.5 = (bf16[128,128]{1,0:T(8,128)(2,1)S(1)}, bf16[128,128]{1,0:T(8,128)(2,1)S(1)}, u32[]{:S(2)}, u32[]{:S(2)}) collective-permute-start(bf16[128,128]{1,0:T(8,128)(2,1)S(1)} %get-tuple-element.21), channel_id=1, source_target_pairs={{352,0},{320,32},{288,64},{256,96},{353,1},{321,33},{289,65},{257,... | collective-permute-start | bytes 98312 | tf_op jit(solution)/shard_map/ppermute | solution.py:478

commit v4 on v3

--- a/solution.py
+++ b/solution.py
@@ -27,18 +27,19 @@
 LOG_SCALE = math.log2(SCALE)
 X_AXES = ("xh", "pair")
 Z_AXES = ("zg", "zr")
-MIRROR = [(r, 11 - r) for r in range(4)]
+FAR = [(r, 8 + (r + 2) % 4) for r in range(4)]
 PLANE = ("xh", "core", "pair")
 NT = (((1,), (1,)), ((), ()))
 NN = (((1,), (0,)), ((), ()))
 VMEM_LIMIT = 40 * 1024 * 1024
+LONG = pl.CostEstimate(flops=40_000_000_000, bytes_accessed=120_000_000, transcendentals=0)
 
 
 def dot(a, b, dims):
     return lax.dot_general(a, b, dims, preferred_element_type=F32)
 
 
-def call(kernel, name, out_shape, scratch=(), near=(), far=(), far_out=()):
+def call(kernel, name, out_shape, scratch=(), near=(), far=(), far_out=(), cost=None):
     def bound(*args):
         specs = [
             pl.BlockSpec(memory_space=pltpu.HBM if i in far else pltpu.VMEM)
@@ -60,6 +61,7 @@
             out_specs=out_specs,
             scratch_shapes=scratch,
             name=name,
+            cost_estimate=cost,
             compiler_params=pltpu.CompilerParams(vmem_limit_bytes=VMEM_LIMIT),
         )
         got = run(*kept)
@@ -79,17 +81,21 @@
         pltpu.make_async_copy(far, ref, sems.at[i])
         for i, (far, ref) in enumerate(
             (
+                (q_hbm, q_ref),
                 (mask_hbm, mask_ref),
+                (seg_hbm, seg_ref),
                 (g_hbm, g_ref),
                 (o_hbm, o_ref),
-                (q_hbm, q_ref),
-                (seg_hbm, seg_ref),
             )
         )
     ]
     for copy in copies:
         copy.start()
-    for copy in copies:
+    copies[0].wait()
+    for h in range(HEADS):
+        for x in range(4):
+            out_ref[x, h * TOK : (h + 1) * TOK, :] = q_ref[:, h * HEAD : (h + 1) * HEAD]
+    for copy in copies[1:]:
         copy.wait()
     mask = jnp.broadcast_to(mask_ref[...].astype(F32), (TOK, TOK)).T
     rows = []
@@ -99,7 +105,6 @@
         rows.append(jnp.sum((cot * o_ref[:, lanes].astype(F32)).T, axis=0, keepdims=True))
         cot = cot.astype(BF)
         for x in range(4):
-            out_ref[x, h * TOK : (h + 1) * TOK, :] = q_ref[:, lanes]
             out_ref[x, COLS + h * TOK : COLS + (h + 1) * TOK, :] = cot
     delta = jnp.concatenate(rows, axis=0)
     high = delta.astype(BF).astype(F32)
@@ -111,7 +116,7 @@
         out_ref[x, 2 * COLS :, :] = tail
 
 
-def pack_keys(own_ref, one_ref, two_ref, seg_ref, out_ref):
+def pack_keys(own_ref, two_ref, one_ref, seg_ref, out_ref):
     tail = jnp.concatenate(
         [seg_ref[...].astype(F32), jnp.zeros((15, TOK), F32)], axis=0
     ).astype(BF)
@@ -192,7 +197,7 @@
     key_segments(kv_ref, pair, turn_ref, seg_ref)
 
     def body(n):
-        def sources(hx, _):
+        def sources(hx):
             for other, q_ref in enumerate((same_ref, other_ref)):
                 from_core = (1 - core) if other else core
                 segs = q_ref[2 * hx, 2 * COLS :, :].astype(F32)[8:9]
@@ -217,9 +222,9 @@
                         piece = jnp.broadcast_to(norm[:, lanes], (8, TOK))
                         out_ref[:, from_core, x, h : h + 1, :] = piece.reshape(8, 1, TOK)
                     blocks(prob_ref, prob_hbm, n, other, x, sems).start()
-            return 0
-
-        lax.fori_loop(0, 2, sources, 0)
+
+        sources(0)
+        sources(1)
         for other in range(2):
             for x in range(4):
                 blocks(prob_ref, prob_hbm, n, other, x, sems).wait()
@@ -363,16 +368,19 @@
     out_ref[...] = (same_ref[...].astype(F32) + other_ref[...].astype(F32)).astype(BF)
 
 
-def finish(dq_ref, own_ref, one_ref, two_ref, out_q_ref, out_kv_ref):
+def finish_keys(own_ref, one_ref, two_ref, out_ref):
+    out_ref[...] = (
+        own_ref[...] + one_ref[...].astype(F32) + two_ref[...].astype(F32)
+    ).astype(BF)
+
+
+def finish_queries(dq_ref, out_ref):
     total = dq_ref[0].astype(F32)
     for x in range(1, 4):
         total += dq_ref[x].astype(F32)
     for h in range(HEADS):
         lanes = slice(h * HEAD, (h + 1) * HEAD)
-        out_q_ref[:, lanes] = total[:, lanes].T.astype(BF)
-    out_kv_ref[...] = (
-        own_ref[...] + one_ref[...].astype(F32) + two_ref[...].astype(F32)
-    ).astype(BF)
+        out_ref[:, lanes] = total[:, lanes].T.astype(BF)
 
 
 def local_kernels(same, other, kv, exchange):
@@ -380,7 +388,7 @@
         row_sums,
         "row_sums",
         (
-            shape((8, 2, 4, HEADS, TOK), F32),
+            pltpu.VMEM((8, 2, 4, HEADS, TOK), F32),
             pltpu.VMEM((2, 4, HEADS, TOK), F32),
             pltpu.HBM(FULL, BF),
         ),
@@ -412,7 +420,7 @@
         key_gradients,
         "key_gradients",
         (
-            shape((2 * GROUP, SLOTS * HALF, HEAD), BF),
+            pltpu.VMEM((2 * GROUP, SLOTS * HALF, HEAD), BF),
             pltpu.VMEM((2, 4, HEADS, TOK), F32),
         ),
         [
@@ -428,7 +436,7 @@
     dq_same, dq_other = call(
         query_gradients,
         "query_gradients",
-        (pltpu.VMEM((4, HEAD, COLS), BF), shape((4, HEAD, COLS), BF)),
+        (pltpu.VMEM((4, HEAD, COLS), BF), pltpu.VMEM((4, HEAD, COLS), BF)),
         [
             pltpu.VMEM((SLOTS, HEAD, KEYS), BF),
             pltpu.VMEM(FULL, BF),
@@ -445,21 +453,23 @@
     mask = loss_mask.reshape(1, TOK)
     swap = [(0, 1), (1, 0)]
 
-    two = lax.ppermute(stored_key_value, Z_AXES, MIRROR)
+    two = lax.ppermute(stored_key_value, Z_AXES, FAR)
     one = lax.ppermute(stored_key_value, "zg", [(0, 1), (1, 2)])
     wide = pltpu.VMEM((TOK, HEADS * HEAD), BF)
     line = pltpu.VMEM((1, TOK), jnp.int32)
     packed = call(
         pack_queries,
         "pack_queries",
-        shape((4, Q_ROWS, HEAD), BF),
+        pltpu.VMEM((4, Q_ROWS, HEAD), BF),
         [wide, wide, wide, line, line, pltpu.SemaphoreType.DMA((5,))],
         far=range(5),
     )(queries, out_grad, attn_out, seg, mask)
     same = lax.all_to_all(packed, X_AXES, 0, 0, tiled=True)
     other = lax.ppermute(same, "core", swap)
-    kv = call(pack_keys, "pack_keys", shape((2 * GROUP, KV_ROWS, HEAD), BF), near=(1, 2))(
-        stored_key_value, one, two, seg
+    kv = call(
+        pack_keys, "pack_keys", pltpu.VMEM((2 * GROUP, KV_ROWS, HEAD), BF), near=range(4)
+    )(
+        stored_key_value, two, one, seg
     )
     kv = lax.all_to_all(kv, ("zr", "pair"), 0, 0, tiled=True).reshape(GROUP, 2, KV_ROWS, HEAD)
 
@@ -468,22 +478,31 @@
     )
     dkv = lax.all_to_all(dkv, ("zr", "pair"), 0, 0, tiled=True)
     dq_other = lax.ppermute(dq_other, "core", swap)
+    dq = call(sum_cores, "sum_cores", pltpu.VMEM((4, HEAD, COLS), BF), near=(0, 1))(
+        dq_same, dq_other
+    )
+    dkv, dq = lax.optimization_barrier((dkv, dq))
     own, one, two = call(
         sum_keys,
         "sum_keys",
-        (pltpu.VMEM((TOK, HEAD), F32), shape((TOK, HEAD), BF), shape((TOK, HEAD), BF)),
+        (
+            pltpu.VMEM((TOK, HEAD), F32),
+            pltpu.VMEM((TOK, HEAD), BF),
+            pltpu.VMEM((TOK, HEAD), BF),
+        ),
         near=(0,),
     )(dkv)
     one = lax.ppermute(one, "zg", [(1, 0), (2, 1)])
-    two = lax.ppermute(two, Z_AXES, [(b, a) for a, b in MIRROR])
-    dq = call(sum_cores, "sum_cores", shape((4, HEAD, COLS), BF), near=(0, 1))(dq_same, dq_other)
+    two = lax.ppermute(two, Z_AXES, [(b, a) for a, b in FAR])
     dq = lax.all_to_all(dq, X_AXES, 0, 0, tiled=True)
-    return call(
-        finish,
-        "finish",
-        (shape((TOK, HEADS * HEAD), BF), shape((TOK, HEAD), BF)),
-        near=range(4),
-    )(dq, own, one, two)
+    kv_grad = call(
+        finish_keys, "finish_keys", shape((TOK, HEAD), BF), near=range(3), cost=LONG
+    )(own, one, two)
+    dq, kv_grad = lax.optimization_barrier((dq, kv_grad))
+    query_gradient = call(
+        finish_queries, "finish_queries", shape((TOK, HEADS * HEAD), BF), near=(0,)
+    )(dq)
+    return query_gradient, kv_grad
 
 
 def solution(mesh):

time: 100 us -> 93.8 us (0.938)
  waiting for transfers between devices: 36.6 us -> 30.1 us
  starting transfers between devices: 42.2 us -> 43.4 us
    ppermute x2, starting transfers between devices: 7.88 us -> 16.1 us  [the longest x1 14.8 us: per_device(): two = lax.ppermute(stored_key_value, Z_AXES, FAR)]
    ppermute x1, starting transfers between devices: 9.08 us -> 1.29 us  [per_device(): one = lax.ppermute(stored_key_value, 'zg', [(0, 1), (1, 2)])]
    all_to_all x1, waiting for transfers between devices: 5.59 us -> 0.01 us  [per_device(): dq = lax.all_to_all(dq, X_AXES, 0, 0, tiled=True)]
    ppermute x2, waiting for transfers between devices: 9.28 us -> 5.45 us  [the longest x1 5.18 us: per_device(): two = lax.ppermute(two, Z_AXES, [(b, a) for a, b in FAR])]
    ppermute x1, waiting for transfers between devices: 4.11 us -> 6.8 us  [per_device(): one = lax.ppermute(one, 'zg', [(1, 0), (2, 1)])]
    ppermute x1, waiting for transfers between devices: 0.01 us -> 1.3 us  [per_device(): one = lax.ppermute(stored_key_value, 'zg', [(0, 1), (1, 2)])]
    all_to_all x1, waiting for transfers between devices: 9.05 us -> 8.02 us  [per_device(): lax.all_to_all(kv, ('zr', 'pair'), 0, 0, tiled=True)]
    pallas_call x9 -> x10, Pallas kernels: 19.2 us -> 18.8 us  [bound(): got = run(*kept)]
where the time goes in v4:
time: 93.8 us; the launch traced here: 93.1 us
  starting transfers between devices  43.4 us (46%)
  waiting for transfers between devices  30.1 us (32%)
  Pallas kernels  18.8 us (20%)
    pallas_call x10, Pallas kernels, bound(): got = run(*kept)  18.8 us
    ppermute x1, starting transfers between devices, per_device(): two = lax.ppermute(stored_key_value, Z_AXES, FAR)  14.8 us
    all_to_all x1, waiting for transfers between devices, per_device(): lax.all_to_all(kv, ('zr', 'pair'), 0, 0, tiled=True)  8.02 us
    ppermute x1, waiting for transfers between devices, per_device(): one = lax.ppermute(one, 'zg', [(1, 0), (2, 1)])  6.8 us
    all_to_all x1, starting transfers between devices, per_device(): lax.all_to_all(kv, ('zr', 'pair'), 0, 0, tiled=True)  5.67 us
    ppermute x1, waiting for transfers between devices, per_device(): two = lax.ppermute(two, Z_AXES, [(b, a) for a, b in FAR])  5.18 us
    all_to_all x1, starting transfers between devices, per_device(): same = lax.all_to_all(packed, X_AXES, 0, 0, tiled=True)  4.3 us
    all_to_all x1, waiting for transfers between devices, per_device(): dkv = lax.all_to_all(dkv, ('zr', 'pair'), 0, 0, tiled=True)  4.24 us
  transfers between devices with their start and end apart: 11, of which 8 were waited for; matrix products, arithmetic and copies ran while one was open for 0% of the time, Pallas kernels for 9%

profile of v4, /device:TPU:24, one launch (start us, length us, event | category | flops | bytes accessed | tf_op | source)
XLA Modules:
  0.0 93.1 jit_solution(4790076612833040084)
XLA Ops:
  0.6 2.3 %pack_queries.1 = bf16[4,1040,128]{2,1,0:T(8,128)(2,1)} custom-call(bf16[128,512]{1,0:T(8,128)(2,1)} %q_hbm.1, bf16[128,512]{1,0:T(8,128)(2,1)} %g_hbm.1, bf16[128,512]{1,0:T(8,128)(2,1)} %o_hbm.1, s32[1,128]{1,0:T(1,128)} %bitcast.6, s32[1,128]{1,0:T(1,128)} %bitcast.8), custom_call_target="tpu_custom_call" | custom-call | tf_op jit(solution)/shard_map/pack_queries/pallas_call | solution.py:67
  3.0 4.3 %all-to-all-start = ((bf16[4,1040,128]{2,1,0:T(8,128)(2,1)}), bf16[4,1040,128]{2,1,0:T(8,128)(2,1)S(1)}, u32[]{:S(2)}, u32[]{:S(2)}) async-start(bf16[4,1040,128]{2,1,0:T(8,128)(2,1)} %pack_queries.1), calls=%async_computation | async-start | bytes 2129920 | tf_op jit(solution)/shard_map/all_to_all | solution.py:467
  7.3 14.8 %collective-permute-start.1 = (bf16[128,128]{1,0:T(8,128)(2,1)S(1)}, bf16[128,128]{1,0:T(8,128)(2,1)S(1)}, u32[]{:S(2)}, u32[]{:S(2)}) collective-permute-start(bf16[128,128]{1,0:T(8,128)(2,1)S(1)} %copy-done), channel_id=1, source_target_pairs={{0,320},{32,352},{64,256},{96,288},{1,321},{33,353},{65,257},{97,2... | collective-permute-start | bytes 98312 | tf_op jit(solution)/shard_map/ppermute | solution.py:456
  22.1 1.3 %collective-permute-start.2 = (bf16[128,128]{1,0:T(8,128)(2,1)S(1)}, bf16[128,128]{1,0:T(8,128)(2,1)S(1)}, u32[]{:S(2)}, u32[]{:S(2)}) collective-permute-start(bf16[128,128]{1,0:T(8,128)(2,1)S(1)} %copy-done), channel_id=1, source_target_pairs={{0,128},{128,256},{1,129},{129,257},{2,130},{130,258},{3,131},{131... | collective-permute-start | bytes 98312 | tf_op jit(solution)/shard_map/ppermute | solution.py:457
  23.7 1.3 %collective-permute-done.2.one_ref = bf16[128,128]{1,0:T(8,128)(2,1)S(1)} collective-permute-done((bf16[128,128]{1,0:T(8,128)(2,1)S(1)}, bf16[128,128]{1,0:T(8,128)(2,1)S(1)}, u32[]{:S(2)}, u32[]{:S(2)}) %collective-permute-start.2) | collective-permute-done | bytes 32800 | tf_op jit(solution)/shard_map/ppermute | solution.py:457
  25.8 5.7 %all-to-all-start.1 = ((bf16[8,208,128]{2,1,0:T(8,128)(2,1)}), bf16[8,208,128]{2,1,0:T(8,128)(2,1)S(1)}, u32[]{:S(2)}, u32[]{:S(2)}) async-start(bf16[8,208,128]{2,1,0:T(8,128)(2,1)} %pack_keys.1), calls=%async_computation.1 | async-start | bytes 851968 | tf_op jit(solution)/shard_map/all_to_all | solution.py:474
  31.5 1.9 %collective-permute-start = (bf16[4,1040,128]{2,1,0:T(8,128)(2,1)S(1)}, bf16[4,1040,128]{2,1,0:T(8,128)(2,1)S(1)}, u32[]{:S(2)}, u32[]{:S(2)}) collective-permute-start(bf16[4,1040,128]{2,1,0:T(8,128)(2,1)S(1)} %all-to-all-done.same_ref), channel_id=1, source_target_pairs={{0,8},{8,0},{1,9},{9,1},{2,10},{10,2},{3,11},{11,3},{4,12},{12,4},... | collective-permute-start | bytes 3194888 | tf_op jit(solution)/shard_map/ppermute | solution.py:468
  33.4 8.0 %all-to-all-done.1 = bf16[8,208,128]{2,1,0:T(8,128)(2,1)S(1)} async-done(((bf16[8,208,128]{2,1,0:T(8,128)(2,1)}), bf16[8,208,128]{2,1,0:T(8,128)(2,1)S(1)}, u32[]{:S(2)}, u32[]{:S(2)}) %all-to-all-start.1) | async-done | bytes 426016 | tf_op jit(solution)/shard_map/all_to_all | solution.py:474
  41.5 3.1 %row_sums.1 = (f32[8,2,4,4,128]{4,3,2,1,0:T(4,128)}, f32[2,4,4,128]{3,2,1,0:T(4,128)S(1)}, bf16[2,4,3,256,512]{4,3,2,1,0:T(8,128)(2,1)}) custom-call(bf16[4,1040,128]{2,1,0:T(8,128)(2,1)S(1)} %all-to-all-done.same_ref, bf16[4,1040,128]{2,1,0:T(8,128)(2,1)S(1)} %collective-permute-done.other_ref, bf16[4,2,208,128]{3,2,1,0:T(8,128)(2,1)S(1)} %bitcast.3), custom_call_target="tpu_custom_call" | custom-call | tf_op jit(solution)/shard_map/row_sums/pallas_call | solution.py:67
  44.6 4.0 %all-to-all-start.2 = ((f32[8,2,4,4,128]{4,3,2,1,0:T(4,128)}), f32[8,2,4,4,128]{4,3,2,1,0:T(4,128)S(1)}, u32[]{:S(2)}, u32[]{:S(2)}) async-start(f32[8,2,4,4,128]{4,3,2,1,0:T(4,128)} %get-tuple-element.16), calls=%async_computation.2 | async-start | bytes 262144 | tf_op jit(solution)/shard_map/all_to_all | solution.py:477
  48.6 3.7 %raw_scores.1.score_hbm = bf16[2,4,3,256,512]{4,3,2,1,0:T(8,128)(2,1)} custom-call(bf16[4,1040,128]{2,1,0:T(8,128)(2,1)S(1)} %all-to-all-done.same_ref, bf16[4,1040,128]{2,1,0:T(8,128)(2,1)S(1)} %collective-permute-done.other_ref, bf16[4,2,208,128]{3,2,1,0:T(8,128)(2,1)S(1)} %bitcast.4, bf16[2,4,3,256,512]{4,3,2,1,0:T(8,128)(2,1)} %get-tuple-element.18.prob_hbm), custom_call_target="tpu_custom_call" | custom-call | tf_op jit(solution)/shard_map/raw_scores/pallas_call | solution.py:67
  52.3 2.4 %all-to-all-done.2.norm_ref = f32[8,2,4,4,128]{4,3,2,1,0:T(4,128)S(1)} async-done(((f32[8,2,4,4,128]{4,3,2,1,0:T(4,128)}), f32[8,2,4,4,128]{4,3,2,1,0:T(4,128)S(1)}, u32[]{:S(2)}, u32[]{:S(2)}) %all-to-all-start.2) | async-done | bytes 131104 | tf_op jit(solution)/shard_map/all_to_all | solution.py:477
  54.7 3.8 %key_gradients.1 = (bf16[8,192,128]{2,1,0:T(8,128)(2,1)}, f32[2,4,4,128]{3,2,1,0:T(4,128)S(1)}) custom-call(bf16[4,1040,128]{2,1,0:T(8,128)(2,1)S(1)} %all-to-all-done.same_ref, bf16[4,1040,128]{2,1,0:T(8,128)(2,1)S(1)} %collective-permute-done.other_ref, f32[8,2,4,4,128]{4,3,2,1,0:T(4,128)S(1)} %all-to-all-done.2.norm_ref, ...), custom_call_target="tpu_custom_call" | custom-call | tf_op jit(solution)/shard_map/key_gradients/pallas_call | solution.py:67
  58.5 3.5 %all-to-all-start.3 = ((bf16[8,192,128]{2,1,0:T(8,128)(2,1)}), bf16[8,192,128]{2,1,0:T(8,128)(2,1)S(1)}, u32[]{:S(2)}, u32[]{:S(2)}) async-start(bf16[8,192,128]{2,1,0:T(8,128)(2,1)} %get-tuple-element.19), calls=%async_computation.3 | async-start | bytes 786432 | tf_op jit(solution)/shard_map/all_to_all | solution.py:479
  62.0 2.6 %query_gradients.1 = (bf16[4,128,512]{2,1,0:T(8,128)(2,1)S(1)}, bf16[4,128,512]{2,1,0:T(8,128)(2,1)S(1)}) custom-call(bf16[4,2,208,128]{3,2,1,0:T(8,128)(2,1)S(1)} %bitcast.5, bf16[2,4,3,256,512]{4,3,2,1,0:T(8,128)(2,1)} %raw_scores.1.score_hbm, f32[2,4,4,128]{3,2,1,0:T(4,128)S(1)} %get-tuple-element.20.weight_ref), custom_call_target="tpu_custom_call" | custom-call | tf_op jit(solution)/shard_map/query_gradients/pallas_call | solution.py:67
  64.6 1.9 %collective-permute-start.3 = (bf16[4,128,512]{2,1,0:T(8,128)(2,1)S(1)}, bf16[4,128,512]{2,1,0:T(8,128)(2,1)S(1)}, u32[]{:S(2)}, u32[]{:S(2)}) collective-permute-start(bf16[4,128,512]{2,1,0:T(8,128)(2,1)S(1)} %get-tuple-element.22), channel_id=1, source_target_pairs={{0,8},{8,0},{1,9},{9,1},{2,10},{10,2},{3,11},{11,3},{4,12},{12,4},... | collective-permute-start | bytes 1572872 | tf_op jit(solution)/shard_map/ppermute | solution.py:480
  66.5 1.9 %collective-permute-done.3.other_ref = bf16[4,128,512]{2,1,0:T(8,128)(2,1)S(1)} collective-permute-done((bf16[4,128,512]{2,1,0:T(8,128)(2,1)S(1)}, bf16[4,128,512]{2,1,0:T(8,128)(2,1)S(1)}, u32[]{:S(2)}, u32[]{:S(2)}) %collective-permute-start.3) | collective-permute-done | bytes 524320 | tf_op jit(solution)/shard_map/ppermute | solution.py:480
  68.4 0.9 sum_cores.1
  69.3 4.2 %all-to-all-done.3.dkv_ref = bf16[8,192,128]{2,1,0:T(8,128)(2,1)S(1)} async-done(((bf16[8,192,128]{2,1,0:T(8,128)(2,1)}), bf16[8,192,128]{2,1,0:T(8,128)(2,1)S(1)}, u32[]{:S(2)}, u32[]{:S(2)}) %all-to-all-start.3) | async-done | bytes 393248 | tf_op jit(solution)/shard_map/all_to_all | solution.py:479
  73.6 1.3 %collective-permute-start.4 = (bf16[128,128]{1,0:T(8,128)(2,1)S(1)}, bf16[128,128]{1,0:T(8,128)(2,1)S(1)}, u32[]{:S(2)}, u32[]{:S(2)}) collective-permute-start(bf16[128,128]{1,0:T(8,128)(2,1)S(1)} %get-tuple-element.26), channel_id=1, source_target_pairs={{128,0},{256,128},{129,1},{257,129},{130,2},{258,130},{131,3},{259... | collective-permute-start | bytes 98312 | tf_op jit(solution)/shard_map/ppermute | solution.py:495
  74.9 1.3 %collective-permute-start.5 = (bf16[128,128]{1,0:T(8,128)(2,1)S(1)}, bf16[128,128]{1,0:T(8,128)(2,1)S(1)}, u32[]{:S(2)}, u32[]{:S(2)}) collective-permute-start(bf16[128,128]{1,0:T(8,128)(2,1)S(1)} %get-tuple-element.27), channel_id=1, source_target_pairs={{320,0},{352,32},{256,64},{288,96},{321,1},{353,33},{257,65},{289,... | collective-permute-start | bytes 98312 | tf_op jit(solution)/shard_map/ppermute | solution.py:496
  76.2 3.5 %all-to-all-start.4 = ((bf16[4,128,512]{2,1,0:T(8,128)(2,1)}), bf16[4,128,512]{2,1,0:T(8,128)(2,1)S(1)}, u32[]{:S(2)}, u32[]{:S(2)}) async-start(bf16[4,128,512]{2,1,0:T(8,128)(2,1)} %sum_cores.1), calls=%async_computation.4 | async-start | bytes 1048576 | tf_op jit(solution)/shard_map/all_to_all | solution.py:497
  79.7 6.8 %collective-permute-done.4.one_ref = bf16[128,128]{1,0:T(8,128)(2,1)S(1)} collective-permute-done((bf16[128,128]{1,0:T(8,128)(2,1)S(1)}, bf16[128,128]{1,0:T(8,128)(2,1)S(1)}, u32[]{:S(2)}, u32[]{:S(2)}) %collective-permute-start.4) | collective-permute-done | bytes 32800 | tf_op jit(solution)/shard_map/ppermute | solution.py:495
  86.5 5.2 %collective-permute-done.5.two_ref = bf16[128,128]{1,0:T(8,128)(2,1)S(1)} collective-permute-done((bf16[128,128]{1,0:T(8,128)(2,1)S(1)}, bf16[128,128]{1,0:T(8,128)(2,1)S(1)}, u32[]{:S(2)}, u32[]{:S(2)}) %collective-permute-start.5) | collective-permute-done | bytes 32800 | tf_op jit(solution)/shard_map/ppermute | solution.py:496
  (12 shorter events, 2.6 us)
Async XLA Ops:
  3.0 4.3 %copy-start = (bf16[128,128]{1,0:T(8,128)(2,1)S(1)}, bf16[128,128]{1,0:T(8,128)(2,1)}, u32[]{:S(2)}) copy-start(bf16[128,128]{1,0:T(8,128)(2,1)} %own_ref.1) | copy-start | bytes 98308
  3.0 22.0 %copy-start.1 = (s32[128]{0:T(128)S(1)}, s32[128]{0:T(128)}, u32[]{:S(2)}) copy-start(s32[128]{0:T(128)} %param.10) | copy-start | bytes 1540
  3.0 22.9 %all-to-all-start = ((bf16[4,1040,128]{2,1,0:T(8,128)(2,1)}), bf16[4,1040,128]{2,1,0:T(8,128)(2,1)S(1)}, u32[]{:S(2)}, u32[]{:S(2)}) async-start(bf16[4,1040,128]{2,1,0:T(8,128)(2,1)} %pack_queries.1), calls=%async_computation | async-start | bytes 2129920 | tf_op jit(solution)/shard_map/all_to_all | solution.py:467
  7.3 16.4 %collective-permute-start.1 = (bf16[128,128]{1,0:T(8,128)(2,1)S(1)}, bf16[128,128]{1,0:T(8,128)(2,1)S(1)}, u32[]{:S(2)}, u32[]{:S(2)}) collective-permute-start(bf16[128,128]{1,0:T(8,128)(2,1)S(1)} %copy-done), channel_id=1, source_target_pairs={{0,320},{32,352},{64,256},{96,288},{1,321},{33,353},{65,257},{97,2... | collective-permute-start | bytes 98312 | tf_op jit(solution)/shard_map/ppermute | solution.py:456
  22.1 2.9 %collective-permute-start.2 = (bf16[128,128]{1,0:T(8,128)(2,1)S(1)}, bf16[128,128]{1,0:T(8,128)(2,1)S(1)}, u32[]{:S(2)}, u32[]{:S(2)}) collective-permute-start(bf16[128,128]{1,0:T(8,128)(2,1)S(1)} %copy-done), channel_id=1, source_target_pairs={{0,128},{128,256},{1,129},{129,257},{2,130},{130,258},{3,131},{131... | collective-permute-start | bytes 98312 | tf_op jit(solution)/shard_map/ppermute | solution.py:457
  25.8 15.6 %all-to-all-start.1 = ((bf16[8,208,128]{2,1,0:T(8,128)(2,1)}), bf16[8,208,128]{2,1,0:T(8,128)(2,1)S(1)}, u32[]{:S(2)}, u32[]{:S(2)}) async-start(bf16[8,208,128]{2,1,0:T(8,128)(2,1)} %pack_keys.1), calls=%async_computation.1 | async-start | bytes 851968 | tf_op jit(solution)/shard_map/all_to_all | solution.py:474
  31.5 9.9 %collective-permute-start = (bf16[4,1040,128]{2,1,0:T(8,128)(2,1)S(1)}, bf16[4,1040,128]{2,1,0:T(8,128)(2,1)S(1)}, u32[]{:S(2)}, u32[]{:S(2)}) collective-permute-start(bf16[4,1040,128]{2,1,0:T(8,128)(2,1)S(1)} %all-to-all-done.same_ref), channel_id=1, source_target_pairs={{0,8},{8,0},{1,9},{9,1},{2,10},{10,2},{3,11},{11,3},{4,12},{12,4},... | collective-permute-start | bytes 3194888 | tf_op jit(solution)/shard_map/ppermute | solution.py:468
  44.6 10.1 %all-to-all-start.2 = ((f32[8,2,4,4,128]{4,3,2,1,0:T(4,128)}), f32[8,2,4,4,128]{4,3,2,1,0:T(4,128)S(1)}, u32[]{:S(2)}, u32[]{:S(2)}) async-start(f32[8,2,4,4,128]{4,3,2,1,0:T(4,128)} %get-tuple-element.16), calls=%async_computation.2 | async-start | bytes 262144 | tf_op jit(solution)/shard_map/all_to_all | solution.py:477
  58.5 15.0 %all-to-all-start.3 = ((bf16[8,192,128]{2,1,0:T(8,128)(2,1)}), bf16[8,192,128]{2,1,0:T(8,128)(2,1)S(1)}, u32[]{:S(2)}, u32[]{:S(2)}) async-start(bf16[8,192,128]{2,1,0:T(8,128)(2,1)} %get-tuple-element.19), calls=%async_computation.3 | async-start | bytes 786432 | tf_op jit(solution)/shard_map/all_to_all | solution.py:479
  64.6 3.8 %collective-permute-start.3 = (bf16[4,128,512]{2,1,0:T(8,128)(2,1)S(1)}, bf16[4,128,512]{2,1,0:T(8,128)(2,1)S(1)}, u32[]{:S(2)}, u32[]{:S(2)}) collective-permute-start(bf16[4,128,512]{2,1,0:T(8,128)(2,1)S(1)} %get-tuple-element.22), channel_id=1, source_target_pairs={{0,8},{8,0},{1,9},{9,1},{2,10},{10,2},{3,11},{11,3},{4,12},{12,4},... | collective-permute-start | bytes 1572872 | tf_op jit(solution)/shard_map/ppermute | solution.py:480
  73.6 12.9 %collective-permute-start.4 = (bf16[128,128]{1,0:T(8,128)(2,1)S(1)}, bf16[128,128]{1,0:T(8,128)(2,1)S(1)}, u32[]{:S(2)}, u32[]{:S(2)}) collective-permute-start(bf16[128,128]{1,0:T(8,128)(2,1)S(1)} %get-tuple-element.26), channel_id=1, source_target_pairs={{128,0},{256,128},{129,1},{257,129},{130,2},{258,130},{131,3},{259... | collective-permute-start | bytes 98312 | tf_op jit(solution)/shard_map/ppermute | solution.py:495
  74.9 16.8 %collective-permute-start.5 = (bf16[128,128]{1,0:T(8,128)(2,1)S(1)}, bf16[128,128]{1,0:T(8,128)(2,1)S(1)}, u32[]{:S(2)}, u32[]{:S(2)}) collective-permute-start(bf16[128,128]{1,0:T(8,128)(2,1)S(1)} %get-tuple-element.27), channel_id=1, source_target_pairs={{320,0},{352,32},{256,64},{288,96},{321,1},{353,33},{257,65},{289,... | collective-permute-start | bytes 98312 | tf_op jit(solution)/shard_map/ppermute | solution.py:496
  76.2 16.1 %all-to-all-start.4 = ((bf16[4,128,512]{2,1,0:T(8,128)(2,1)}), bf16[4,128,512]{2,1,0:T(8,128)(2,1)S(1)}, u32[]{:S(2)}, u32[]{:S(2)}) async-start(bf16[4,128,512]{2,1,0:T(8,128)(2,1)} %sum_cores.1), calls=%async_computation.4 | async-start | bytes 1048576 | tf_op jit(solution)/shard_map/all_to_all | solution.py:497

commit v5 on v4

--- a/solution.py
+++ b/solution.py
@@ -75,7 +75,9 @@
 
 
 def pack_queries(
-    q_hbm, g_hbm, o_hbm, seg_hbm, mask_hbm, out_ref, q_ref, g_ref, o_ref, seg_ref, mask_ref, sems
+    q_hbm, g_hbm, o_hbm, seg_hbm, mask_hbm, kv_hbm,
+    out_ref, own_ref,
+    q_ref, g_ref, o_ref, seg_ref, mask_ref, kv_ref, sems,
 ):
     copies = [
         pltpu.make_async_copy(far, ref, sems.at[i])
@@ -86,6 +88,7 @@
                 (seg_hbm, seg_ref),
                 (g_hbm, g_ref),
                 (o_hbm, o_ref),
+                (kv_hbm, kv_ref),
             )
         )
     ]
@@ -93,8 +96,7 @@
         copy.start()
     copies[0].wait()
     for h in range(HEADS):
-        for x in range(4):
-            out_ref[x, h * TOK : (h + 1) * TOK, :] = q_ref[:, h * HEAD : (h + 1) * HEAD]
+        out_ref[h * TOK : (h + 1) * TOK, :] = q_ref[:, h * HEAD : (h + 1) * HEAD]
     for copy in copies[1:]:
         copy.wait()
     mask = jnp.broadcast_to(mask_ref[...].astype(F32), (TOK, TOK)).T
@@ -103,23 +105,27 @@
         lanes = slice(h * HEAD, (h + 1) * HEAD)
         cot = g_ref[:, lanes].astype(F32) * mask
         rows.append(jnp.sum((cot * o_ref[:, lanes].astype(F32)).T, axis=0, keepdims=True))
-        cot = cot.astype(BF)
-        for x in range(4):
-            out_ref[x, COLS + h * TOK : COLS + (h + 1) * TOK, :] = cot
+        out_ref[COLS + h * TOK : COLS + (h + 1) * TOK, :] = cot.astype(BF)
     delta = jnp.concatenate(rows, axis=0)
     high = delta.astype(BF).astype(F32)
     low = delta - high
-    tail = jnp.concatenate(
-        [high, low, seg_ref[...].astype(F32), jnp.zeros((7, TOK), F32)], axis=0
+    seg = seg_ref[...].astype(F32)
+    out_ref[2 * COLS :, :] = jnp.concatenate(
+        [high, low, seg, jnp.zeros((7, TOK), F32)], axis=0
     ).astype(BF)
-    for x in range(4):
-        out_ref[x, 2 * COLS :, :] = tail
-
-
-def pack_keys(own_ref, two_ref, one_ref, seg_ref, out_ref):
-    tail = jnp.concatenate(
-        [seg_ref[...].astype(F32), jnp.zeros((15, TOK), F32)], axis=0
-    ).astype(BF)
+    own_ref[:TOK, :] = kv_ref[...]
+    own_ref[TOK:, :] = jnp.concatenate([seg, jnp.zeros((15, TOK), F32)], axis=0).astype(BF)
+
+
+def gather_sources(both_ref, far_ref, near_ref, own_ref, out_ref):
+    place = position()
+    own = 2 * place[2] + place[4]
+    for step, ref in enumerate((own_ref, near_ref, far_ref, both_ref)):
+        out_ref[own ^ step] = ref[...]
+
+
+def pack_keys(own_ref, one_ref, two_ref, out_ref):
+    tail = own_ref[TOK:, :]
     for s, ref in enumerate((own_ref, one_ref, two_ref)):
         for half in range(2):
             part = ref[half * HALF : (half + 1) * HALF, :]
@@ -298,21 +304,22 @@
     weight_ref[0] = jnp.exp2(top_ref[0] - own)
     weight_ref[1] = jnp.exp2(top_ref[1] - far)
 
-    def scaled(x, _):
-        for other, source_ref in enumerate((same_ref, other_ref)):
-            weights = weight_ref[other, x]
+    for other, source_ref in enumerate((same_ref, other_ref)):
+        columns = jnp.concatenate(
+            [weight_ref[other].reshape(4 * HEADS, TOK), jnp.zeros((TOK - 4 * HEADS, TOK), F32)],
+            axis=0,
+        ).T
+        for x in range(4):
             for h in range(HEADS):
                 rows = slice(h * TOK, (h + 1) * TOK)
                 below = slice(COLS + h * TOK, COLS + (h + 1) * TOK)
-                by_row = jnp.broadcast_to(weights[h : h + 1], (TOK, TOK)).T
+                i = x * HEADS + h
+                by_row = jnp.broadcast_to(columns[:, i : i + 1], (TOK, HEAD))
                 q = source_ref[x, rows, :].astype(F32) * (by_row * SCALE)
                 q_ref[other, x, rows, :] = q.astype(BF)
                 g_ref[other, x, rows, :] = (
                     source_ref[x, below, :].astype(F32) * by_row
                 ).astype(BF)
-        return 0
-
-    lax.fori_loop(0, 4, scaled, 0)
 
     def body(n):
         for s in range(SLOTS):
@@ -368,7 +375,7 @@
     out_ref[...] = (same_ref[...].astype(F32) + other_ref[...].astype(F32)).astype(BF)
 
 
-def finish_keys(own_ref, one_ref, two_ref, out_ref):
+def finish_keys(own_ref, two_ref, one_ref, out_ref):
     out_ref[...] = (
         own_ref[...] + one_ref[...].astype(F32) + two_ref[...].astype(F32)
     ).astype(BF)
@@ -457,19 +464,24 @@
     one = lax.ppermute(stored_key_value, "zg", [(0, 1), (1, 2)])
     wide = pltpu.VMEM((TOK, HEADS * HEAD), BF)
     line = pltpu.VMEM((1, TOK), jnp.int32)
-    packed = call(
+    packed, own = call(
         pack_queries,
         "pack_queries",
-        pltpu.VMEM((4, Q_ROWS, HEAD), BF),
-        [wide, wide, wide, line, line, pltpu.SemaphoreType.DMA((5,))],
-        far=range(5),
-    )(queries, out_grad, attn_out, seg, mask)
-    same = lax.all_to_all(packed, X_AXES, 0, 0, tiled=True)
+        (pltpu.VMEM((Q_ROWS, HEAD), BF), pltpu.VMEM((TOK + 16, HEAD), BF)),
+        [wide, wide, wide, line, line, pltpu.VMEM((TOK, HEAD), BF), pltpu.SemaphoreType.DMA((6,))],
+        far=range(6),
+    )(queries, out_grad, attn_out, seg, mask, stored_key_value)
+    near = lax.ppermute(packed, "pair", swap)
+    far = lax.ppermute(packed, "xh", swap)
+    both = lax.ppermute(packed, X_AXES, [(i, 3 - i) for i in range(4)])
+    same = call(
+        gather_sources, "gather_sources", pltpu.VMEM((4, Q_ROWS, HEAD), BF), near=range(4), cost=LONG
+    )(both, far, near, packed)
     other = lax.ppermute(same, "core", swap)
     kv = call(
-        pack_keys, "pack_keys", pltpu.VMEM((2 * GROUP, KV_ROWS, HEAD), BF), near=range(4)
+        pack_keys, "pack_keys", pltpu.VMEM((2 * GROUP, KV_ROWS, HEAD), BF), near=range(3), cost=LONG
     )(
-        stored_key_value, two, one, seg
+        own, one, two
     )
     kv = lax.all_to_all(kv, ("zr", "pair"), 0, 0, tiled=True).reshape(GROUP, 2, KV_ROWS, HEAD)
 
@@ -492,12 +504,12 @@
         ),
         near=(0,),
     )(dkv)
+    two = lax.ppermute(two, Z_AXES, [(b, a) for a, b in FAR])
     one = lax.ppermute(one, "zg", [(1, 0), (2, 1)])
-    two = lax.ppermute(two, Z_AXES, [(b, a) for a, b in FAR])
     dq = lax.all_to_all(dq, X_AXES, 0, 0, tiled=True)
     kv_grad = call(
         finish_keys, "finish_keys", shape((TOK, HEAD), BF), near=range(3), cost=LONG
-    )(own, one, two)
+    )(own, two, one)
     dq, kv_grad = lax.optimization_barrier((dq, kv_grad))
     query_gradient = call(
         finish_queries, "finish_queries", shape((TOK, HEADS * HEAD), BF), near=(0,)

time: 93.8 us -> 93 us (level)
  starting transfers between devices: 43.4 us -> 46.8 us
  waiting for transfers between devices: 30.1 us -> 26.8 us
    ppermute x0 -> x3, starting transfers between devices: none -> 10.4 us  [the longest x1 4.64 us: per_device(): far = lax.ppermute(packed, 'xh', swap)]
    ppermute x0 -> x3, waiting for transfers between devices: none -> 8.26 us  [the longest x1 5.27 us: per_device(): both = lax.ppermute(packed, X_AXES, [(i, 3 - i) for i in range(4)])]
    all_to_all x1, waiting for transfers between devices: 8.02 us -> 0.01 us  [per_device(): lax.all_to_all(kv, ('zr', 'pair'), 0, 0, tiled=True)]
    ppermute x1, waiting for transfers between devices: 6.8 us -> 0.01 us  [per_device(): one = lax.ppermute(one, 'zg', [(1, 0), (2, 1)])]
    all_to_all x1 -> x0, starting transfers between devices: 4.3 us -> none  [per_device(): same = lax.all_to_all(packed, X_AXES, 0, 0, tiled=True)]
    ppermute x1, waiting for transfers between devices: 0.01 us -> 2.65 us  [per_device(): other = lax.ppermute(same, 'core', swap)]
    all_to_all x1, starting transfers between devices: 5.67 us -> 3.46 us  [per_device(): lax.all_to_all(kv, ('zr', 'pair'), 0, 0, tiled=True)]
    ppermute x1, waiting for transfers between devices: 5.18 us -> 6.64 us  [per_device(): two = lax.ppermute(two, Z_AXES, [(b, a) for a, b in FAR])]
  transfers between devices with their start and end apart: 11 -> 13, of which waited for: 8 -> 8; matrix products, arithmetic and copies ran while one was open for 0% -> 0% of each run, Pallas kernels for 9% -> 11%
where the time goes in v5:
time: 93 us; the launch traced here: 92.3 us
  starting transfers between devices  46.8 us (50%)
  waiting for transfers between devices  26.8 us (29%)
  Pallas kernels  18 us (19%)
    pallas_call x11, Pallas kernels, bound(): got = run(*kept)  18 us
    ppermute x1, starting transfers between devices, per_device(): two = lax.ppermute(stored_key_value, Z_AXES, FAR)  14.8 us
    ppermute x1, waiting for transfers between devices, per_device(): two = lax.ppermute(two, Z_AXES, [(b, a) for a, b in FAR])  6.64 us
    ppermute x1, waiting for transfers between devices, per_device(): both = lax.ppermute(packed, X_AXES, [(i, 3 - i) for i in range(4)])  5.27 us
    ppermute x1, starting transfers between devices, per_device(): far = lax.ppermute(packed, 'xh', swap)  4.64 us
    all_to_all x1, waiting for transfers between devices, per_device(): dkv = lax.all_to_all(dkv, ('zr', 'pair'), 0, 0, tiled=True)  4.24 us
    all_to_all x1, starting transfers between devices, per_device(): dq = lax.all_to_all(dq, X_AXES, 0, 0, tiled=True)  3.48 us
    all_to_all x1, starting transfers between devices, per_device(): dkv = lax.all_to_all(dkv, ('zr', 'pair'), 0, 0, tiled=True)  3.46 us
  transfers between devices with their start and end apart: 13, of which 8 were waited for; matrix products, arithmetic and copies ran while one was open for 0% of the time, Pallas kernels for 11%

profile of v5, /device:TPU:24, one launch (start us, length us, event | category | flops | bytes accessed | tf_op | source)
XLA Modules:
  0.0 92.3 jit_solution(4858298942927710174)
XLA Ops:
  0.6 14.8 %collective-permute-start.5 = (bf16[128,128]{1,0:T(8,128)(2,1)}, bf16[128,128]{1,0:T(8,128)(2,1)S(1)}, u32[]{:S(2)}, u32[]{:S(2)}) collective-permute-start(bf16[128,128]{1,0:T(8,128)(2,1)} %kv_hbm.1), channel_id=1, source_target_pairs={{0,320},{32,352},{64,256},{96,288},{1,321},{33,353},{65,257},{97,2... | collective-permute-start | bytes 98312 | tf_op jit(solution)/shard_map/ppermute | solution.py:463
  16.8 1.3 %pack_queries.1 = (bf16[1040,128]{1,0:T(8,128)(2,1)S(1)}, bf16[144,128]{1,0:T(8,128)(2,1)S(1)}) custom-call(bf16[128,512]{1,0:T(8,128)(2,1)} %q_hbm.1, bf16[128,512]{1,0:T(8,128)(2,1)} %g_hbm.1, bf16[128,512]{1,0:T(8,128)(2,1)} %o_hbm.1, s32[1,128]{1,0:T(1,128)} %bitcast.6, s32[1,128]{1,0:T(1,128)} %bitcast.7, bf16[128,128]{1,0:T(8,128)(2,1)} %kv_hbm.1), custom_call_target="tpu_custom_call" | custom-call | tf_op jit(solution)/shard_map/pack_queries/pallas_call | solution.py:67
  18.1 3.4 %collective-permute-start.2 = (bf16[1040,128]{1,0:T(8,128)(2,1)S(1)}, bf16[1040,128]{1,0:T(8,128)(2,1)S(1)}, u32[]{:S(2)}, u32[]{:S(2)}) collective-permute-start(bf16[1040,128]{1,0:T(8,128)(2,1)S(1)} %get-tuple-element.18.own_ref), channel_id=1, source_target_pairs={{0,1},{1,0},{2,3},{3,2},{4,5},{5,4},{6,7},{7,6},{8,9},{9,8},{10,11... | collective-permute-start | bytes 798728 | tf_op jit(solution)/shard_map/ppermute | solution.py:474
  21.5 4.6 %collective-permute-start.1 = (bf16[1040,128]{1,0:T(8,128)(2,1)S(1)}, bf16[1040,128]{1,0:T(8,128)(2,1)S(1)}, u32[]{:S(2)}, u32[]{:S(2)}) collective-permute-start(bf16[1040,128]{1,0:T(8,128)(2,1)S(1)} %get-tuple-element.18.own_ref), channel_id=1, source_target_pairs={{0,16},{16,0},{1,17},{17,1},{2,18},{18,2},{3,19},{19,3},{4,20},{20... | collective-permute-start | bytes 798728 | tf_op jit(solution)/shard_map/ppermute | solution.py:475
  26.2 2.4 %collective-permute-start = (bf16[1040,128]{1,0:T(8,128)(2,1)S(1)}, bf16[1040,128]{1,0:T(8,128)(2,1)S(1)}, u32[]{:S(2)}, u32[]{:S(2)}) collective-permute-start(bf16[1040,128]{1,0:T(8,128)(2,1)S(1)} %get-tuple-element.18.own_ref), channel_id=1, source_target_pairs={{0,17},{1,16},{16,1},{17,0},{2,19},{3,18},{18,3},{19,2},{4,21},{5,... | collective-permute-start | bytes 798728 | tf_op jit(solution)/shard_map/ppermute | solution.py:476
  29.4 3.5 %all-to-all-start = ((bf16[8,208,128]{2,1,0:T(8,128)(2,1)}), bf16[8,208,128]{2,1,0:T(8,128)(2,1)S(1)}, u32[]{:S(2)}, u32[]{:S(2)}) async-start(bf16[8,208,128]{2,1,0:T(8,128)(2,1)} %pack_keys.1), calls=%async_computation | async-start | bytes 851968 | tf_op jit(solution)/shard_map/all_to_all | solution.py:486
  32.9 3.0 %collective-permute-done.1.far_ref = bf16[1040,128]{1,0:T(8,128)(2,1)S(1)} collective-permute-done((bf16[1040,128]{1,0:T(8,128)(2,1)S(1)}, bf16[1040,128]{1,0:T(8,128)(2,1)S(1)}, u32[]{:S(2)}, u32[]{:S(2)}) %collective-permute-start.1) | collective-permute-done | bytes 266272 | tf_op jit(solution)/shard_map/ppermute | solution.py:475
  35.9 5.3 %collective-permute-done.both_ref = bf16[1040,128]{1,0:T(8,128)(2,1)S(1)} collective-permute-done((bf16[1040,128]{1,0:T(8,128)(2,1)S(1)}, bf16[1040,128]{1,0:T(8,128)(2,1)S(1)}, u32[]{:S(2)}, u32[]{:S(2)}) %collective-permute-start) | collective-permute-done | bytes 266272 | tf_op jit(solution)/shard_map/ppermute | solution.py:476
  41.2 1.9 %collective-permute-start.3 = (bf16[4,1040,128]{2,1,0:T(8,128)(2,1)S(1)}, bf16[4,1040,128]{2,1,0:T(8,128)(2,1)S(1)}, u32[]{:S(2)}, u32[]{:S(2)}) collective-permute-start(bf16[4,1040,128]{2,1,0:T(8,128)(2,1)S(1)} %gather_sources.1.same_ref), channel_id=1, source_target_pairs={{0,8},{8,0},{1,9},{9,1},{2,10},{10,2},{3,11},{11,3},{4,12},{12,4},... | collective-permute-start | bytes 3194888 | tf_op jit(solution)/shard_map/ppermute | solution.py:480
  43.2 2.6 %collective-permute-done.3.other_ref = bf16[4,1040,128]{2,1,0:T(8,128)(2,1)S(1)} collective-permute-done((bf16[4,1040,128]{2,1,0:T(8,128)(2,1)S(1)}, bf16[4,1040,128]{2,1,0:T(8,128)(2,1)S(1)}, u32[]{:S(2)}, u32[]{:S(2)}) %collective-permute-start.3) | collective-permute-done | bytes 1064992 | tf_op jit(solution)/shard_map/ppermute | solution.py:480
  45.8 3.1 %row_sums.1 = (f32[8,2,4,4,128]{4,3,2,1,0:T(4,128)}, f32[2,4,4,128]{3,2,1,0:T(4,128)S(1)}, bf16[2,4,3,256,512]{4,3,2,1,0:T(8,128)(2,1)}) custom-call(bf16[4,1040,128]{2,1,0:T(8,128)(2,1)S(1)} %gather_sources.1.same_ref, bf16[4,1040,128]{2,1,0:T(8,128)(2,1)S(1)} %collective-permute-done.3.other_ref, bf16[4,2,208,128]{3,2,1,0:T(8,128)(2,1)S(1)} %bitcast.3), custom_call_target="tpu_custom_call" | custom-call | tf_op jit(solution)/shard_map/row_sums/pallas_call | solution.py:67
  49.0 3.4 %all-to-all-start.1 = ((f32[8,2,4,4,128]{4,3,2,1,0:T(4,128)}), f32[8,2,4,4,128]{4,3,2,1,0:T(4,128)S(1)}, u32[]{:S(2)}, u32[]{:S(2)}) async-start(f32[8,2,4,4,128]{4,3,2,1,0:T(4,128)} %get-tuple-element.20), calls=%async_computation.1 | async-start | bytes 262144 | tf_op jit(solution)/shard_map/all_to_all | solution.py:489
  52.3 3.7 %raw_scores.1.score_hbm = bf16[2,4,3,256,512]{4,3,2,1,0:T(8,128)(2,1)} custom-call(bf16[4,1040,128]{2,1,0:T(8,128)(2,1)S(1)} %gather_sources.1.same_ref, bf16[4,1040,128]{2,1,0:T(8,128)(2,1)S(1)} %collective-permute-done.3.other_ref, bf16[4,2,208,128]{3,2,1,0:T(8,128)(2,1)S(1)} %bitcast.4, bf16[2,4,3,256,512]{4,3,2,1,0:T(8,128)(2,1)} %get-tuple-element.22.prob_hbm), custom_call_target="tpu_custom_call" | custom-call | tf_op jit(solution)/shard_map/raw_scores/pallas_call | solution.py:67
  56.0 2.4 %all-to-all-done.1.norm_ref = f32[8,2,4,4,128]{4,3,2,1,0:T(4,128)S(1)} async-done(((f32[8,2,4,4,128]{4,3,2,1,0:T(4,128)}), f32[8,2,4,4,128]{4,3,2,1,0:T(4,128)S(1)}, u32[]{:S(2)}, u32[]{:S(2)}) %all-to-all-start.1) | async-done | bytes 131104 | tf_op jit(solution)/shard_map/all_to_all | solution.py:489
  58.4 3.9 %key_gradients.1 = (bf16[8,192,128]{2,1,0:T(8,128)(2,1)}, f32[2,4,4,128]{3,2,1,0:T(4,128)S(1)}) custom-call(bf16[4,1040,128]{2,1,0:T(8,128)(2,1)S(1)} %gather_sources.1.same_ref, bf16[4,1040,128]{2,1,0:T(8,128)(2,1)S(1)} %collective-permute-done.3.other_ref, f32[8,2,4,4,128]{4,3,2,1,0:T(4,128)S(1)} %all-to-all-done.1.norm_ref, ...), custom_call_target="tpu_custom_call" | custom-call | tf_op jit(solution)/shard_map/key_gradients/pallas_call | solution.py:67
  62.3 3.5 %all-to-all-start.2 = ((bf16[8,192,128]{2,1,0:T(8,128)(2,1)}), bf16[8,192,128]{2,1,0:T(8,128)(2,1)S(1)}, u32[]{:S(2)}, u32[]{:S(2)}) async-start(bf16[8,192,128]{2,1,0:T(8,128)(2,1)} %get-tuple-element.23), calls=%async_computation.2 | async-start | bytes 786432 | tf_op jit(solution)/shard_map/all_to_all | solution.py:491
  65.8 2.6 %query_gradients.1 = (bf16[4,128,512]{2,1,0:T(8,128)(2,1)S(1)}, bf16[4,128,512]{2,1,0:T(8,128)(2,1)S(1)}) custom-call(bf16[4,2,208,128]{3,2,1,0:T(8,128)(2,1)S(1)} %bitcast.5, bf16[2,4,3,256,512]{4,3,2,1,0:T(8,128)(2,1)} %raw_scores.1.score_hbm, f32[2,4,4,128]{3,2,1,0:T(4,128)S(1)} %get-tuple-element.24.weight_ref), custom_call_target="tpu_custom_call" | custom-call | tf_op jit(solution)/shard_map/query_gradients/pallas_call | solution.py:67
  68.4 1.9 %collective-permute-start.6 = (bf16[4,128,512]{2,1,0:T(8,128)(2,1)S(1)}, bf16[4,128,512]{2,1,0:T(8,128)(2,1)S(1)}, u32[]{:S(2)}, u32[]{:S(2)}) collective-permute-start(bf16[4,128,512]{2,1,0:T(8,128)(2,1)S(1)} %get-tuple-element.26), channel_id=1, source_target_pairs={{0,8},{8,0},{1,9},{9,1},{2,10},{10,2},{3,11},{11,3},{4,12},{12,4},... | collective-permute-start | bytes 1572872 | tf_op jit(solution)/shard_map/ppermute | solution.py:492
  70.3 1.9 %collective-permute-done.6.other_ref = bf16[4,128,512]{2,1,0:T(8,128)(2,1)S(1)} collective-permute-done((bf16[4,128,512]{2,1,0:T(8,128)(2,1)S(1)}, bf16[4,128,512]{2,1,0:T(8,128)(2,1)S(1)}, u32[]{:S(2)}, u32[]{:S(2)}) %collective-permute-start.6) | collective-permute-done | bytes 524320 | tf_op jit(solution)/shard_map/ppermute | solution.py:492
  73.1 4.2 %all-to-all-done.2.dkv_ref = bf16[8,192,128]{2,1,0:T(8,128)(2,1)S(1)} async-done(((bf16[8,192,128]{2,1,0:T(8,128)(2,1)}), bf16[8,192,128]{2,1,0:T(8,128)(2,1)S(1)}, u32[]{:S(2)}, u32[]{:S(2)}) %all-to-all-start.2) | async-done | bytes 393248 | tf_op jit(solution)/shard_map/all_to_all | solution.py:491
  77.4 1.3 %collective-permute-start.7 = (bf16[128,128]{1,0:T(8,128)(2,1)S(1)}, bf16[128,128]{1,0:T(8,128)(2,1)S(1)}, u32[]{:S(2)}, u32[]{:S(2)}) collective-permute-start(bf16[128,128]{1,0:T(8,128)(2,1)S(1)} %get-tuple-element.30), channel_id=1, source_target_pairs={{320,0},{352,32},{256,64},{288,96},{321,1},{353,33},{257,65},{289,... | collective-permute-start | bytes 98312 | tf_op jit(solution)/shard_map/ppermute | solution.py:507
  78.7 1.3 %collective-permute-start.8 = (bf16[128,128]{1,0:T(8,128)(2,1)S(1)}, bf16[128,128]{1,0:T(8,128)(2,1)S(1)}, u32[]{:S(2)}, u32[]{:S(2)}) collective-permute-start(bf16[128,128]{1,0:T(8,128)(2,1)S(1)} %get-tuple-element.31), channel_id=1, source_target_pairs={{128,0},{256,128},{129,1},{257,129},{130,2},{258,130},{131,3},{259... | collective-permute-start | bytes 98312 | tf_op jit(solution)/shard_map/ppermute | solution.py:508
  80.0 3.5 %all-to-all-start.3 = ((bf16[4,128,512]{2,1,0:T(8,128)(2,1)}), bf16[4,128,512]{2,1,0:T(8,128)(2,1)S(1)}, u32[]{:S(2)}, u32[]{:S(2)}) async-start(bf16[4,128,512]{2,1,0:T(8,128)(2,1)} %sum_cores.1), calls=%async_computation.3 | async-start | bytes 1048576 | tf_op jit(solution)/shard_map/all_to_all | solution.py:509
  83.5 6.6 %collective-permute-done.7.two_ref = bf16[128,128]{1,0:T(8,128)(2,1)S(1)} collective-permute-done((bf16[128,128]{1,0:T(8,128)(2,1)S(1)}, bf16[128,128]{1,0:T(8,128)(2,1)S(1)}, u32[]{:S(2)}, u32[]{:S(2)}) %collective-permute-start.7) | collective-permute-done | bytes 32800 | tf_op jit(solution)/shard_map/ppermute | solution.py:507
  (13 shorter events, 5.4 us)
Async XLA Ops:
  0.6 27.9 %collective-permute-start.5 = (bf16[128,128]{1,0:T(8,128)(2,1)}, bf16[128,128]{1,0:T(8,128)(2,1)S(1)}, u32[]{:S(2)}, u32[]{:S(2)}) collective-permute-start(bf16[128,128]{1,0:T(8,128)(2,1)} %kv_hbm.1), channel_id=1, source_target_pairs={{0,320},{32,352},{64,256},{96,288},{1,321},{33,353},{65,257},{97,2... | collective-permute-start | bytes 98312 | tf_op jit(solution)/shard_map/ppermute | solution.py:463
  15.5 13.1 %collective-permute-start.4 = (bf16[128,128]{1,0:T(8,128)(2,1)}, bf16[128,128]{1,0:T(8,128)(2,1)S(1)}, u32[]{:S(2)}, u32[]{:S(2)}) collective-permute-start(bf16[128,128]{1,0:T(8,128)(2,1)} %kv_hbm.1), channel_id=1, source_target_pairs={{0,128},{128,256},{1,129},{129,257},{2,130},{130,258},{3,131},{131... | collective-permute-start | bytes 98312 | tf_op jit(solution)/shard_map/ppermute | solution.py:464
  18.1 14.8 %collective-permute-start.2 = (bf16[1040,128]{1,0:T(8,128)(2,1)S(1)}, bf16[1040,128]{1,0:T(8,128)(2,1)S(1)}, u32[]{:S(2)}, u32[]{:S(2)}) collective-permute-start(bf16[1040,128]{1,0:T(8,128)(2,1)S(1)} %get-tuple-element.18.own_ref), channel_id=1, source_target_pairs={{0,1},{1,0},{2,3},{3,2},{4,5},{5,4},{6,7},{7,6},{8,9},{9,8},{10,11... | collective-permute-start | bytes 798728 | tf_op jit(solution)/shard_map/ppermute | solution.py:474
  21.5 14.3 %collective-permute-start.1 = (bf16[1040,128]{1,0:T(8,128)(2,1)S(1)}, bf16[1040,128]{1,0:T(8,128)(2,1)S(1)}, u32[]{:S(2)}, u32[]{:S(2)}) collective-permute-start(bf16[1040,128]{1,0:T(8,128)(2,1)S(1)} %get-tuple-element.18.own_ref), channel_id=1, source_target_pairs={{0,16},{16,0},{1,17},{17,1},{2,18},{18,2},{3,19},{19,3},{4,20},{20... | collective-permute-start | bytes 798728 | tf_op jit(solution)/shard_map/ppermute | solution.py:475
  26.2 15.0 %collective-permute-start = (bf16[1040,128]{1,0:T(8,128)(2,1)S(1)}, bf16[1040,128]{1,0:T(8,128)(2,1)S(1)}, u32[]{:S(2)}, u32[]{:S(2)}) collective-permute-start(bf16[1040,128]{1,0:T(8,128)(2,1)S(1)} %get-tuple-element.18.own_ref), channel_id=1, source_target_pairs={{0,17},{1,16},{16,1},{17,0},{2,19},{3,18},{18,3},{19,2},{4,21},{5,... | collective-permute-start | bytes 798728 | tf_op jit(solution)/shard_map/ppermute | solution.py:476
  29.4 16.4 %all-to-all-start = ((bf16[8,208,128]{2,1,0:T(8,128)(2,1)}), bf16[8,208,128]{2,1,0:T(8,128)(2,1)S(1)}, u32[]{:S(2)}, u32[]{:S(2)}) async-start(bf16[8,208,128]{2,1,0:T(8,128)(2,1)} %pack_keys.1), calls=%async_computation | async-start | bytes 851968 | tf_op jit(solution)/shard_map/all_to_all | solution.py:486
  41.2 4.6 %collective-permute-start.3 = (bf16[4,1040,128]{2,1,0:T(8,128)(2,1)S(1)}, bf16[4,1040,128]{2,1,0:T(8,128)(2,1)S(1)}, u32[]{:S(2)}, u32[]{:S(2)}) collective-permute-start(bf16[4,1040,128]{2,1,0:T(8,128)(2,1)S(1)} %gather_sources.1.same_ref), channel_id=1, source_target_pairs={{0,8},{8,0},{1,9},{9,1},{2,10},{10,2},{3,11},{11,3},{4,12},{12,4},... | collective-permute-start | bytes 3194888 | tf_op jit(solution)/shard_map/ppermute | solution.py:480
  49.0 9.4 %all-to-all-start.1 = ((f32[8,2,4,4,128]{4,3,2,1,0:T(4,128)}), f32[8,2,4,4,128]{4,3,2,1,0:T(4,128)S(1)}, u32[]{:S(2)}, u32[]{:S(2)}) async-start(f32[8,2,4,4,128]{4,3,2,1,0:T(4,128)} %get-tuple-element.20), calls=%async_computation.1 | async-start | bytes 262144 | tf_op jit(solution)/shard_map/all_to_all | solution.py:489
  62.3 15.0 %all-to-all-start.2 = ((bf16[8,192,128]{2,1,0:T(8,128)(2,1)}), bf16[8,192,128]{2,1,0:T(8,128)(2,1)S(1)}, u32[]{:S(2)}, u32[]{:S(2)}) async-start(bf16[8,192,128]{2,1,0:T(8,128)(2,1)} %get-tuple-element.23), calls=%async_computation.2 | async-start | bytes 786432 | tf_op jit(solution)/shard_map/all_to_all | solution.py:491
  68.4 3.8 %collective-permute-start.6 = (bf16[4,128,512]{2,1,0:T(8,128)(2,1)S(1)}, bf16[4,128,512]{2,1,0:T(8,128)(2,1)S(1)}, u32[]{:S(2)}, u32[]{:S(2)}) collective-permute-start(bf16[4,128,512]{2,1,0:T(8,128)(2,1)S(1)} %get-tuple-element.26), channel_id=1, source_target_pairs={{0,8},{8,0},{1,9},{9,1},{2,10},{10,2},{3,11},{11,3},{4,12},{12,4},... | collective-permute-start | bytes 1572872 | tf_op jit(solution)/shard_map/ppermute | solution.py:492
  77.4 12.7 %collective-permute-start.7 = (bf16[128,128]{1,0:T(8,128)(2,1)S(1)}, bf16[128,128]{1,0:T(8,128)(2,1)S(1)}, u32[]{:S(2)}, u32[]{:S(2)}) collective-permute-start(bf16[128,128]{1,0:T(8,128)(2,1)S(1)} %get-tuple-element.30), channel_id=1, source_target_pairs={{320,0},{352,32},{256,64},{288,96},{321,1},{353,33},{257,65},{289,... | collective-permute-start | bytes 98312 | tf_op jit(solution)/shard_map/ppermute | solution.py:507
  78.7 11.4 %collective-permute-start.8 = (bf16[128,128]{1,0:T(8,128)(2,1)S(1)}, bf16[128,128]{1,0:T(8,128)(2,1)S(1)}, u32[]{:S(2)}, u32[]{:S(2)}) collective-permute-start(bf16[128,128]{1,0:T(8,128)(2,1)S(1)} %get-tuple-element.31), channel_id=1, source_target_pairs={{128,0},{256,128},{129,1},{257,129},{130,2},{258,130},{131,3},{259... | collective-permute-start | bytes 98312 | tf_op jit(solution)/shard_map/ppermute | solution.py:508
  80.0 11.5 %all-to-all-start.3 = ((bf16[4,128,512]{2,1,0:T(8,128)(2,1)}), bf16[4,128,512]{2,1,0:T(8,128)(2,1)S(1)}, u32[]{:S(2)}, u32[]{:S(2)}) async-start(bf16[4,128,512]{2,1,0:T(8,128)(2,1)} %sum_cores.1), calls=%async_computation.3 | async-start | bytes 1048576 | tf_op jit(solution)/shard_map/all_to_all | solution.py:509

commit v6 on v5

--- a/solution.py
+++ b/solution.py
@@ -196,7 +196,7 @@
 
 
 def row_sums(
-    same_ref, other_ref, kv_ref, out_ref, top_ref, prob_hbm, turn_ref, seg_ref, prob_ref, sems
+    same_ref, other_ref, kv_ref, out_ref, turn_ref, seg_ref
 ):
     place = position()
     core, pair = place[3:]
@@ -217,128 +217,84 @@
                     for s in scores:
                         top = jnp.maximum(top, jnp.max(s, axis=0, keepdims=True))
                     total = jnp.zeros((1, COLS), F32)
-                    for j, s in enumerate(scores):
-                        prob = jnp.exp2(s - top)
-                        total += jnp.sum(prob, axis=0, keepdims=True)
-                        prob_ref[other, x, j] = prob.astype(BF)
+                    for s in scores:
+                        total += jnp.sum(jnp.exp2(s - top), axis=0, keepdims=True)
                     norm = jnp.maximum(top + jnp.log2(total), NEGATIVE)
                     for h in range(HEADS):
                         lanes = slice(h * TOK, (h + 1) * TOK)
-                        top_ref[other, x, h : h + 1, :] = top[:, lanes]
                         piece = jnp.broadcast_to(norm[:, lanes], (8, TOK))
                         out_ref[:, from_core, x, h : h + 1, :] = piece.reshape(8, 1, TOK)
-                    blocks(prob_ref, prob_hbm, n, other, x, sems).start()
 
         sources(0)
         sources(1)
-        for other in range(2):
-            for x in range(4):
-                blocks(prob_ref, prob_hbm, n, other, x, sems).wait()
 
     by_count(place, body)
 
 
-def raw_scores(
-    same_ref, other_ref, kv_ref, prob_hbm, score_hbm, prob_ref, score_ref, in_sems, out_sems
-):
-    def body(n):
-        for x in range(4):
-            for other in range(2):
-                blocks(prob_hbm, prob_ref, n, other, x, in_sems).start()
-
-        def sources(x, _):
-            for other, g_ref in enumerate((same_ref, other_ref)):
-                cot = g_ref[x, COLS : 2 * COLS, :]
-                tail = g_ref[x, 2 * COLS :, :].astype(F32)
-                delta = flat(tail[0:HEADS] + tail[HEADS : 2 * HEADS])
-                blocks(prob_hbm, prob_ref, n, other, x, in_sems).wait()
-                for j in range(n):
-                    dprob = dot(key_block(kv_ref, 1, j), cot, NT)
-                    score_ref[other, x, j] = (
-                        prob_ref[other, x, j].astype(F32) * (dprob - delta)
-                    ).astype(BF)
-                blocks(score_ref, score_hbm, n, other, x, out_sems).start()
-            return 0
-
-        lax.fori_loop(0, 4, sources, 0)
-        for x in range(4):
-            for other in range(2):
-                blocks(score_ref, score_hbm, n, other, x, out_sems).wait()
-
-    by_count(position(), body)
-
-
-def over_sources(left_ref, right_ref, j):
-    total = None
-    for other in range(2):
-        for x in range(4):
-            part = dot(left_ref[other, x, j], right_ref[other, x], NN)
-            total = part if total is None else total + part
-    return total
-
-
 def key_gradients(
-    same_ref, other_ref, norm_ref, top_ref, prob_hbm, score_hbm,
-    dkv_ref, weight_ref, q_ref, g_ref, prob_ref, score_ref, sems,
+    same_ref, other_ref, kv_ref, norm_ref,
+    dkv_ref, score_hbm,
+    turn_ref, seg_ref, log_ref, prob_ref, score_ref, sems,
 ):
     place = position()
-    core = place[3]
-    count = slot_count(place[0])
-
-    def fetch(j, kind):
-        far, near = ((score_hbm, score_ref), (prob_hbm, prob_ref))[kind]
-        return pltpu.make_async_copy(far.at[:, :, j], near.at[:, :, j], sems.at[j, kind])
-
-    for j in range(SLOTS):
-
-        @pl.when(j < count)
-        def _(j=j):
-            fetch(j, 0).start()
-            fetch(j, 1).start()
-
+    core, pair = place[3:]
+    key_segments(kv_ref, pair, turn_ref, seg_ref)
     norms = norm_ref[...]
     top = jnp.max(norms, axis=0)
-    log_norm = top + jnp.log2(jnp.sum(jnp.exp2(norms - top[None]), axis=0))
-    own = jnp.where(core == 0, log_norm[0], log_norm[1])
-    far = jnp.where(core == 0, log_norm[1], log_norm[0])
-    weight_ref[0] = jnp.exp2(top_ref[0] - own)
-    weight_ref[1] = jnp.exp2(top_ref[1] - far)
-
-    for other, source_ref in enumerate((same_ref, other_ref)):
-        columns = jnp.concatenate(
-            [weight_ref[other].reshape(4 * HEADS, TOK), jnp.zeros((TOK - 4 * HEADS, TOK), F32)],
-            axis=0,
-        ).T
-        for x in range(4):
-            for h in range(HEADS):
-                rows = slice(h * TOK, (h + 1) * TOK)
-                below = slice(COLS + h * TOK, COLS + (h + 1) * TOK)
-                i = x * HEADS + h
-                by_row = jnp.broadcast_to(columns[:, i : i + 1], (TOK, HEAD))
-                q = source_ref[x, rows, :].astype(F32) * (by_row * SCALE)
-                q_ref[other, x, rows, :] = q.astype(BF)
-                g_ref[other, x, rows, :] = (
-                    source_ref[x, below, :].astype(F32) * by_row
-                ).astype(BF)
+    log_ref[...] = top + jnp.log2(jnp.sum(jnp.exp2(norms - top[None]), axis=0)) - LOG_SCALE
+
+    def over_sources(left_ref, first, j):
+        total = None
+        for other, right_ref in enumerate((same_ref, other_ref)):
+            for x in range(4):
+                part = dot(left_ref[other, x, j], right_ref[x, first : first + COLS, :], NN)
+                total = part if total is None else total + part
+        return total
 
     def body(n):
+        def sources(hx, _):
+            for other, q_ref in enumerate((same_ref, other_ref)):
+                from_core = (1 - core) if other else core
+                segs = q_ref[2 * hx, 2 * COLS :, :].astype(F32)[8:9]
+                allowed = tiled(allowed_pairs(place, segs, hx, from_core, seg_ref))
+                for p in range(2):
+                    x = 2 * hx + p
+                    q = q_ref[x, :COLS, :]
+                    cot = q_ref[x, COLS : 2 * COLS, :]
+                    tail = q_ref[x, 2 * COLS :, :].astype(F32)
+                    delta = flat(tail[0:HEADS] + tail[HEADS : 2 * HEADS])
+                    norm = flat(log_ref[from_core, x])
+                    for j in range(n):
+                        s = dot(key_block(kv_ref, 0, j), q, NT)
+                        prob = jnp.exp2(s * SCALE2 - norm)
+                        if j == 0:
+                            prob = jnp.where(allowed, prob, 0.0)
+                        dprob = dot(key_block(kv_ref, 1, j), cot, NT)
+                        prob_ref[other, x, j] = prob.astype(BF)
+                        score_ref[other, x, j] = (prob * (dprob - delta)).astype(BF)
+                    blocks(score_ref, score_hbm, n, other, x, sems).start()
+            return 0
+
+        lax.fori_loop(0, 2, sources, 0)
         for s in range(SLOTS):
-            for kind, left_ref, right_ref in ((0, score_ref, q_ref), (1, prob_ref, g_ref)):
+            for kind, left_ref, scale in ((0, score_ref, 1.0), (1, prob_ref, 1.0 / SCALE)):
                 if s < n:
-                    fetch(s, kind).wait()
-                    total = over_sources(left_ref, right_ref, s).astype(BF)
+                    total = (over_sources(left_ref, kind * COLS, s) * scale).astype(BF)
                 else:
                     total = jnp.zeros((KEYS, HEAD), BF)
                 for r in range(GROUP):
                     dkv_ref[2 * r + kind, s * HALF : (s + 1) * HALF, :] = total[
                         r * HALF : (r + 1) * HALF
                     ]
+        for other in range(2):
+            for x in range(4):
+                blocks(score_ref, score_hbm, n, other, x, sems).wait()
 
     by_count(place, body)
 
 
 def query_gradients(
-    kv_ref, score_hbm, weight_ref, same_ref, other_ref, turned_ref, score_ref, sems
+    kv_ref, score_hbm, same_ref, other_ref, turned_ref, score_ref, sems
 ):
 
     def body(n):
@@ -354,7 +310,7 @@
                 dq = dot(turned_ref[0], score_ref[other, x, 0], NN)
                 for j in range(1, n):
                     dq += dot(turned_ref[j], score_ref[other, x, j], NN)
-                dq_ref[x] = (dq * (flat(weight_ref[other, x]) * SCALE)).astype(BF)
+                dq_ref[x] = dq.astype(BF)
             return 0
 
         lax.fori_loop(0, 4, sources, 0)
@@ -391,55 +347,25 @@
 
 
 def local_kernels(same, other, kv, exchange):
-    norms, tops, prob = call(
-        row_sums,
-        "row_sums",
-        (
-            pltpu.VMEM((8, 2, 4, HEADS, TOK), F32),
+    segs = [pltpu.VMEM((TOK, TOK), F32), pltpu.VMEM((KEYS, TOK), F32)]
+    norms = call(
+        row_sums, "row_sums", pltpu.VMEM((8, 2, 4, HEADS, TOK), F32), segs, near=range(3)
+    )(same, other, kv)
+    norms = exchange(norms)
+    dkv, scores = call(
+        key_gradients,
+        "key_gradients",
+        (pltpu.VMEM((2 * GROUP, SLOTS * HALF, HEAD), BF), pltpu.HBM(FULL, BF)),
+        segs
+        + [
             pltpu.VMEM((2, 4, HEADS, TOK), F32),
-            pltpu.HBM(FULL, BF),
-        ),
-        [
-            pltpu.VMEM((TOK, TOK), F32),
-            pltpu.VMEM((KEYS, TOK), F32),
+            pltpu.VMEM(FULL, BF),
             pltpu.VMEM(FULL, BF),
             pltpu.SemaphoreType.DMA((2, 4)),
         ],
-        near=range(3),
-        far_out=(2,),
-    )(same, other, kv)
-    norms = exchange(norms)
-    scores = call(
-        raw_scores,
-        "raw_scores",
-        pltpu.HBM(FULL, BF),
-        [
-            pltpu.VMEM(FULL, BF),
-            pltpu.VMEM(FULL, BF),
-            pltpu.SemaphoreType.DMA((2, 4)),
-            pltpu.SemaphoreType.DMA((2, 4)),
-        ],
-        near=range(3),
-        far=(3,),
-        far_out=(0,),
-    )(same, other, kv, prob)
-    dkv, weights = call(
-        key_gradients,
-        "key_gradients",
-        (
-            pltpu.VMEM((2 * GROUP, SLOTS * HALF, HEAD), BF),
-            pltpu.VMEM((2, 4, HEADS, TOK), F32),
-        ),
-        [
-            pltpu.VMEM((2, 4, COLS, HEAD), BF),
-            pltpu.VMEM((2, 4, COLS, HEAD), BF),
-            pltpu.VMEM(FULL, BF),
-            pltpu.VMEM(FULL, BF),
-            pltpu.SemaphoreType.DMA((SLOTS, 2)),
-        ],
         near=range(4),
-        far=(4, 5),
-    )(same, other, norms, tops, prob, scores)
+        far_out=(1,),
+    )(same, other, kv, norms)
     dq_same, dq_other = call(
         query_gradients,
         "query_gradients",
@@ -449,9 +375,9 @@
             pltpu.VMEM(FULL, BF),
             pltpu.SemaphoreType.DMA((2, 4)),
         ],
-        near=(0, 2),
+        near=(0,),
         far=(1,),
-    )(kv, scores, weights)
+    )(kv, scores)
     return dkv, dq_same, dq_other
 
 

time: 93 us -> 90.9 us (0.977)
  blocking collectives: 0 us -> 8.92 us
  Pallas kernels: 18 us -> 12.8 us
  starting transfers between devices: 46.8 us -> 43.4 us
  waiting for transfers between devices: 26.8 us -> 24.4 us
    all_to_all x0 -> x1, blocking collectives: none -> 8.92 us  [per_device(): lax.all_to_all(norms, PLANE, 0, 0, tiled=True)]
    pallas_call x11 -> x10, Pallas kernels: 18 us -> 12.8 us  [bound(): got = run(*kept)]
    all_to_all x1 -> x0, starting transfers between devices: 3.38 us -> none  [per_device(): lax.all_to_all(norms, PLANE, 0, 0, tiled=True)]
    all_to_all x1 -> x0, waiting for transfers between devices: 2.35 us -> none  [per_device(): lax.all_to_all(norms, PLANE, 0, 0, tiled=True)]
  transfers between devices with their start and end apart: 13 -> 12, of which waited for: 8 -> 7; matrix products, arithmetic and copies ran while one was open for 0% -> 0% of each run, Pallas kernels for 11% -> 7%
where the time goes in v6:
time: 90.9 us; the launch traced here: 90.3 us
  starting transfers between devices  43.4 us (48%)
  waiting for transfers between devices  24.4 us (27%)
  Pallas kernels  12.8 us (14%)
  blocking collectives  8.92 us (10%)
    ppermute x1, starting transfers between devices, per_device(): two = lax.ppermute(stored_key_value, Z_AXES, FAR)  14.8 us
    pallas_call x10, Pallas kernels, bound(): got = run(*kept)  12.8 us
    all_to_all x1, blocking collectives, per_device(): lax.all_to_all(norms, PLANE, 0, 0, tiled=True)  8.92 us
    ppermute x1, waiting for transfers between devices, per_device(): two = lax.ppermute(two, Z_AXES, [(b, a) for a, b in FAR])  6.64 us
    ppermute x1, waiting for transfers between devices, per_device(): both = lax.ppermute(packed, X_AXES, [(i, 3 - i) for i in range(4)])  5.27 us
    ppermute x1, starting transfers between devices, per_device(): far = lax.ppermute(packed, 'xh', swap)  4.64 us
    all_to_all x1, waiting for transfers between devices, per_device(): dkv = lax.all_to_all(dkv, ('zr', 'pair'), 0, 0, tiled=True)  4.25 us
    all_to_all x1, starting transfers between devices, per_device(): dq = lax.all_to_all(dq, X_AXES, 0, 0, tiled=True)  3.48 us
  transfers between devices with their start and end apart: 12, of which 7 were waited for; matrix products, arithmetic and copies ran while one was open for 0% of the time, Pallas kernels for 7%

profile of v6, /device:TPU:24, one launch (start us, length us, event | category | flops | bytes accessed | tf_op | source)
XLA Modules:
  0.0 90.3 jit_solution(6014116786578381480)
XLA Ops:
  0.6 14.8 %collective-permute-start.5 = (bf16[128,128]{1,0:T(8,128)(2,1)}, bf16[128,128]{1,0:T(8,128)(2,1)S(1)}, u32[]{:S(2)}, u32[]{:S(2)}) collective-permute-start(bf16[128,128]{1,0:T(8,128)(2,1)} %kv_hbm.1), channel_id=1, source_target_pairs={{0,320},{32,352},{64,256},{96,288},{1,321},{33,353},{65,257},{97,2... | collective-permute-start | bytes 98312 | tf_op jit(solution)/shard_map/ppermute | solution.py:389
  15.5 1.3 %collective-permute-start.4 = (bf16[128,128]{1,0:T(8,128)(2,1)}, bf16[128,128]{1,0:T(8,128)(2,1)S(1)}, u32[]{:S(2)}, u32[]{:S(2)}) collective-permute-start(bf16[128,128]{1,0:T(8,128)(2,1)} %kv_hbm.1), channel_id=1, source_target_pairs={{0,128},{128,256},{1,129},{129,257},{2,130},{130,258},{3,131},{131... | collective-permute-start | bytes 98312 | tf_op jit(solution)/shard_map/ppermute | solution.py:390
  16.8 1.3 %pack_queries.1 = (bf16[1040,128]{1,0:T(8,128)(2,1)S(1)}, bf16[144,128]{1,0:T(8,128)(2,1)S(1)}) custom-call(bf16[128,512]{1,0:T(8,128)(2,1)} %q_hbm.1, bf16[128,512]{1,0:T(8,128)(2,1)} %g_hbm.1, bf16[128,512]{1,0:T(8,128)(2,1)} %o_hbm.1, s32[1,128]{1,0:T(1,128)} %bitcast.6, s32[1,128]{1,0:T(1,128)} %bitcast.7, bf16[128,128]{1,0:T(8,128)(2,1)} %kv_hbm.1), custom_call_target="tpu_custom_call" | custom-call | tf_op jit(solution)/shard_map/pack_queries/pallas_call | solution.py:67
  18.1 3.4 %collective-permute-start.2 = (bf16[1040,128]{1,0:T(8,128)(2,1)S(1)}, bf16[1040,128]{1,0:T(8,128)(2,1)S(1)}, u32[]{:S(2)}, u32[]{:S(2)}) collective-permute-start(bf16[1040,128]{1,0:T(8,128)(2,1)S(1)} %get-tuple-element.15.own_ref), channel_id=1, source_target_pairs={{0,1},{1,0},{2,3},{3,2},{4,5},{5,4},{6,7},{7,6},{8,9},{9,8},{10,11... | collective-permute-start | bytes 798728 | tf_op jit(solution)/shard_map/ppermute | solution.py:400
  21.5 4.6 %collective-permute-start.1 = (bf16[1040,128]{1,0:T(8,128)(2,1)S(1)}, bf16[1040,128]{1,0:T(8,128)(2,1)S(1)}, u32[]{:S(2)}, u32[]{:S(2)}) collective-permute-start(bf16[1040,128]{1,0:T(8,128)(2,1)S(1)} %get-tuple-element.15.own_ref), channel_id=1, source_target_pairs={{0,16},{16,0},{1,17},{17,1},{2,18},{18,2},{3,19},{19,3},{4,20},{20... | collective-permute-start | bytes 798728 | tf_op jit(solution)/shard_map/ppermute | solution.py:401
  26.2 2.4 %collective-permute-start = (bf16[1040,128]{1,0:T(8,128)(2,1)S(1)}, bf16[1040,128]{1,0:T(8,128)(2,1)S(1)}, u32[]{:S(2)}, u32[]{:S(2)}) collective-permute-start(bf16[1040,128]{1,0:T(8,128)(2,1)S(1)} %get-tuple-element.15.own_ref), channel_id=1, source_target_pairs={{0,17},{1,16},{16,1},{17,0},{2,19},{3,18},{18,3},{19,2},{4,21},{5,... | collective-permute-start | bytes 798728 | tf_op jit(solution)/shard_map/ppermute | solution.py:402
  29.4 3.5 %all-to-all-start = ((bf16[8,208,128]{2,1,0:T(8,128)(2,1)}), bf16[8,208,128]{2,1,0:T(8,128)(2,1)S(1)}, u32[]{:S(2)}, u32[]{:S(2)}) async-start(bf16[8,208,128]{2,1,0:T(8,128)(2,1)} %pack_keys.1), calls=%async_computation | async-start | bytes 851968 | tf_op jit(solution)/shard_map/all_to_all | solution.py:412
  32.9 3.0 %collective-permute-done.1.far_ref = bf16[1040,128]{1,0:T(8,128)(2,1)S(1)} collective-permute-done((bf16[1040,128]{1,0:T(8,128)(2,1)S(1)}, bf16[1040,128]{1,0:T(8,128)(2,1)S(1)}, u32[]{:S(2)}, u32[]{:S(2)}) %collective-permute-start.1) | collective-permute-done | bytes 266272 | tf_op jit(solution)/shard_map/ppermute | solution.py:401
  35.9 5.3 %collective-permute-done.both_ref = bf16[1040,128]{1,0:T(8,128)(2,1)S(1)} collective-permute-done((bf16[1040,128]{1,0:T(8,128)(2,1)S(1)}, bf16[1040,128]{1,0:T(8,128)(2,1)S(1)}, u32[]{:S(2)}, u32[]{:S(2)}) %collective-permute-start) | collective-permute-done | bytes 266272 | tf_op jit(solution)/shard_map/ppermute | solution.py:402
  41.2 1.9 %collective-permute-start.3 = (bf16[4,1040,128]{2,1,0:T(8,128)(2,1)S(1)}, bf16[4,1040,128]{2,1,0:T(8,128)(2,1)S(1)}, u32[]{:S(2)}, u32[]{:S(2)}) collective-permute-start(bf16[4,1040,128]{2,1,0:T(8,128)(2,1)S(1)} %gather_sources.1.same_ref), channel_id=1, source_target_pairs={{0,8},{8,0},{1,9},{9,1},{2,10},{10,2},{3,11},{11,3},{4,12},{12,4},... | collective-permute-start | bytes 3194888 | tf_op jit(solution)/shard_map/ppermute | solution.py:406
  43.2 2.6 %collective-permute-done.3.other_ref = bf16[4,1040,128]{2,1,0:T(8,128)(2,1)S(1)} collective-permute-done((bf16[4,1040,128]{2,1,0:T(8,128)(2,1)S(1)}, bf16[4,1040,128]{2,1,0:T(8,128)(2,1)S(1)}, u32[]{:S(2)}, u32[]{:S(2)}) %collective-permute-start.3) | collective-permute-done | bytes 1064992 | tf_op jit(solution)/shard_map/ppermute | solution.py:406
  45.8 1.6 %row_sums.1 = f32[8,2,4,4,128]{4,3,2,1,0:T(4,128)S(1)} custom-call(bf16[4,1040,128]{2,1,0:T(8,128)(2,1)S(1)} %gather_sources.1.same_ref, bf16[4,1040,128]{2,1,0:T(8,128)(2,1)S(1)} %collective-permute-done.3.other_ref, bf16[4,2,208,128]{3,2,1,0:T(8,128)(2,1)S(1)} %bitcast.3), custom_call_target="tpu_custom_call" | custom-call | tf_op jit(solution)/shard_map/row_sums/pallas_call | solution.py:67
  47.5 8.9 %all_to_all.20.norm_ref = f32[8,2,4,4,128]{4,3,2,1,0:T(4,128)S(1)} all-to-all(f32[8,2,4,4,128]{4,3,2,1,0:T(4,128)S(1)} %row_sums.1), channel_id=1, replica_groups=mesh['zg'=4,'zr'=4,'xh'=2,'core'=2,'tp'=4,'pair'=2] {'xh','core','pair'}, dimensions={0} | all-to-all | bytes 262144 | tf_op jit(solution)/shard_map/all_to_all | solution.py:415
  56.4 3.9 %key_gradients.1 = (bf16[8,192,128]{2,1,0:T(8,128)(2,1)}, bf16[2,4,3,256,512]{4,3,2,1,0:T(8,128)(2,1)}) custom-call(bf16[4,1040,128]{2,1,0:T(8,128)(2,1)S(1)} %gather_sources.1.same_ref, bf16[4,1040,128]{2,1,0:T(8,128)(2,1)S(1)} %collective-permute-done.3.other_ref, bf16[4,2,208,128]{3,2,1,0:T(8,128)(2,1)S(1)} %bitcast.4, ...), custom_call_target="tpu_custom_call" | custom-call | tf_op jit(solution)/shard_map/key_gradients/pallas_call | solution.py:67
  60.3 3.5 %all-to-all-start.2 = ((bf16[8,192,128]{2,1,0:T(8,128)(2,1)}), bf16[8,192,128]{2,1,0:T(8,128)(2,1)S(1)}, u32[]{:S(2)}, u32[]{:S(2)}) async-start(bf16[8,192,128]{2,1,0:T(8,128)(2,1)} %get-tuple-element.17), calls=%async_computation.2 | async-start | bytes 786432 | tf_op jit(solution)/shard_map/all_to_all | solution.py:417
  63.8 2.6 %query_gradients.1 = (bf16[4,128,512]{2,1,0:T(8,128)(2,1)S(1)}, bf16[4,128,512]{2,1,0:T(8,128)(2,1)S(1)}) custom-call(bf16[4,2,208,128]{3,2,1,0:T(8,128)(2,1)S(1)} %bitcast.5, bf16[2,4,3,256,512]{4,3,2,1,0:T(8,128)(2,1)} %get-tuple-element.18.score_hbm), custom_call_target="tpu_custom_call" | custom-call | tf_op jit(solution)/shard_map/query_gradients/pallas_call | solution.py:67
  66.3 1.9 %collective-permute-start.6 = (bf16[4,128,512]{2,1,0:T(8,128)(2,1)S(1)}, bf16[4,128,512]{2,1,0:T(8,128)(2,1)S(1)}, u32[]{:S(2)}, u32[]{:S(2)}) collective-permute-start(bf16[4,128,512]{2,1,0:T(8,128)(2,1)S(1)} %get-tuple-element.20), channel_id=1, source_target_pairs={{0,8},{8,0},{1,9},{9,1},{2,10},{10,2},{3,11},{11,3},{4,12},{12,4},... | collective-permute-start | bytes 1572872 | tf_op jit(solution)/shard_map/ppermute | solution.py:418
  68.3 1.9 %collective-permute-done.6.other_ref = bf16[4,128,512]{2,1,0:T(8,128)(2,1)S(1)} collective-permute-done((bf16[4,128,512]{2,1,0:T(8,128)(2,1)S(1)}, bf16[4,128,512]{2,1,0:T(8,128)(2,1)S(1)}, u32[]{:S(2)}, u32[]{:S(2)}) %collective-permute-start.6) | collective-permute-done | bytes 524320 | tf_op jit(solution)/shard_map/ppermute | solution.py:418
  70.1 0.9 %sum_cores.1 = bf16[4,128,512]{2,1,0:T(8,128)(2,1)} custom-call(bf16[4,128,512]{2,1,0:T(8,128)(2,1)S(1)} %get-tuple-element.19.same_ref, bf16[4,128,512]{2,1,0:T(8,128)(2,1)S(1)} %collective-permute-done.6.other_ref), custom_call_target="tpu_custom_call" | custom-call | tf_op jit(solution)/shard_map/sum_cores/pallas_call | solution.py:67
  71.1 4.2 %all-to-all-done.2.dkv_ref = bf16[8,192,128]{2,1,0:T(8,128)(2,1)S(1)} async-done(((bf16[8,192,128]{2,1,0:T(8,128)(2,1)}), bf16[8,192,128]{2,1,0:T(8,128)(2,1)S(1)}, u32[]{:S(2)}, u32[]{:S(2)}) %all-to-all-start.2) | async-done | bytes 393248 | tf_op jit(solution)/shard_map/all_to_all | solution.py:417
  75.4 1.3 %collective-permute-start.7 = (bf16[128,128]{1,0:T(8,128)(2,1)S(1)}, bf16[128,128]{1,0:T(8,128)(2,1)S(1)}, u32[]{:S(2)}, u32[]{:S(2)}) collective-permute-start(bf16[128,128]{1,0:T(8,128)(2,1)S(1)} %get-tuple-element.24), channel_id=1, source_target_pairs={{320,0},{352,32},{256,64},{288,96},{321,1},{353,33},{257,65},{289,... | collective-permute-start | bytes 98312 | tf_op jit(solution)/shard_map/ppermute | solution.py:433
  76.7 1.3 %collective-permute-start.8 = (bf16[128,128]{1,0:T(8,128)(2,1)S(1)}, bf16[128,128]{1,0:T(8,128)(2,1)S(1)}, u32[]{:S(2)}, u32[]{:S(2)}) collective-permute-start(bf16[128,128]{1,0:T(8,128)(2,1)S(1)} %get-tuple-element.25), channel_id=1, source_target_pairs={{128,0},{256,128},{129,1},{257,129},{130,2},{258,130},{131,3},{259... | collective-permute-start | bytes 98312 | tf_op jit(solution)/shard_map/ppermute | solution.py:434
  78.0 3.5 %all-to-all-start.3 = ((bf16[4,128,512]{2,1,0:T(8,128)(2,1)}), bf16[4,128,512]{2,1,0:T(8,128)(2,1)S(1)}, u32[]{:S(2)}, u32[]{:S(2)}) async-start(bf16[4,128,512]{2,1,0:T(8,128)(2,1)} %sum_cores.1), calls=%async_computation.3 | async-start | bytes 1048576 | tf_op jit(solution)/shard_map/all_to_all | solution.py:435
  81.5 6.6 %collective-permute-done.7.two_ref = bf16[128,128]{1,0:T(8,128)(2,1)S(1)} collective-permute-done((bf16[128,128]{1,0:T(8,128)(2,1)S(1)}, bf16[128,128]{1,0:T(8,128)(2,1)S(1)}, u32[]{:S(2)}, u32[]{:S(2)}) %collective-permute-start.7) | collective-permute-done | bytes 32800 | tf_op jit(solution)/shard_map/ppermute | solution.py:433
  (11 shorter events, 3.2 us)
Async XLA Ops:
  0.6 27.9 %collective-permute-start.5 = (bf16[128,128]{1,0:T(8,128)(2,1)}, bf16[128,128]{1,0:T(8,128)(2,1)S(1)}, u32[]{:S(2)}, u32[]{:S(2)}) collective-permute-start(bf16[128,128]{1,0:T(8,128)(2,1)} %kv_hbm.1), channel_id=1, source_target_pairs={{0,320},{32,352},{64,256},{96,288},{1,321},{33,353},{65,257},{97,2... | collective-permute-start | bytes 98312 | tf_op jit(solution)/shard_map/ppermute | solution.py:389
  15.5 13.1 %collective-permute-start.4 = (bf16[128,128]{1,0:T(8,128)(2,1)}, bf16[128,128]{1,0:T(8,128)(2,1)S(1)}, u32[]{:S(2)}, u32[]{:S(2)}) collective-permute-start(bf16[128,128]{1,0:T(8,128)(2,1)} %kv_hbm.1), channel_id=1, source_target_pairs={{0,128},{128,256},{1,129},{129,257},{2,130},{130,258},{3,131},{131... | collective-permute-start | bytes 98312 | tf_op jit(solution)/shard_map/ppermute | solution.py:390
  18.1 14.8 %collective-permute-start.2 = (bf16[1040,128]{1,0:T(8,128)(2,1)S(1)}, bf16[1040,128]{1,0:T(8,128)(2,1)S(1)}, u32[]{:S(2)}, u32[]{:S(2)}) collective-permute-start(bf16[1040,128]{1,0:T(8,128)(2,1)S(1)} %get-tuple-element.15.own_ref), channel_id=1, source_target_pairs={{0,1},{1,0},{2,3},{3,2},{4,5},{5,4},{6,7},{7,6},{8,9},{9,8},{10,11... | collective-permute-start | bytes 798728 | tf_op jit(solution)/shard_map/ppermute | solution.py:400
  21.5 14.3 %collective-permute-start.1 = (bf16[1040,128]{1,0:T(8,128)(2,1)S(1)}, bf16[1040,128]{1,0:T(8,128)(2,1)S(1)}, u32[]{:S(2)}, u32[]{:S(2)}) collective-permute-start(bf16[1040,128]{1,0:T(8,128)(2,1)S(1)} %get-tuple-element.15.own_ref), channel_id=1, source_target_pairs={{0,16},{16,0},{1,17},{17,1},{2,18},{18,2},{3,19},{19,3},{4,20},{20... | collective-permute-start | bytes 798728 | tf_op jit(solution)/shard_map/ppermute | solution.py:401
  26.2 15.0 %collective-permute-start = (bf16[1040,128]{1,0:T(8,128)(2,1)S(1)}, bf16[1040,128]{1,0:T(8,128)(2,1)S(1)}, u32[]{:S(2)}, u32[]{:S(2)}) collective-permute-start(bf16[1040,128]{1,0:T(8,128)(2,1)S(1)} %get-tuple-element.15.own_ref), channel_id=1, source_target_pairs={{0,17},{1,16},{16,1},{17,0},{2,19},{3,18},{18,3},{19,2},{4,21},{5,... | collective-permute-start | bytes 798728 | tf_op jit(solution)/shard_map/ppermute | solution.py:402
  29.4 16.4 %all-to-all-start = ((bf16[8,208,128]{2,1,0:T(8,128)(2,1)}), bf16[8,208,128]{2,1,0:T(8,128)(2,1)S(1)}, u32[]{:S(2)}, u32[]{:S(2)}) async-start(bf16[8,208,128]{2,1,0:T(8,128)(2,1)} %pack_keys.1), calls=%async_computation | async-start | bytes 851968 | tf_op jit(solution)/shard_map/all_to_all | solution.py:412
  41.2 4.6 %collective-permute-start.3 = (bf16[4,1040,128]{2,1,0:T(8,128)(2,1)S(1)}, bf16[4,1040,128]{2,1,0:T(8,128)(2,1)S(1)}, u32[]{:S(2)}, u32[]{:S(2)}) collective-permute-start(bf16[4,1040,128]{2,1,0:T(8,128)(2,1)S(1)} %gather_sources.1.same_ref), channel_id=1, source_target_pairs={{0,8},{8,0},{1,9},{9,1},{2,10},{10,2},{3,11},{11,3},{4,12},{12,4},... | collective-permute-start | bytes 3194888 | tf_op jit(solution)/shard_map/ppermute | solution.py:406
  60.3 15.0 %all-to-all-start.2 = ((bf16[8,192,128]{2,1,0:T(8,128)(2,1)}), bf16[8,192,128]{2,1,0:T(8,128)(2,1)S(1)}, u32[]{:S(2)}, u32[]{:S(2)}) async-start(bf16[8,192,128]{2,1,0:T(8,128)(2,1)} %get-tuple-element.17), calls=%async_computation.2 | async-start | bytes 786432 | tf_op jit(solution)/shard_map/all_to_all | solution.py:417
  66.3 3.8 %collective-permute-start.6 = (bf16[4,128,512]{2,1,0:T(8,128)(2,1)S(1)}, bf16[4,128,512]{2,1,0:T(8,128)(2,1)S(1)}, u32[]{:S(2)}, u32[]{:S(2)}) collective-permute-start(bf16[4,128,512]{2,1,0:T(8,128)(2,1)S(1)} %get-tuple-element.20), channel_id=1, source_target_pairs={{0,8},{8,0},{1,9},{9,1},{2,10},{10,2},{3,11},{11,3},{4,12},{12,4},... | collective-permute-start | bytes 1572872 | tf_op jit(solution)/shard_map/ppermute | solution.py:418
  75.4 12.7 %collective-permute-start.7 = (bf16[128,128]{1,0:T(8,128)(2,1)S(1)}, bf16[128,128]{1,0:T(8,128)(2,1)S(1)}, u32[]{:S(2)}, u32[]{:S(2)}) collective-permute-start(bf16[128,128]{1,0:T(8,128)(2,1)S(1)} %get-tuple-element.24), channel_id=1, source_target_pairs={{320,0},{352,32},{256,64},{288,96},{321,1},{353,33},{257,65},{289,... | collective-permute-start | bytes 98312 | tf_op jit(solution)/shard_map/ppermute | solution.py:433
  76.7 11.4 %collective-permute-start.8 = (bf16[128,128]{1,0:T(8,128)(2,1)S(1)}, bf16[128,128]{1,0:T(8,128)(2,1)S(1)}, u32[]{:S(2)}, u32[]{:S(2)}) collective-permute-start(bf16[128,128]{1,0:T(8,128)(2,1)S(1)} %get-tuple-element.25), channel_id=1, source_target_pairs={{128,0},{256,128},{129,1},{257,129},{130,2},{258,130},{131,3},{259... | collective-permute-start | bytes 98312 | tf_op jit(solution)/shard_map/ppermute | solution.py:434
  78.0 11.5 %all-to-all-start.3 = ((bf16[4,128,512]{2,1,0:T(8,128)(2,1)}), bf16[4,128,512]{2,1,0:T(8,128)(2,1)S(1)}, u32[]{:S(2)}, u32[]{:S(2)}) async-start(bf16[4,128,512]{2,1,0:T(8,128)(2,1)} %sum_cores.1), calls=%async_computation.3 | async-start | bytes 1048576 | tf_op jit(solution)/shard_map/all_to_all | solution.py:435

commit v7 on v6

--- a/solution.py
+++ b/solution.py
@@ -20,7 +20,7 @@
 HALF = TOK // 2
 KEYS = GROUP * HALF
 Q_ROWS = 2 * COLS + 16
-KV_ROWS = SLOTS * HALF + 16
+KV_ROWS = SLOTS * HALF
 FULL = (2, 4, SLOTS, KEYS, COLS)
 SCALE = 1.0 / math.sqrt(HEAD)
 SCALE2 = SCALE * math.log2(math.e)
@@ -131,8 +131,11 @@
             part = ref[half * HALF : (half + 1) * HALF, :]
             for r in range(GROUP):
                 out_ref[2 * r + half, s * HALF : (s + 1) * HALF, :] = part
-    for i in range(2 * GROUP):
-        out_ref[i, SLOTS * HALF :, :] = tail
+
+    @pl.when(lax.axis_index("zg") == 3)
+    def _():
+        for i in range(2 * GROUP):
+            out_ref[i, HALF : HALF + 16, :] = tail
 
 
 def position():
@@ -156,7 +159,7 @@
 
 def key_segments(kv_ref, pair, turn_ref, seg_ref):
     for r in range(GROUP):
-        row = kv_ref[r, 0, SLOTS * HALF :, :].astype(F32)[0:1]
+        row = kv_ref[r, 0, HALF : HALF + 16, :].astype(F32)[0:1]
         turn_ref[...] = jnp.broadcast_to(row, (TOK, TOK)).T
         seg_ref[r * HALF : (r + 1) * HALF, :] = turn_ref[
             pl.ds(pl.multiple_of(pair * HALF, HALF), HALF), :
@@ -169,7 +172,8 @@
     key_pos = (row // HALF) * 512 + row % HALF + ((2 * xh + core) * TOK + pair * HALF)
     lane = lax.broadcasted_iota(jnp.int32, (KEYS, TOK), 1)
     query_pos = lane + (zr * 512 + (2 * hx + from_core) * TOK)
-    return (key_pos <= query_pos) & (seg_ref[...] == query_seg)
+    one_document = jnp.broadcast_to(zg, (KEYS, TOK)) < 3
+    return (key_pos <= query_pos) & ((seg_ref[...] == query_seg) | one_document)
 
 
 def tiled(mask):
@@ -398,8 +402,9 @@
         far=range(6),
     )(queries, out_grad, attn_out, seg, mask, stored_key_value)
     near = lax.ppermute(packed, "pair", swap)
-    far = lax.ppermute(packed, "xh", swap)
-    both = lax.ppermute(packed, X_AXES, [(i, 3 - i) for i in range(4)])
+    across = [(i, 3 - i) for i in range(4)]
+    both = lax.ppermute(packed, X_AXES, across)
+    far = lax.ppermute(near, X_AXES, across)
     same = call(
         gather_sources, "gather_sources", pltpu.VMEM((4, Q_ROWS, HEAD), BF), near=range(4), cost=LONG
     )(both, far, near, packed)

time: 90.9 us -> 89.6 us (0.986)
  waiting for transfers between devices: 24.4 us -> 22.3 us
    all_to_all x1, waiting for transfers between devices: 0.01 us -> 3.72 us  [per_device(): lax.all_to_all(kv, ('zr', 'pair'), 0, 0, tiled=True)]
    ppermute x2, waiting for transfers between devices: 8.24 us -> 5.02 us  [the longest x1 3.94 us: per_device(): far = lax.ppermute(near, X_AXES, across)]
    ppermute x1, waiting for transfers between devices: 2.65 us -> 0.01 us  [per_device(): other = lax.ppermute(same, 'core', swap)]
  transfers between devices with their start and end apart: 12 -> 12, of which waited for: 7 -> 7; matrix products, arithmetic and copies ran while one was open for 0% -> 0% of each run, Pallas kernels for 7% -> 6%
where the time goes in v7:
time: 89.6 us; the launch traced here: 89 us
  starting transfers between devices  43.4 us (48%)
  waiting for transfers between devices  22.3 us (25%)
  Pallas kernels  12.8 us (14%)
  blocking collectives  9.74 us (11%)
    ppermute x1, starting transfers between devices, per_device(): two = lax.ppermute(stored_key_value, Z_AXES, FAR)  14.8 us
    pallas_call x10, Pallas kernels, bound(): got = run(*kept)  12.8 us
    all_to_all x1, blocking collectives, per_device(): lax.all_to_all(norms, PLANE, 0, 0, tiled=True)  9.74 us
    ppermute x1, waiting for transfers between devices, per_device(): two = lax.ppermute(two, Z_AXES, [(b, a) for a, b in FAR])  6.64 us
    all_to_all x1, waiting for transfers between devices, per_device(): dkv = lax.all_to_all(dkv, ('zr', 'pair'), 0, 0, tiled=True)  4.24 us
    ppermute x1, starting transfers between devices, per_device(): both = lax.ppermute(packed, X_AXES, across)  4 us
    ppermute x1, waiting for transfers between devices, per_device(): far = lax.ppermute(near, X_AXES, across)  3.94 us
    all_to_all x1, waiting for transfers between devices, per_device(): lax.all_to_all(kv, ('zr', 'pair'), 0, 0, tiled=True)  3.72 us
  transfers between devices with their start and end apart: 12, of which 7 were waited for; matrix products, arithmetic and copies ran while one was open for 0% of the time, Pallas kernels for 6%

profile of v7, /device:TPU:24, one launch (start us, length us, event | category | flops | bytes accessed | tf_op | source)
XLA Modules:
  0.0 89.0 jit_solution(16483412430716906934)
XLA Ops:
  0.6 1.3 %pack_queries.1 = (bf16[1040,128]{1,0:T(8,128)(2,1)S(1)}, bf16[144,128]{1,0:T(8,128)(2,1)S(1)}) custom-call(bf16[128,512]{1,0:T(8,128)(2,1)} %q_hbm.1, bf16[128,512]{1,0:T(8,128)(2,1)} %g_hbm.1, bf16[128,512]{1,0:T(8,128)(2,1)} %o_hbm.1, s32[1,128]{1,0:T(1,128)} %bitcast.6, s32[1,128]{1,0:T(1,128)} %bitcast.7, bf16[128,128]{1,0:T(8,128)(2,1)} %kv_hbm.1), custom_call_target="tpu_custom_call" | custom-call | tf_op jit(solution)/shard_map/pack_queries/pallas_call | solution.py:67
  2.0 3.4 %collective-permute-start.1 = (bf16[1040,128]{1,0:T(8,128)(2,1)S(1)}, bf16[1040,128]{1,0:T(8,128)(2,1)S(1)}, u32[]{:S(2)}, u32[]{:S(2)}) collective-permute-start(bf16[1040,128]{1,0:T(8,128)(2,1)S(1)} %get-tuple-element.15.own_ref), channel_id=1, source_target_pairs={{0,1},{1,0},{2,3},{3,2},{4,5},{5,4},{6,7},{7,6},{8,9},{9,8},{10,11... | collective-permute-start | bytes 798728 | tf_op jit(solution)/shard_map/ppermute | solution.py:404
  5.4 14.8 %collective-permute-start.5 = (bf16[128,128]{1,0:T(8,128)(2,1)}, bf16[128,128]{1,0:T(8,128)(2,1)S(1)}, u32[]{:S(2)}, u32[]{:S(2)}) collective-permute-start(bf16[128,128]{1,0:T(8,128)(2,1)} %kv_hbm.1), channel_id=1, source_target_pairs={{0,320},{32,352},{64,256},{96,288},{1,321},{33,353},{65,257},{97,2... | collective-permute-start | bytes 98312 | tf_op jit(solution)/shard_map/ppermute | solution.py:393
  20.2 1.3 %collective-permute-start.4 = (bf16[128,128]{1,0:T(8,128)(2,1)}, bf16[128,128]{1,0:T(8,128)(2,1)S(1)}, u32[]{:S(2)}, u32[]{:S(2)}) collective-permute-start(bf16[128,128]{1,0:T(8,128)(2,1)} %kv_hbm.1), channel_id=1, source_target_pairs={{0,128},{128,256},{1,129},{129,257},{2,130},{130,258},{3,131},{131... | collective-permute-start | bytes 98312 | tf_op jit(solution)/shard_map/ppermute | solution.py:394
  21.5 4.0 %collective-permute-start = (bf16[1040,128]{1,0:T(8,128)(2,1)S(1)}, bf16[1040,128]{1,0:T(8,128)(2,1)S(1)}, u32[]{:S(2)}, u32[]{:S(2)}) collective-permute-start(bf16[1040,128]{1,0:T(8,128)(2,1)S(1)} %get-tuple-element.15.own_ref), channel_id=1, source_target_pairs={{0,17},{1,16},{16,1},{17,0},{2,19},{3,18},{18,3},{19,2},{4,21},{5,... | collective-permute-start | bytes 798728 | tf_op jit(solution)/shard_map/ppermute | solution.py:406
  25.6 3.0 %collective-permute-start.2 = (bf16[1040,128]{1,0:T(8,128)(2,1)S(1)}, bf16[1040,128]{1,0:T(8,128)(2,1)S(1)}, u32[]{:S(2)}, u32[]{:S(2)}) collective-permute-start(bf16[1040,128]{1,0:T(8,128)(2,1)S(1)} %collective-permute-done.1.near_ref), channel_id=1, source_target_pairs={{0,17},{1,16},{16,1},{17,0},{2,19},{3,18},{18,3},{19,2},{4,21},{5,... | collective-permute-start | bytes 798728 | tf_op jit(solution)/shard_map/ppermute | solution.py:407
  29.4 3.5 %all-to-all-start = ((bf16[8,192,128]{2,1,0:T(8,128)(2,1)}), bf16[8,192,128]{2,1,0:T(8,128)(2,1)S(1)}, u32[]{:S(2)}, u32[]{:S(2)}) async-start(bf16[8,192,128]{2,1,0:T(8,128)(2,1)} %pack_keys.1), calls=%async_computation | async-start | bytes 786432 | tf_op jit(solution)/shard_map/all_to_all | solution.py:417
  32.9 1.1 %collective-permute-done.both_ref = bf16[1040,128]{1,0:T(8,128)(2,1)S(1)} collective-permute-done((bf16[1040,128]{1,0:T(8,128)(2,1)S(1)}, bf16[1040,128]{1,0:T(8,128)(2,1)S(1)}, u32[]{:S(2)}, u32[]{:S(2)}) %collective-permute-start) | collective-permute-done | bytes 266272 | tf_op jit(solution)/shard_map/ppermute | solution.py:406
  34.0 3.9 %collective-permute-done.2.far_ref = bf16[1040,128]{1,0:T(8,128)(2,1)S(1)} collective-permute-done((bf16[1040,128]{1,0:T(8,128)(2,1)S(1)}, bf16[1040,128]{1,0:T(8,128)(2,1)S(1)}, u32[]{:S(2)}, u32[]{:S(2)}) %collective-permute-start.2) | collective-permute-done | bytes 266272 | tf_op jit(solution)/shard_map/ppermute | solution.py:407
  38.0 1.9 %collective-permute-start.3 = (bf16[4,1040,128]{2,1,0:T(8,128)(2,1)S(1)}, bf16[4,1040,128]{2,1,0:T(8,128)(2,1)S(1)}, u32[]{:S(2)}, u32[]{:S(2)}) collective-permute-start(bf16[4,1040,128]{2,1,0:T(8,128)(2,1)S(1)} %gather_sources.1.same_ref), channel_id=1, source_target_pairs={{0,8},{8,0},{1,9},{9,1},{2,10},{10,2},{3,11},{11,3},{4,12},{12,4},... | collective-permute-start | bytes 3194888 | tf_op jit(solution)/shard_map/ppermute | solution.py:411
  39.9 3.7 %all-to-all-done = bf16[8,192,128]{2,1,0:T(8,128)(2,1)S(1)} async-done(((bf16[8,192,128]{2,1,0:T(8,128)(2,1)}), bf16[8,192,128]{2,1,0:T(8,128)(2,1)S(1)}, u32[]{:S(2)}, u32[]{:S(2)}) %all-to-all-start) | async-done | bytes 393248 | tf_op jit(solution)/shard_map/all_to_all | solution.py:417
  43.7 1.7 %row_sums.1 = f32[8,2,4,4,128]{4,3,2,1,0:T(4,128)S(1)} custom-call(bf16[4,1040,128]{2,1,0:T(8,128)(2,1)S(1)} %gather_sources.1.same_ref, bf16[4,1040,128]{2,1,0:T(8,128)(2,1)S(1)} %collective-permute-done.3.other_ref, bf16[4,2,192,128]{3,2,1,0:T(8,128)(2,1)S(1)} %bitcast.3), custom_call_target="tpu_custom_call" | custom-call | tf_op jit(solution)/shard_map/row_sums/pallas_call | solution.py:67
  45.3 9.7 %all_to_all.20.norm_ref = f32[8,2,4,4,128]{4,3,2,1,0:T(4,128)S(1)} all-to-all(f32[8,2,4,4,128]{4,3,2,1,0:T(4,128)S(1)} %row_sums.1), channel_id=1, replica_groups=mesh['zg'=4,'zr'=4,'xh'=2,'core'=2,'tp'=4,'pair'=2] {'xh','core','pair'}, dimensions={0} | all-to-all | bytes 262144 | tf_op jit(solution)/shard_map/all_to_all | solution.py:420
  55.1 3.9 %key_gradients.1 = (bf16[8,192,128]{2,1,0:T(8,128)(2,1)}, bf16[2,4,3,256,512]{4,3,2,1,0:T(8,128)(2,1)}) custom-call(bf16[4,1040,128]{2,1,0:T(8,128)(2,1)S(1)} %gather_sources.1.same_ref, bf16[4,1040,128]{2,1,0:T(8,128)(2,1)S(1)} %collective-permute-done.3.other_ref, bf16[4,2,192,128]{3,2,1,0:T(8,128)(2,1)S(1)} %bitcast.4, ...), custom_call_target="tpu_custom_call" | custom-call | tf_op jit(solution)/shard_map/key_gradients/pallas_call | solution.py:67
  59.0 3.5 %all-to-all-start.2 = ((bf16[8,192,128]{2,1,0:T(8,128)(2,1)}), bf16[8,192,128]{2,1,0:T(8,128)(2,1)S(1)}, u32[]{:S(2)}, u32[]{:S(2)}) async-start(bf16[8,192,128]{2,1,0:T(8,128)(2,1)} %get-tuple-element.17), calls=%async_computation.2 | async-start | bytes 786432 | tf_op jit(solution)/shard_map/all_to_all | solution.py:422
  62.5 2.6 %query_gradients.1 = (bf16[4,128,512]{2,1,0:T(8,128)(2,1)S(1)}, bf16[4,128,512]{2,1,0:T(8,128)(2,1)S(1)}) custom-call(bf16[4,2,192,128]{3,2,1,0:T(8,128)(2,1)S(1)} %bitcast.5, bf16[2,4,3,256,512]{4,3,2,1,0:T(8,128)(2,1)} %get-tuple-element.18.score_hbm), custom_call_target="tpu_custom_call" | custom-call | tf_op jit(solution)/shard_map/query_gradients/pallas_call | solution.py:67
  65.0 1.9 %collective-permute-start.6 = (bf16[4,128,512]{2,1,0:T(8,128)(2,1)S(1)}, bf16[4,128,512]{2,1,0:T(8,128)(2,1)S(1)}, u32[]{:S(2)}, u32[]{:S(2)}) collective-permute-start(bf16[4,128,512]{2,1,0:T(8,128)(2,1)S(1)} %get-tuple-element.20), channel_id=1, source_target_pairs={{0,8},{8,0},{1,9},{9,1},{2,10},{10,2},{3,11},{11,3},{4,12},{12,4},... | collective-permute-start | bytes 1572872 | tf_op jit(solution)/shard_map/ppermute | solution.py:423
  67.0 1.9 %collective-permute-done.6.other_ref = bf16[4,128,512]{2,1,0:T(8,128)(2,1)S(1)} collective-permute-done((bf16[4,128,512]{2,1,0:T(8,128)(2,1)S(1)}, bf16[4,128,512]{2,1,0:T(8,128)(2,1)S(1)}, u32[]{:S(2)}, u32[]{:S(2)}) %collective-permute-start.6) | collective-permute-done | bytes 524320 | tf_op jit(solution)/shard_map/ppermute | solution.py:423
  68.8 0.9 %sum_cores.1 = bf16[4,128,512]{2,1,0:T(8,128)(2,1)} custom-call(bf16[4,128,512]{2,1,0:T(8,128)(2,1)S(1)} %get-tuple-element.19.same_ref, bf16[4,128,512]{2,1,0:T(8,128)(2,1)S(1)} %collective-permute-done.6.other_ref), custom_call_target="tpu_custom_call" | custom-call | tf_op jit(solution)/shard_map/sum_cores/pallas_call | solution.py:67
  69.8 4.2 %all-to-all-done.2.dkv_ref = bf16[8,192,128]{2,1,0:T(8,128)(2,1)S(1)} async-done(((bf16[8,192,128]{2,1,0:T(8,128)(2,1)}), bf16[8,192,128]{2,1,0:T(8,128)(2,1)S(1)}, u32[]{:S(2)}, u32[]{:S(2)}) %all-to-all-start.2) | async-done | bytes 393248 | tf_op jit(solution)/shard_map/all_to_all | solution.py:422
  74.1 1.3 %collective-permute-start.7 = (bf16[128,128]{1,0:T(8,128)(2,1)S(1)}, bf16[128,128]{1,0:T(8,128)(2,1)S(1)}, u32[]{:S(2)}, u32[]{:S(2)}) collective-permute-start(bf16[128,128]{1,0:T(8,128)(2,1)S(1)} %get-tuple-element.24), channel_id=1, source_target_pairs={{320,0},{352,32},{256,64},{288,96},{321,1},{353,33},{257,65},{289,... | collective-permute-start | bytes 98312 | tf_op jit(solution)/shard_map/ppermute | solution.py:438
  75.4 1.3 %collective-permute-start.8 = (bf16[128,128]{1,0:T(8,128)(2,1)S(1)}, bf16[128,128]{1,0:T(8,128)(2,1)S(1)}, u32[]{:S(2)}, u32[]{:S(2)}) collective-permute-start(bf16[128,128]{1,0:T(8,128)(2,1)S(1)} %get-tuple-element.25), channel_id=1, source_target_pairs={{128,0},{256,128},{129,1},{257,129},{130,2},{258,130},{131,3},{259... | collective-permute-start | bytes 98312 | tf_op jit(solution)/shard_map/ppermute | solution.py:439
  76.7 3.5 %all-to-all-start.3 = ((bf16[4,128,512]{2,1,0:T(8,128)(2,1)}), bf16[4,128,512]{2,1,0:T(8,128)(2,1)S(1)}, u32[]{:S(2)}, u32[]{:S(2)}) async-start(bf16[4,128,512]{2,1,0:T(8,128)(2,1)} %sum_cores.1), calls=%async_computation.3 | async-start | bytes 1048576 | tf_op jit(solution)/shard_map/all_to_all | solution.py:440
  80.1 6.6 %collective-permute-done.7.two_ref = bf16[128,128]{1,0:T(8,128)(2,1)S(1)} collective-permute-done((bf16[128,128]{1,0:T(8,128)(2,1)S(1)}, bf16[128,128]{1,0:T(8,128)(2,1)S(1)}, u32[]{:S(2)}, u32[]{:S(2)}) %collective-permute-start.7) | collective-permute-done | bytes 32800 | tf_op jit(solution)/shard_map/ppermute | solution.py:438
  (11 shorter events, 3.2 us)
Async XLA Ops:
  2.0 23.6 %collective-permute-start.1 = (bf16[1040,128]{1,0:T(8,128)(2,1)S(1)}, bf16[1040,128]{1,0:T(8,128)(2,1)S(1)}, u32[]{:S(2)}, u32[]{:S(2)}) collective-permute-start(bf16[1040,128]{1,0:T(8,128)(2,1)S(1)} %get-tuple-element.15.own_ref), channel_id=1, source_target_pairs={{0,1},{1,0},{2,3},{3,2},{4,5},{5,4},{6,7},{7,6},{8,9},{9,8},{10,11... | collective-permute-start | bytes 798728 | tf_op jit(solution)/shard_map/ppermute | solution.py:404
  5.4 23.2 %collective-permute-start.5 = (bf16[128,128]{1,0:T(8,128)(2,1)}, bf16[128,128]{1,0:T(8,128)(2,1)S(1)}, u32[]{:S(2)}, u32[]{:S(2)}) collective-permute-start(bf16[128,128]{1,0:T(8,128)(2,1)} %kv_hbm.1), channel_id=1, source_target_pairs={{0,320},{32,352},{64,256},{96,288},{1,321},{33,353},{65,257},{97,2... | collective-permute-start | bytes 98312 | tf_op jit(solution)/shard_map/ppermute | solution.py:393
  20.2 8.4 %collective-permute-start.4 = (bf16[128,128]{1,0:T(8,128)(2,1)}, bf16[128,128]{1,0:T(8,128)(2,1)S(1)}, u32[]{:S(2)}, u32[]{:S(2)}) collective-permute-start(bf16[128,128]{1,0:T(8,128)(2,1)} %kv_hbm.1), channel_id=1, source_target_pairs={{0,128},{128,256},{1,129},{129,257},{2,130},{130,258},{3,131},{131... | collective-permute-start | bytes 98312 | tf_op jit(solution)/shard_map/ppermute | solution.py:394
  21.5 12.4 %collective-permute-start = (bf16[1040,128]{1,0:T(8,128)(2,1)S(1)}, bf16[1040,128]{1,0:T(8,128)(2,1)S(1)}, u32[]{:S(2)}, u32[]{:S(2)}) collective-permute-start(bf16[1040,128]{1,0:T(8,128)(2,1)S(1)} %get-tuple-element.15.own_ref), channel_id=1, source_target_pairs={{0,17},{1,16},{16,1},{17,0},{2,19},{3,18},{18,3},{19,2},{4,21},{5,... | collective-permute-start | bytes 798728 | tf_op jit(solution)/shard_map/ppermute | solution.py:406
  25.6 12.4 %collective-permute-start.2 = (bf16[1040,128]{1,0:T(8,128)(2,1)S(1)}, bf16[1040,128]{1,0:T(8,128)(2,1)S(1)}, u32[]{:S(2)}, u32[]{:S(2)}) collective-permute-start(bf16[1040,128]{1,0:T(8,128)(2,1)S(1)} %collective-permute-done.1.near_ref), channel_id=1, source_target_pairs={{0,17},{1,16},{16,1},{17,0},{2,19},{3,18},{18,3},{19,2},{4,21},{5,... | collective-permute-start | bytes 798728 | tf_op jit(solution)/shard_map/ppermute | solution.py:407
  29.4 14.2 %all-to-all-start = ((bf16[8,192,128]{2,1,0:T(8,128)(2,1)}), bf16[8,192,128]{2,1,0:T(8,128)(2,1)S(1)}, u32[]{:S(2)}, u32[]{:S(2)}) async-start(bf16[8,192,128]{2,1,0:T(8,128)(2,1)} %pack_keys.1), calls=%async_computation | async-start | bytes 786432 | tf_op jit(solution)/shard_map/all_to_all | solution.py:417
  38.0 5.7 %collective-permute-start.3 = (bf16[4,1040,128]{2,1,0:T(8,128)(2,1)S(1)}, bf16[4,1040,128]{2,1,0:T(8,128)(2,1)S(1)}, u32[]{:S(2)}, u32[]{:S(2)}) collective-permute-start(bf16[4,1040,128]{2,1,0:T(8,128)(2,1)S(1)} %gather_sources.1.same_ref), channel_id=1, source_target_pairs={{0,8},{8,0},{1,9},{9,1},{2,10},{10,2},{3,11},{11,3},{4,12},{12,4},... | collective-permute-start | bytes 3194888 | tf_op jit(solution)/shard_map/ppermute | solution.py:411
  59.0 15.0 %all-to-all-start.2 = ((bf16[8,192,128]{2,1,0:T(8,128)(2,1)}), bf16[8,192,128]{2,1,0:T(8,128)(2,1)S(1)}, u32[]{:S(2)}, u32[]{:S(2)}) async-start(bf16[8,192,128]{2,1,0:T(8,128)(2,1)} %get-tuple-element.17), calls=%async_computation.2 | async-start | bytes 786432 | tf_op jit(solution)/shard_map/all_to_all | solution.py:422
  65.0 3.8 %collective-permute-start.6 = (bf16[4,128,512]{2,1,0:T(8,128)(2,1)S(1)}, bf16[4,128,512]{2,1,0:T(8,128)(2,1)S(1)}, u32[]{:S(2)}, u32[]{:S(2)}) collective-permute-start(bf16[4,128,512]{2,1,0:T(8,128)(2,1)S(1)} %get-tuple-element.20), channel_id=1, source_target_pairs={{0,8},{8,0},{1,9},{9,1},{2,10},{10,2},{3,11},{11,3},{4,12},{12,4},... | collective-permute-start | bytes 1572872 | tf_op jit(solution)/shard_map/ppermute | solution.py:423
  74.1 12.7 %collective-permute-start.7 = (bf16[128,128]{1,0:T(8,128)(2,1)S(1)}, bf16[128,128]{1,0:T(8,128)(2,1)S(1)}, u32[]{:S(2)}, u32[]{:S(2)}) collective-permute-start(bf16[128,128]{1,0:T(8,128)(2,1)S(1)} %get-tuple-element.24), channel_id=1, source_target_pairs={{320,0},{352,32},{256,64},{288,96},{321,1},{353,33},{257,65},{289,... | collective-permute-start | bytes 98312 | tf_op jit(solution)/shard_map/ppermute | solution.py:438
  75.4 11.4 %collective-permute-start.8 = (bf16[128,128]{1,0:T(8,128)(2,1)S(1)}, bf16[128,128]{1,0:T(8,128)(2,1)S(1)}, u32[]{:S(2)}, u32[]{:S(2)}) collective-permute-start(bf16[128,128]{1,0:T(8,128)(2,1)S(1)} %get-tuple-element.25), channel_id=1, source_target_pairs={{128,0},{256,128},{129,1},{257,129},{130,2},{258,130},{131,3},{259... | collective-permute-start | bytes 98312 | tf_op jit(solution)/shard_map/ppermute | solution.py:439
  76.7 11.5 %all-to-all-start.3 = ((bf16[4,128,512]{2,1,0:T(8,128)(2,1)}), bf16[4,128,512]{2,1,0:T(8,128)(2,1)S(1)}, u32[]{:S(2)}, u32[]{:S(2)}) async-start(bf16[4,128,512]{2,1,0:T(8,128)(2,1)} %sum_cores.1), calls=%async_computation.3 | async-start | bytes 1048576 | tf_op jit(solution)/shard_map/all_to_all | solution.py:440

commit v8 on v7

--- a/solution.py
+++ b/solution.py
@@ -256,7 +256,7 @@
         return total
 
     def body(n):
-        def sources(hx, _):
+        def sources(hx):
             for other, q_ref in enumerate((same_ref, other_ref)):
                 from_core = (1 - core) if other else core
                 segs = q_ref[2 * hx, 2 * COLS :, :].astype(F32)[8:9]
@@ -277,9 +277,9 @@
                         prob_ref[other, x, j] = prob.astype(BF)
                         score_ref[other, x, j] = (prob * (dprob - delta)).astype(BF)
                     blocks(score_ref, score_hbm, n, other, x, sems).start()
-            return 0
-
-        lax.fori_loop(0, 2, sources, 0)
+
+        sources(0)
+        sources(1)
         for s in range(SLOTS):
             for kind, left_ref, scale in ((0, score_ref, 1.0), (1, prob_ref, 1.0 / SCALE)):
                 if s < n:

time: 89.6 us -> 89.3 us (level)
  no operation moved by 1% of the time
where the time goes in v8:
time: 89.3 us; the launch traced here: 88.7 us
  starting transfers between devices  43.4 us (49%)
  waiting for transfers between devices  22.3 us (25%)
  Pallas kernels  12.5 us (14%)
  blocking collectives  9.74 us (11%)
    ppermute x1, starting transfers between devices, per_device(): two = lax.ppermute(stored_key_value, Z_AXES, FAR)  14.8 us
    pallas_call x10, Pallas kernels, bound(): got = run(*kept)  12.5 us
    all_to_all x1, blocking collectives, per_device(): lax.all_to_all(norms, PLANE, 0, 0, tiled=True)  9.74 us
    ppermute x1, waiting for transfers between devices, per_device(): two = lax.ppermute(two, Z_AXES, [(b, a) for a, b in FAR])  6.64 us
    all_to_all x1, waiting for transfers between devices, per_device(): dkv = lax.all_to_all(dkv, ('zr', 'pair'), 0, 0, tiled=True)  4.25 us
    ppermute x1, starting transfers between devices, per_device(): both = lax.ppermute(packed, X_AXES, across)  4 us
    ppermute x1, waiting for transfers between devices, per_device(): far = lax.ppermute(near, X_AXES, across)  3.94 us
    all_to_all x1, waiting for transfers between devices, per_device(): lax.all_to_all(kv, ('zr', 'pair'), 0, 0, tiled=True)  3.72 us
  transfers between devices with their start and end apart: 12, of which 7 were waited for; matrix products, arithmetic and copies ran while one was open for 0% of the time, Pallas kernels for 6%

profile of v8, /device:TPU:24, one launch (start us, length us, event | category | flops | bytes accessed | tf_op | source)
XLA Modules:
  0.0 88.7 jit_solution(5825764773107721776)
XLA Ops:
  0.6 1.3 %pack_queries.1 = (bf16[1040,128]{1,0:T(8,128)(2,1)S(1)}, bf16[144,128]{1,0:T(8,128)(2,1)S(1)}) custom-call(bf16[128,512]{1,0:T(8,128)(2,1)} %q_hbm.1, bf16[128,512]{1,0:T(8,128)(2,1)} %g_hbm.1, bf16[128,512]{1,0:T(8,128)(2,1)} %o_hbm.1, s32[1,128]{1,0:T(1,128)} %bitcast.6, s32[1,128]{1,0:T(1,128)} %bitcast.7, bf16[128,128]{1,0:T(8,128)(2,1)} %kv_hbm.1), custom_call_target="tpu_custom_call" | custom-call | tf_op jit(solution)/shard_map/pack_queries/pallas_call | solution.py:67
  2.0 3.4 %collective-permute-start.1 = (bf16[1040,128]{1,0:T(8,128)(2,1)S(1)}, bf16[1040,128]{1,0:T(8,128)(2,1)S(1)}, u32[]{:S(2)}, u32[]{:S(2)}) collective-permute-start(bf16[1040,128]{1,0:T(8,128)(2,1)S(1)} %get-tuple-element.15.own_ref), channel_id=1, source_target_pairs={{0,1},{1,0},{2,3},{3,2},{4,5},{5,4},{6,7},{7,6},{8,9},{9,8},{10,11... | collective-permute-start | bytes 798728 | tf_op jit(solution)/shard_map/ppermute | solution.py:404
  5.4 14.8 %collective-permute-start.5 = (bf16[128,128]{1,0:T(8,128)(2,1)}, bf16[128,128]{1,0:T(8,128)(2,1)S(1)}, u32[]{:S(2)}, u32[]{:S(2)}) collective-permute-start(bf16[128,128]{1,0:T(8,128)(2,1)} %kv_hbm.1), channel_id=1, source_target_pairs={{0,320},{32,352},{64,256},{96,288},{1,321},{33,353},{65,257},{97,2... | collective-permute-start | bytes 98312 | tf_op jit(solution)/shard_map/ppermute | solution.py:393
  20.2 1.3 %collective-permute-start.4 = (bf16[128,128]{1,0:T(8,128)(2,1)}, bf16[128,128]{1,0:T(8,128)(2,1)S(1)}, u32[]{:S(2)}, u32[]{:S(2)}) collective-permute-start(bf16[128,128]{1,0:T(8,128)(2,1)} %kv_hbm.1), channel_id=1, source_target_pairs={{0,128},{128,256},{1,129},{129,257},{2,130},{130,258},{3,131},{131... | collective-permute-start | bytes 98312 | tf_op jit(solution)/shard_map/ppermute | solution.py:394
  21.5 4.0 %collective-permute-start = (bf16[1040,128]{1,0:T(8,128)(2,1)S(1)}, bf16[1040,128]{1,0:T(8,128)(2,1)S(1)}, u32[]{:S(2)}, u32[]{:S(2)}) collective-permute-start(bf16[1040,128]{1,0:T(8,128)(2,1)S(1)} %get-tuple-element.15.own_ref), channel_id=1, source_target_pairs={{0,17},{1,16},{16,1},{17,0},{2,19},{3,18},{18,3},{19,2},{4,21},{5,... | collective-permute-start | bytes 798728 | tf_op jit(solution)/shard_map/ppermute | solution.py:406
  25.6 3.0 %collective-permute-start.2 = (bf16[1040,128]{1,0:T(8,128)(2,1)S(1)}, bf16[1040,128]{1,0:T(8,128)(2,1)S(1)}, u32[]{:S(2)}, u32[]{:S(2)}) collective-permute-start(bf16[1040,128]{1,0:T(8,128)(2,1)S(1)} %collective-permute-done.1.near_ref), channel_id=1, source_target_pairs={{0,17},{1,16},{16,1},{17,0},{2,19},{3,18},{18,3},{19,2},{4,21},{5,... | collective-permute-start | bytes 798728 | tf_op jit(solution)/shard_map/ppermute | solution.py:407
  29.4 3.5 %all-to-all-start = ((bf16[8,192,128]{2,1,0:T(8,128)(2,1)}), bf16[8,192,128]{2,1,0:T(8,128)(2,1)S(1)}, u32[]{:S(2)}, u32[]{:S(2)}) async-start(bf16[8,192,128]{2,1,0:T(8,128)(2,1)} %pack_keys.1), calls=%async_computation | async-start | bytes 786432 | tf_op jit(solution)/shard_map/all_to_all | solution.py:417
  32.9 1.1 %collective-permute-done.both_ref = bf16[1040,128]{1,0:T(8,128)(2,1)S(1)} collective-permute-done((bf16[1040,128]{1,0:T(8,128)(2,1)S(1)}, bf16[1040,128]{1,0:T(8,128)(2,1)S(1)}, u32[]{:S(2)}, u32[]{:S(2)}) %collective-permute-start) | collective-permute-done | bytes 266272 | tf_op jit(solution)/shard_map/ppermute | solution.py:406
  34.0 3.9 %collective-permute-done.2.far_ref = bf16[1040,128]{1,0:T(8,128)(2,1)S(1)} collective-permute-done((bf16[1040,128]{1,0:T(8,128)(2,1)S(1)}, bf16[1040,128]{1,0:T(8,128)(2,1)S(1)}, u32[]{:S(2)}, u32[]{:S(2)}) %collective-permute-start.2) | collective-permute-done | bytes 266272 | tf_op jit(solution)/shard_map/ppermute | solution.py:407
  38.0 1.9 %collective-permute-start.3 = (bf16[4,1040,128]{2,1,0:T(8,128)(2,1)S(1)}, bf16[4,1040,128]{2,1,0:T(8,128)(2,1)S(1)}, u32[]{:S(2)}, u32[]{:S(2)}) collective-permute-start(bf16[4,1040,128]{2,1,0:T(8,128)(2,1)S(1)} %gather_sources.1.same_ref), channel_id=1, source_target_pairs={{0,8},{8,0},{1,9},{9,1},{2,10},{10,2},{3,11},{11,3},{4,12},{12,4},... | collective-permute-start | bytes 3194888 | tf_op jit(solution)/shard_map/ppermute | solution.py:411
  39.9 3.7 %all-to-all-done = bf16[8,192,128]{2,1,0:T(8,128)(2,1)S(1)} async-done(((bf16[8,192,128]{2,1,0:T(8,128)(2,1)}), bf16[8,192,128]{2,1,0:T(8,128)(2,1)S(1)}, u32[]{:S(2)}, u32[]{:S(2)}) %all-to-all-start) | async-done | bytes 393248 | tf_op jit(solution)/shard_map/all_to_all | solution.py:417
  43.7 1.7 %row_sums.1 = f32[8,2,4,4,128]{4,3,2,1,0:T(4,128)S(1)} custom-call(bf16[4,1040,128]{2,1,0:T(8,128)(2,1)S(1)} %gather_sources.1.same_ref, bf16[4,1040,128]{2,1,0:T(8,128)(2,1)S(1)} %collective-permute-done.3.other_ref, bf16[4,2,192,128]{3,2,1,0:T(8,128)(2,1)S(1)} %bitcast.3), custom_call_target="tpu_custom_call" | custom-call | tf_op jit(solution)/shard_map/row_sums/pallas_call | solution.py:67
  45.3 9.7 %all_to_all.20.norm_ref = f32[8,2,4,4,128]{4,3,2,1,0:T(4,128)S(1)} all-to-all(f32[8,2,4,4,128]{4,3,2,1,0:T(4,128)S(1)} %row_sums.1), channel_id=1, replica_groups=mesh['zg'=4,'zr'=4,'xh'=2,'core'=2,'tp'=4,'pair'=2] {'xh','core','pair'}, dimensions={0} | all-to-all | bytes 262144 | tf_op jit(solution)/shard_map/all_to_all | solution.py:420
  55.1 3.6 %key_gradients.1 = (bf16[8,192,128]{2,1,0:T(8,128)(2,1)}, bf16[2,4,3,256,512]{4,3,2,1,0:T(8,128)(2,1)}) custom-call(bf16[4,1040,128]{2,1,0:T(8,128)(2,1)S(1)} %gather_sources.1.same_ref, bf16[4,1040,128]{2,1,0:T(8,128)(2,1)S(1)} %collective-permute-done.3.other_ref, bf16[4,2,192,128]{3,2,1,0:T(8,128)(2,1)S(1)} %bitcast.4, ...), custom_call_target="tpu_custom_call" | custom-call | tf_op jit(solution)/shard_map/key_gradients/pallas_call | solution.py:67
  58.7 3.5 %all-to-all-start.2 = ((bf16[8,192,128]{2,1,0:T(8,128)(2,1)}), bf16[8,192,128]{2,1,0:T(8,128)(2,1)S(1)}, u32[]{:S(2)}, u32[]{:S(2)}) async-start(bf16[8,192,128]{2,1,0:T(8,128)(2,1)} %get-tuple-element.17), calls=%async_computation.2 | async-start | bytes 786432 | tf_op jit(solution)/shard_map/all_to_all | solution.py:422
  62.1 2.6 %query_gradients.1 = (bf16[4,128,512]{2,1,0:T(8,128)(2,1)S(1)}, bf16[4,128,512]{2,1,0:T(8,128)(2,1)S(1)}) custom-call(bf16[4,2,192,128]{3,2,1,0:T(8,128)(2,1)S(1)} %bitcast.5, bf16[2,4,3,256,512]{4,3,2,1,0:T(8,128)(2,1)} %get-tuple-element.18.score_hbm), custom_call_target="tpu_custom_call" | custom-call | tf_op jit(solution)/shard_map/query_gradients/pallas_call | solution.py:67
  64.7 1.9 %collective-permute-start.6 = (bf16[4,128,512]{2,1,0:T(8,128)(2,1)S(1)}, bf16[4,128,512]{2,1,0:T(8,128)(2,1)S(1)}, u32[]{:S(2)}, u32[]{:S(2)}) collective-permute-start(bf16[4,128,512]{2,1,0:T(8,128)(2,1)S(1)} %get-tuple-element.20), channel_id=1, source_target_pairs={{0,8},{8,0},{1,9},{9,1},{2,10},{10,2},{3,11},{11,3},{4,12},{12,4},... | collective-permute-start | bytes 1572872 | tf_op jit(solution)/shard_map/ppermute | solution.py:423
  66.6 1.9 %collective-permute-done.6.other_ref = bf16[4,128,512]{2,1,0:T(8,128)(2,1)S(1)} collective-permute-done((bf16[4,128,512]{2,1,0:T(8,128)(2,1)S(1)}, bf16[4,128,512]{2,1,0:T(8,128)(2,1)S(1)}, u32[]{:S(2)}, u32[]{:S(2)}) %collective-permute-start.6) | collective-permute-done | bytes 524320 | tf_op jit(solution)/shard_map/ppermute | solution.py:423
  68.5 0.9 %sum_cores.1 = bf16[4,128,512]{2,1,0:T(8,128)(2,1)} custom-call(bf16[4,128,512]{2,1,0:T(8,128)(2,1)S(1)} %get-tuple-element.19.same_ref, bf16[4,128,512]{2,1,0:T(8,128)(2,1)S(1)} %collective-permute-done.6.other_ref), custom_call_target="tpu_custom_call" | custom-call | tf_op jit(solution)/shard_map/sum_cores/pallas_call | solution.py:67
  69.4 4.3 %all-to-all-done.2.dkv_ref = bf16[8,192,128]{2,1,0:T(8,128)(2,1)S(1)} async-done(((bf16[8,192,128]{2,1,0:T(8,128)(2,1)}), bf16[8,192,128]{2,1,0:T(8,128)(2,1)S(1)}, u32[]{:S(2)}, u32[]{:S(2)}) %all-to-all-start.2) | async-done | bytes 393248 | tf_op jit(solution)/shard_map/all_to_all | solution.py:422
  73.7 1.3 %collective-permute-start.7 = (bf16[128,128]{1,0:T(8,128)(2,1)S(1)}, bf16[128,128]{1,0:T(8,128)(2,1)S(1)}, u32[]{:S(2)}, u32[]{:S(2)}) collective-permute-start(bf16[128,128]{1,0:T(8,128)(2,1)S(1)} %get-tuple-element.24), channel_id=1, source_target_pairs={{320,0},{352,32},{256,64},{288,96},{321,1},{353,33},{257,65},{289,... | collective-permute-start | bytes 98312 | tf_op jit(solution)/shard_map/ppermute | solution.py:438
  75.0 1.3 %collective-permute-start.8 = (bf16[128,128]{1,0:T(8,128)(2,1)S(1)}, bf16[128,128]{1,0:T(8,128)(2,1)S(1)}, u32[]{:S(2)}, u32[]{:S(2)}) collective-permute-start(bf16[128,128]{1,0:T(8,128)(2,1)S(1)} %get-tuple-element.25), channel_id=1, source_target_pairs={{128,0},{256,128},{129,1},{257,129},{130,2},{258,130},{131,3},{259... | collective-permute-start | bytes 98312 | tf_op jit(solution)/shard_map/ppermute | solution.py:439
  76.3 3.5 %all-to-all-start.3 = ((bf16[4,128,512]{2,1,0:T(8,128)(2,1)}), bf16[4,128,512]{2,1,0:T(8,128)(2,1)S(1)}, u32[]{:S(2)}, u32[]{:S(2)}) async-start(bf16[4,128,512]{2,1,0:T(8,128)(2,1)} %sum_cores.1), calls=%async_computation.3 | async-start | bytes 1048576 | tf_op jit(solution)/shard_map/all_to_all | solution.py:440
  79.8 6.6 %collective-permute-done.7.two_ref = bf16[128,128]{1,0:T(8,128)(2,1)S(1)} collective-permute-done((bf16[128,128]{1,0:T(8,128)(2,1)S(1)}, bf16[128,128]{1,0:T(8,128)(2,1)S(1)}, u32[]{:S(2)}, u32[]{:S(2)}) %collective-permute-start.7) | collective-permute-done | bytes 32800 | tf_op jit(solution)/shard_map/ppermute | solution.py:438
  (11 shorter events, 3.2 us)
Async XLA Ops:
  2.0 23.6 %collective-permute-start.1 = (bf16[1040,128]{1,0:T(8,128)(2,1)S(1)}, bf16[1040,128]{1,0:T(8,128)(2,1)S(1)}, u32[]{:S(2)}, u32[]{:S(2)}) collective-permute-start(bf16[1040,128]{1,0:T(8,128)(2,1)S(1)} %get-tuple-element.15.own_ref), channel_id=1, source_target_pairs={{0,1},{1,0},{2,3},{3,2},{4,5},{5,4},{6,7},{7,6},{8,9},{9,8},{10,11... | collective-permute-start | bytes 798728 | tf_op jit(solution)/shard_map/ppermute | solution.py:404
  5.4 23.2 %collective-permute-start.5 = (bf16[128,128]{1,0:T(8,128)(2,1)}, bf16[128,128]{1,0:T(8,128)(2,1)S(1)}, u32[]{:S(2)}, u32[]{:S(2)}) collective-permute-start(bf16[128,128]{1,0:T(8,128)(2,1)} %kv_hbm.1), channel_id=1, source_target_pairs={{0,320},{32,352},{64,256},{96,288},{1,321},{33,353},{65,257},{97,2... | collective-permute-start | bytes 98312 | tf_op jit(solution)/shard_map/ppermute | solution.py:393
  20.2 8.4 %collective-permute-start.4 = (bf16[128,128]{1,0:T(8,128)(2,1)}, bf16[128,128]{1,0:T(8,128)(2,1)S(1)}, u32[]{:S(2)}, u32[]{:S(2)}) collective-permute-start(bf16[128,128]{1,0:T(8,128)(2,1)} %kv_hbm.1), channel_id=1, source_target_pairs={{0,128},{128,256},{1,129},{129,257},{2,130},{130,258},{3,131},{131... | collective-permute-start | bytes 98312 | tf_op jit(solution)/shard_map/ppermute | solution.py:394
  21.5 12.4 %collective-permute-start = (bf16[1040,128]{1,0:T(8,128)(2,1)S(1)}, bf16[1040,128]{1,0:T(8,128)(2,1)S(1)}, u32[]{:S(2)}, u32[]{:S(2)}) collective-permute-start(bf16[1040,128]{1,0:T(8,128)(2,1)S(1)} %get-tuple-element.15.own_ref), channel_id=1, source_target_pairs={{0,17},{1,16},{16,1},{17,0},{2,19},{3,18},{18,3},{19,2},{4,21},{5,... | collective-permute-start | bytes 798728 | tf_op jit(solution)/shard_map/ppermute | solution.py:406
  25.6 12.4 %collective-permute-start.2 = (bf16[1040,128]{1,0:T(8,128)(2,1)S(1)}, bf16[1040,128]{1,0:T(8,128)(2,1)S(1)}, u32[]{:S(2)}, u32[]{:S(2)}) collective-permute-start(bf16[1040,128]{1,0:T(8,128)(2,1)S(1)} %collective-permute-done.1.near_ref), channel_id=1, source_target_pairs={{0,17},{1,16},{16,1},{17,0},{2,19},{3,18},{18,3},{19,2},{4,21},{5,... | collective-permute-start | bytes 798728 | tf_op jit(solution)/shard_map/ppermute | solution.py:407
  29.4 14.2 %all-to-all-start = ((bf16[8,192,128]{2,1,0:T(8,128)(2,1)}), bf16[8,192,128]{2,1,0:T(8,128)(2,1)S(1)}, u32[]{:S(2)}, u32[]{:S(2)}) async-start(bf16[8,192,128]{2,1,0:T(8,128)(2,1)} %pack_keys.1), calls=%async_computation | async-start | bytes 786432 | tf_op jit(solution)/shard_map/all_to_all | solution.py:417
  38.0 5.7 %collective-permute-start.3 = (bf16[4,1040,128]{2,1,0:T(8,128)(2,1)S(1)}, bf16[4,1040,128]{2,1,0:T(8,128)(2,1)S(1)}, u32[]{:S(2)}, u32[]{:S(2)}) collective-permute-start(bf16[4,1040,128]{2,1,0:T(8,128)(2,1)S(1)} %gather_sources.1.same_ref), channel_id=1, source_target_pairs={{0,8},{8,0},{1,9},{9,1},{2,10},{10,2},{3,11},{11,3},{4,12},{12,4},... | collective-permute-start | bytes 3194888 | tf_op jit(solution)/shard_map/ppermute | solution.py:411
  58.7 15.0 %all-to-all-start.2 = ((bf16[8,192,128]{2,1,0:T(8,128)(2,1)}), bf16[8,192,128]{2,1,0:T(8,128)(2,1)S(1)}, u32[]{:S(2)}, u32[]{:S(2)}) async-start(bf16[8,192,128]{2,1,0:T(8,128)(2,1)} %get-tuple-element.17), calls=%async_computation.2 | async-start | bytes 786432 | tf_op jit(solution)/shard_map/all_to_all | solution.py:422
  64.7 3.8 %collective-permute-start.6 = (bf16[4,128,512]{2,1,0:T(8,128)(2,1)S(1)}, bf16[4,128,512]{2,1,0:T(8,128)(2,1)S(1)}, u32[]{:S(2)}, u32[]{:S(2)}) collective-permute-start(bf16[4,128,512]{2,1,0:T(8,128)(2,1)S(1)} %get-tuple-element.20), channel_id=1, source_target_pairs={{0,8},{8,0},{1,9},{9,1},{2,10},{10,2},{3,11},{11,3},{4,12},{12,4},... | collective-permute-start | bytes 1572872 | tf_op jit(solution)/shard_map/ppermute | solution.py:423
  73.7 12.7 %collective-permute-start.7 = (bf16[128,128]{1,0:T(8,128)(2,1)S(1)}, bf16[128,128]{1,0:T(8,128)(2,1)S(1)}, u32[]{:S(2)}, u32[]{:S(2)}) collective-permute-start(bf16[128,128]{1,0:T(8,128)(2,1)S(1)} %get-tuple-element.24), channel_id=1, source_target_pairs={{320,0},{352,32},{256,64},{288,96},{321,1},{353,33},{257,65},{289,... | collective-permute-start | bytes 98312 | tf_op jit(solution)/shard_map/ppermute | solution.py:438
  75.0 11.4 %collective-permute-start.8 = (bf16[128,128]{1,0:T(8,128)(2,1)S(1)}, bf16[128,128]{1,0:T(8,128)(2,1)S(1)}, u32[]{:S(2)}, u32[]{:S(2)}) collective-permute-start(bf16[128,128]{1,0:T(8,128)(2,1)S(1)} %get-tuple-element.25), channel_id=1, source_target_pairs={{128,0},{256,128},{129,1},{257,129},{130,2},{258,130},{131,3},{259... | collective-permute-start | bytes 98312 | tf_op jit(solution)/shard_map/ppermute | solution.py:439
  76.3 11.5 %all-to-all-start.3 = ((bf16[4,128,512]{2,1,0:T(8,128)(2,1)}), bf16[4,128,512]{2,1,0:T(8,128)(2,1)S(1)}, u32[]{:S(2)}, u32[]{:S(2)}) async-start(bf16[4,128,512]{2,1,0:T(8,128)(2,1)} %sum_cores.1), calls=%async_computation.3 | async-start | bytes 1048576 | tf_op jit(solution)/shard_map/all_to_all | solution.py:440
